TPU v7x, 32 devices: a whole 2x2x4 slice. The times are simulated.
32 devices in a mesh: groups: 2 (over y), patch: 4 (over z), head: 4 (over x, core).
Axes of the slice: x: 2, y: 2, z: 4, core: 2. Of those that a mesh axis runs over, the one named last changes fastest.
Arguments:
- queries: bfloat16 [1024, 2560], P(('groups', 'patch', 'head')), parts along dimension 0, may hold values from -500 to 500
- keys: bfloat16 [1024, 2560], P(('groups', 'patch', 'head')), parts along dimension 0, may hold values from -500 to 500
- values: bfloat16 [1024, 2560], P(('groups', 'patch', 'head')), parts along dimension 0, may hold values from -6 to 6
- q_gain: float32 [2560], replicated, may hold values from 1.2 to 2
- k_gain: float32 [2560], replicated, may hold values from 1.2 to 2
- prev_keys: bfloat16 [1024, 2560], P('groups', 'head'), parts along dimension 0, may hold values from -200 to 200
- prev_values: bfloat16 [1024, 2560], P('groups', 'head'), parts along dimension 0, may hold values from -6 to 6
- res_keys: bfloat16 [16, 16, 2560], P(('groups', 'patch'), None, 'head'), parts along dimension 0, may hold values from -3 to 3
- res_values: bfloat16 [16, 16, 2560], P(('groups', 'patch'), None, 'head'), parts along dimension 0, may hold values from -3 to 3
- block_ids: int32 [16], P(('groups', 'patch')), parts along dimension 0, may hold values from 0 to 7, as said below
- scale_exps: int32 [16, 20], P(('groups', 'patch'), 'head'), parts along dimension 0, may hold values from -2 to 1
Outputs:
- attended: bfloat16 [1024, 2560], P(('groups', 'patch', 'head')), parts along dimension 0
There are 2 independent parts, one for each index of `groups`. A program takes and returns all parts, laid end to end along the dimension named above; an argument that names none is the same for every part. Nothing has to cross between parts.
Inputs may be any that keep to these rules, and one draw needn't show every extreme that they name: `block_ids`: the 2 entries of one patch are distinct block numbers of that patch.
All inputs are finite; a program needn't handle non-finite values.
Results may differ from a plain program's by a relative error of at most 0.004.
The roundings to bfloat16 on the way count: a program that leaves them out, or rounds other values in their place, can miss the bound.
Values may be sent and summed in bfloat16 or wider, within the bound.
No kernel may reach another device: no remote copies, remote signals or barrier semaphores. Data moves between devices by JAX's collectives and lax.ppermute only.
A program may use at most 128 MiB of HBM per device.

v0:
```python
import math

import jax
import jax.numpy as jnp
from jax import lax
from jax.sharding import PartitionSpec as P

epsilon = 1e-06


def rms_scale(token_rows, gain_row):
    widened = token_rows.astype(jnp.float32)
    inverse = lax.rsqrt(jnp.mean(widened * widened, axis=-1, keepdims=True) + epsilon)
    return (widened * inverse * gain_row).astype(jnp.bfloat16)


def attend(running, query_heads, key_rows, value_rows, key_keep):
    peak_so, denominator, summed = running
    head_count = query_heads.shape[1]
    head_size = query_heads.shape[2]
    key_heads = key_rows.reshape(key_rows.shape[0], head_count, head_size)
    value_heads = value_rows.reshape(value_rows.shape[0], head_count, head_size)
    scores = jnp.einsum(
        "qhd,khd->hqk", query_heads, key_heads, preferred_element_type=jnp.float32
    ) / math.sqrt(head_size)
    scores = jnp.where(key_keep[None, None, :], scores, -jnp.inf)
    new_peak = jnp.maximum(peak_so, jnp.max(scores, axis=-1))
    rescale = jnp.exp(peak_so - new_peak)
    powered = jnp.exp(scores - new_peak[..., None])
    denominator = denominator * rescale + jnp.sum(powered, axis=-1)
    weights = powered.astype(jnp.bfloat16)
    summed = summed * rescale[..., None] + jnp.einsum(
        "hqk,khd->hqd", weights, value_heads, preferred_element_type=jnp.float32
    )
    return (new_peak, denominator, summed)


def local(
    queries,
    keys,
    values,
    q_gain,
    k_gain,
    prev_keys,
    prev_values,
    res_keys,
    res_values,
    block_ids,
    scale_exps,
):
    head_count = scale_exps.shape[1]
    feature_count = prev_keys.shape[1]
    head_size = feature_count // head_count
    sent_each = res_keys.shape[0]
    block_len = res_keys.shape[1]
    query_norm = rms_scale(queries, q_gain)
    key_norm = rms_scale(keys, k_gain)
    query_norm, key_norm, value_local = (
        lax.all_to_all(query_norm, "head", split_axis=1, concat_axis=0, tiled=True),
        lax.all_to_all(key_norm, "head", split_axis=1, concat_axis=0, tiled=True),
        lax.all_to_all(values, "head", split_axis=1, concat_axis=0, tiled=True),
    )
    tok_patch = query_norm.shape[0]
    blocks_each = tok_patch // block_len
    own_patch = lax.axis_index("patch")
    query_heads = query_norm.reshape(tok_patch, head_count, head_size)
    empty = (
        jnp.full((head_count, tok_patch), -jnp.inf, jnp.float32),
        jnp.zeros((head_count, tok_patch), jnp.float32),
        jnp.zeros((head_count, tok_patch, head_size), jnp.float32),
    )
    starting = attend(empty, query_heads, key_norm, value_local, jnp.ones((tok_patch,), jnp.bool_))
    running = starting
    residual_keys = lax.all_gather(res_keys, "patch", axis=0, tiled=True)
    residual_values = lax.all_gather(res_values, "patch", axis=0, tiled=True)
    part_ids = lax.all_gather(block_ids, "patch", axis=0, tiled=True)
    part_exponents = lax.all_gather(scale_exps, "patch", axis=0, tiled=True)
    sent_here = part_ids.shape[0]
    patches_here = sent_here // sent_each
    block_total = patches_here * blocks_each
    owner_local = jnp.arange(sent_here, dtype=jnp.int32) // sent_each
    where_local = (owner_local * blocks_each + part_ids).astype(jnp.int32)
    block_numbers = jnp.arange(block_total, dtype=jnp.int32)
    refreshed = jnp.any(where_local[None, :] == block_numbers[:, None], axis=1)
    block_owner = block_numbers // blocks_each
    block_keep = jnp.logical_and(jnp.logical_not(refreshed), block_owner != own_patch)
    stale_keep = jnp.repeat(block_keep, block_len)
    running = attend(running, query_heads, prev_keys, prev_values, stale_keep)
    factor = jnp.repeat(jnp.exp2(part_exponents.astype(jnp.float32)), head_size, axis=1)
    key_blocks = prev_keys.reshape(block_total, block_len, feature_count)[where_local]
    value_blocks = prev_values.reshape(block_total, block_len, feature_count)[where_local]
    new_keys = (
        key_blocks.astype(jnp.float32) + residual_keys.astype(jnp.float32) * factor[:, None, :]
    ).astype(jnp.bfloat16)
    new_values = (
        value_blocks.astype(jnp.float32) + residual_values.astype(jnp.float32) * factor[:, None, :]
    ).astype(jnp.bfloat16)
    fresh_keep = jnp.repeat(owner_local != own_patch, block_len)
    finished = attend(
        running,
        query_heads,
        new_keys.reshape(sent_here * block_len, feature_count),
        new_values.reshape(sent_here * block_len, feature_count),
        fresh_keep,
    )
    peak_so, denominator, summed = finished
    result = summed / denominator[..., None]
    attended = (
        jnp.transpose(result, (1, 0, 2)).reshape(tok_patch, feature_count).astype(jnp.bfloat16)
    )
    return lax.all_to_all(attended, "head", split_axis=0, concat_axis=1, tiled=True)


def solution(mesh):
    in_specs = (
        P(("groups", "patch", "head"), None),
        P(("groups", "patch", "head"), None),
        P(("groups", "patch", "head"), None),
        P(),
        P(),
        P("groups", "head"),
        P("groups", "head"),
        P(("groups", "patch"), None, "head"),
        P(("groups", "patch"), None, "head"),
        P(("groups", "patch")),
        P(("groups", "patch"), "head"),
    )
    out_specs = P(("groups", "patch", "head"), None)
    return jax.shard_map(local, mesh=mesh, in_specs=in_specs, out_specs=out_specs, check_vma=False)
```

profile of v0, /device:TPU:0, one launch (start us, length us, event | category | flops | bytes accessed | tf_op | source)
XLA Modules:
  0.0 86.3 jit_solution(10143836025868375058)
XLA Ops:
  0.0 1.1 %fusion.13 = f32[32]{0:T(128)S(1)} fusion(bf16[32,2560]{1,0:T(8,128)(2,1)} %param.11), kind=kLoop, calls=%fused_computation.25 | loop fusion | flops 245728 | bytes 163968 | tf_op jit(solution)/shard_map/reduce_sum | solution.py:13
  1.2 1.0 %fusion.15 = bf16[32,2560]{1,0:T(8,128)(2,1)S(1)} fusion(bf16[32,2560]{1,0:T(8,128)(2,1)} %param.11, f32[2560]{0:T(1024)} %param.14, f32[32]{0:T(128)S(1)} %add_rsqrt_fusion.1), kind=kLoop, calls=%fused_computation.27 | loop fusion | flops 327680 | bytes 338048 | tf_op jit(solution)/shard_map/convert_element_type | solution.py:14
  2.2 0.7 copy.131
  2.9 1.3 %dynamic-slice = u32[1]{0:T(128)} dynamic-slice(u32[32]{0:T(128)} %constant.71, u32[]{:T(128)S(6)} %add.79), dynamic_slice_sizes={1} | dynamic-slice | bytes 12
  4.9 0.9 dynamic-update-slice
  5.8 4.2 %all-to-all-start = ((bf16[32,4,640]{2,0,1:T(8,128)(2,1)}), bf16[32,4,640]{2,0,1:T(8,128)(2,1)S(1)}, u32[]{:S(2)}, u32[]{:S(2)}) async-start(bf16[32,4,640]{2,0,1:T(8,128)(2,1)} %bitcast.91), calls=%async_computation | async-start | bytes 327680 | tf_op jit(solution)/shard_map/all_to_all | solution.py:59
  10.0 9.1 %all-reduce = s32[8]{0:T(128)S(1)} all-reduce(s32[8]{0:T(128)S(1)} %dynamic-update-slice), channel_id=1, replica_groups=mesh['groups'=2,'patch'=4,'head'=4] {'patch'}, use_global_device_ids=true, to_apply=%add | all-reduce | flops 8 | bytes 64
  19.1 1.7 %gather_fusion = bf16[8,16,640]{2,1,0:T(8,128)(2,1)S(1)} fusion(bf16[32,16,640]{2,1,0:T(8,128)(2,1)} %bitcast.94, s32[1024]{0:T(1024)S(1)} %pad_clamp_fusion), kind=kCustom, calls=%fused_computation | custom fusion | bytes 327712 | tf_op jit(solution)/shard_map/gather | solution.py:90
  20.8 0.6 gather_fusion.1
  21.4 13.8 %all_gather.13 = bf16[8,16,640]{2,1,0:T(8,128)(2,1)S(1)} all-gather(bf16[2,16,640]{2,1,0:T(8,128)(2,1)S(1)} %copy-done.4), channel_id=1, replica_groups=mesh['groups'=2,'patch'=4,'head'=4] {'patch'}, dimensions={0}, use_global_device_ids=true | all-gather | bytes 204800 | tf_op jit(solution)/shard_map/all_gather | solution.py:74
  35.3 13.7 %all_gather.15 = bf16[8,16,640]{2,1,0:T(8,128)(2,1)S(1)} all-gather(bf16[2,16,640]{2,1,0:T(8,128)(2,1)S(1)} %copy-done.5), channel_id=1, replica_groups=mesh['groups'=2,'patch'=4,'head'=4] {'patch'}, dimensions={0}, use_global_device_ids=true | all-gather | bytes 204800 | tf_op jit(solution)/shard_map/all_gather | solution.py:75
  49.0 8.9 %all-gather = s32[4,2,5]{2,1,0:T(2,128)S(1)} all-gather(s32[1,2,5]{2,1,0:T(2,128)S(1)} %bitcast.104), channel_id=1, replica_groups=mesh['groups'=2,'patch'=4,'head'=4] {'patch'}, dimensions={0}, use_global_device_ids=true | all-gather | bytes 200 | tf_op jit(solution)/shard_map/all_gather | solution.py:77
  58.4 0.3 copy.82
  58.7 0.3 copy.85
  59.0 0.2 reshape_reshape.6
  59.3 0.7 copy.130
  60.1 3.5 %all-to-all-start.1 = ((bf16[32,4,640]{2,0,1:T(8,128)(2,1)}), bf16[32,4,640]{2,0,1:T(8,128)(2,1)S(1)}, u32[]{:S(2)}, u32[]{:S(2)}) async-start(bf16[32,4,640]{2,0,1:T(8,128)(2,1)} %bitcast.90), calls=%async_computation.1 | async-start | bytes 327680 | tf_op jit(solution)/shard_map/all_to_all | solution.py:60
  63.8 0.7 copy.129
  64.6 0.2 reshape.110
  64.8 3.7 %all-to-all-done.1 = bf16[32,4,640]{2,0,1:T(8,128)(2,1)S(1)} async-done(((bf16[32,4,640]{2,0,1:T(8,128)(2,1)}), bf16[32,4,640]{2,0,1:T(8,128)(2,1)S(1)}, u32[]{:S(2)}, u32[]{:S(2)}) %all-to-all-start.1) | async-done | bytes 163872 | tf_op jit(solution)/shard_map/all_to_all | solution.py:60
  68.6 3.3 %all-to-all-start.2 = ((bf16[32,4,640]{2,0,1:T(8,128)(2,1)}), bf16[32,4,640]{2,0,1:T(8,128)(2,1)S(1)}, u32[]{:S(2)}, u32[]{:S(2)}) async-start(bf16[32,4,640]{2,0,1:T(8,128)(2,1)} %bitcast.89), calls=%async_computation.2 | async-start | bytes 327680 | tf_op jit(solution)/shard_map/all_to_all | solution.py:61
  72.1 0.3 fusion.45
  72.4 0.3 fusion.44
  72.7 0.4 fusion.46
  73.1 0.4 convolution_bitcast_fusion.1
  73.5 0.4 fusion.9
  73.9 3.0 %all-to-all-done.2 = bf16[32,4,640]{2,0,1:T(8,128)(2,1)S(1)} async-done(((bf16[32,4,640]{2,0,1:T(8,128)(2,1)}), bf16[32,4,640]{2,0,1:T(8,128)(2,1)S(1)}, u32[]{:S(2)}, u32[]{:S(2)}) %all-to-all-start.2) | async-done | bytes 163872 | tf_op jit(solution)/shard_map/all_to_all | solution.py:61
  77.2 0.4 fusion.7
  77.6 0.3 fusion.8
  78.0 0.2 convert_element_type.64
  78.2 7.3 %all_to_all.64 = bf16[4,32,640]{2,1,0:T(8,128)(2,1)S(1)} all-to-all(bf16[4,32,640]{2,1,0:T(8,128)(2,1)S(1)} %convert_element_type.64), channel_id=1, replica_groups=mesh['groups'=2,'patch'=4,'head'=4] {'head'}, dimensions={0} | all-to-all | bytes 327680 | tf_op jit(solution)/shard_map/all_to_all | solution.py:111
  85.6 0.7 copy.101
  (42 shorter events, 1.9 us)
Async XLA Ops:
  0.0 20.8 %copy-start.1 = (bf16[512,640]{1,0:T(8,128)(2,1)S(1)}, bf16[512,640]{1,0:T(8,128)(2,1)}, u32[]{:S(2)}) copy-start(bf16[512,640]{1,0:T(8,128)(2,1)} %param.17) | copy-start | bytes 1966084
  0.0 21.4 %copy-start.4 = (bf16[2,16,640]{2,1,0:T(8,128)(2,1)S(1)}, bf16[2,16,640]{2,1,0:T(8,128)(2,1)}, u32[]{:S(2)}) copy-start(bf16[2,16,640]{2,1,0:T(8,128)(2,1)} %param.18) | copy-start | bytes 122884
  0.0 35.3 %copy-start.5 = (bf16[2,16,640]{2,1,0:T(8,128)(2,1)S(1)}, bf16[2,16,640]{2,1,0:T(8,128)(2,1)}, u32[]{:S(2)}) copy-start(bf16[2,16,640]{2,1,0:T(8,128)(2,1)} %param.19) | copy-start | bytes 122884
  0.0 48.9 %copy-start.7 = (s32[2,5]{1,0:T(2,128)S(1)}, s32[2,5]{1,0:T(2,128)}, u32[]{:S(2)}) copy-start(s32[2,5]{1,0:T(2,128)} %param.21) | copy-start | bytes 124
  0.0 58.0 %copy-start.2 = (bf16[32,2560]{1,0:T(8,128)(2,1)S(1)}, bf16[32,2560]{1,0:T(8,128)(2,1)}, u32[]{:S(2)}) copy-start(bf16[32,2560]{1,0:T(8,128)(2,1)} %param.12) | copy-start | bytes 491524
  0.0 58.2 %copy-start.6 = (f32[2560]{0:T(1024)S(1)}, f32[2560]{0:T(1024)}, u32[]{:S(2)}) copy-start(f32[2560]{0:T(1024)} %param.15) | copy-start | bytes 30724
  5.8 54.3 %all-to-all-start = ((bf16[32,4,640]{2,0,1:T(8,128)(2,1)}), bf16[32,4,640]{2,0,1:T(8,128)(2,1)S(1)}, u32[]{:S(2)}, u32[]{:S(2)}) async-start(bf16[32,4,640]{2,0,1:T(8,128)(2,1)} %bitcast.91), calls=%async_computation | async-start | bytes 327680 | tf_op jit(solution)/shard_map/all_to_all | solution.py:59
  19.1 39.4 %copy-start = (bf16[512,640]{1,0:T(8,128)(2,1)S(1)}, bf16[512,640]{1,0:T(8,128)(2,1)}, u32[]{:S(2)}) copy-start(bf16[512,640]{1,0:T(8,128)(2,1)} %param.16) | copy-start | bytes 1966084
  58.7 5.0 %copy-start.3 = (bf16[32,2560]{1,0:T(8,128)(2,1)S(1)}, bf16[32,2560]{1,0:T(8,128)(2,1)}, u32[]{:S(2)}) copy-start(bf16[32,2560]{1,0:T(8,128)(2,1)} %param.13) | copy-start | bytes 491524
  60.1 8.5 %all-to-all-start.1 = ((bf16[32,4,640]{2,0,1:T(8,128)(2,1)}), bf16[32,4,640]{2,0,1:T(8,128)(2,1)S(1)}, u32[]{:S(2)}, u32[]{:S(2)}) async-start(bf16[32,4,640]{2,0,1:T(8,128)(2,1)} %bitcast.90), calls=%async_computation.1 | async-start | bytes 327680 | tf_op jit(solution)/shard_map/all_to_all | solution.py:60
  68.6 8.3 %all-to-all-start.2 = ((bf16[32,4,640]{2,0,1:T(8,128)(2,1)}), bf16[32,4,640]{2,0,1:T(8,128)(2,1)S(1)}, u32[]{:S(2)}, u32[]{:S(2)}) async-start(bf16[32,4,640]{2,0,1:T(8,128)(2,1)} %bitcast.89), calls=%async_computation.2 | async-start | bytes 327680 | tf_op jit(solution)/shard_map/all_to_all | solution.py:61
where the time goes:
time: 86.8 us; the launch traced here: 86.3 us
  blocking collectives  52.8 us (61%)
  starting transfers between devices  11 us (13%)
  local copies, waits for them, and re-layouts  9.55 us (11%)
  waiting for transfers between devices  6.68 us (8%)
  other arithmetic  3.21 us (4%)
  matrix products  2.02 us (2%)
  between operations  0.93 us (1%)
    all_gather x1, blocking collectives, local(): residual_keys = lax.all_gather(res_keys, 'patch', axis=0, tiled=True)  13.8 us
    all_gather x1, blocking collectives, local(): residual_values = lax.all_gather(res_values, 'patch', axis=0, tiled=True)  13.7 us
    unnamed x1, blocking collectives  9.07 us
    all_gather x1, blocking collectives, local(): part_exponents = lax.all_gather(scale_exps, 'patch', axis=0, tiled=True)  8.9 us
    all_to_all x1, blocking collectives, local(): lax.all_to_all(attended, 'head', split_axis=0, concat_axis=1, tiled=True)  7.34 us
    all_to_all x1, starting transfers between devices, local(): lax.all_to_all(query_norm, 'head', split_axis=1, concat_axis=0, tiled=True)  4.22 us
    all_to_all x1, waiting for transfers between devices, local(): lax.all_to_all(key_norm, 'head', split_axis=1, concat_axis=0, tiled=True)  3.71 us
    all_to_all x1, starting transfers between devices, local(): lax.all_to_all(key_norm, 'head', split_axis=1, concat_axis=0, tiled=True)  3.47 us
  transfers between devices with their start and end apart: 3, of which 2 were waited for; matrix products, arithmetic and copies ran while one was open for 9% of the time, Pallas kernels for 0%

commit v1 on v0

v1 whole, which is shorter than its diff:
```python
import functools
import math

import jax
import jax.numpy as jnp
from jax import lax
from jax.experimental import pallas as pl
from jax.experimental.pallas import tpu as pltpu
from jax.sharding import PartitionSpec as P

epsilon = 1e-06
DIRECT_PATCHES = 8
VM = pl.BlockSpec(memory_space=pltpu.VMEM)
SM = pl.BlockSpec(memory_space=pltpu.SMEM)


def trade(array, axis, step, count):
    return lax.ppermute(array, axis, [(i, i ^ step) for i in range(count)])


def pack_kernel(sent, block_len, heads, size, tail, ids, exps, res_k, res_v, out):
    rows = sent * block_len
    for h in range(heads):
        for r in range(sent):
            power = (1 << (exps[r, h] + 16)).astype(jnp.float32) * (1.0 / 65536.0)
            lanes = pl.ds(h * size, size)
            k = res_k[r, :, lanes].astype(jnp.float32) * power
            v = res_v[r, :, lanes].astype(jnp.float32) * power
            out[pl.ds(h * 2 * rows + r * block_len, block_len), :] = k.astype(jnp.bfloat16)
            out[pl.ds((h * 2 + 1) * rows + r * block_len, block_len), :] = v.astype(jnp.bfloat16)
    lane = lax.broadcasted_iota(jnp.int32, (tail, size), 1) // block_len
    numbers = jnp.zeros((tail, size), jnp.float32)
    for r in range(sent):
        numbers = jnp.where(lane == r, ids[r].astype(jnp.float32), numbers)
    out[pl.ds(heads * 2 * rows, tail), :] = numbers.astype(jnp.bfloat16)


def norm_kernel(count, me, q_ref, k_ref, v_ref, qg_ref, kg_ref, *outs):
    rows, width = q_ref.shape[0], q_ref.shape[1] // count

    def inverse(ref):
        x = ref[...].astype(jnp.float32)
        return lax.rsqrt(jnp.mean(x * x, axis=-1, keepdims=True) + epsilon)

    q_inv, k_inv = inverse(q_ref), inverse(k_ref)
    for step in range(count):
        cols = pl.ds(pl.multiple_of((me[0] ^ step) * width, 128), width)
        q = q_ref[:, cols].astype(jnp.float32) * q_inv * qg_ref[:, cols]
        k = k_ref[:, cols].astype(jnp.float32) * k_inv * kg_ref[:, cols]
        outs[step][pl.ds(0, rows), :] = q.astype(jnp.bfloat16)
        outs[step][pl.ds(rows, rows), :] = k.astype(jnp.bfloat16)
        outs[step][pl.ds(2 * rows, rows), :] = v_ref[:, cols]


def attend_kernel(head_n, patch_n, direct, sent, block_len, size, me, *refs):
    parts = refs[:head_n]
    prev_k, prev_v = refs[head_n : head_n + 2]
    n_res = patch_n - 1 if direct else 1
    res = refs[head_n + 2 : head_n + 2 + n_res]
    outs = refs[head_n + 2 + n_res : head_n + 2 + n_res + head_n]
    q_all, k_all, v_all = refs[-3:]
    rows = parts[0].shape[0] // 3
    tok = rows * head_n
    width = parts[0].shape[1]
    heads = width // size
    fresh = sent * block_len

    for step in range(head_n):
        q_all[pl.ds(step * rows, rows), :] = parts[step][pl.ds(0, rows), :]
        k_all[pl.ds(step * rows, rows), :] = parts[step][pl.ds(rows, rows), :]
        v_all[pl.ds(step * rows, rows), :] = parts[step][pl.ds(2 * rows, rows), :]

    row = lax.broadcasted_iota(jnp.int32, (tok, fresh), 0)
    col = lax.broadcasted_iota(jnp.int32, (tok, fresh), 1)
    fits = row % block_len == col % block_len
    block = (row // block_len).astype(jnp.float32)

    def refresh(step, packed):
        owner = me[0] ^ step
        numbers = packed[pl.ds(heads * 2 * fresh, 16), :].astype(jnp.float32)[0:1, :fresh]
        chosen = jnp.logical_and(fits, block == numbers).astype(jnp.bfloat16)
        source = pl.ds(pl.multiple_of(owner * tok, 128), tok)
        target = pl.ds(pl.multiple_of(step * tok, 128), tok)
        for h in range(heads):
            lanes = pl.ds(h * size, size)
            for which, (old, new) in enumerate(((prev_k, k_all), (prev_v, v_all))):
                change = jnp.dot(
                    chosen,
                    packed[pl.ds((h * 2 + which) * fresh, fresh), :],
                    preferred_element_type=jnp.float32,
                )
                new[target, lanes] = (old[source, lanes].astype(jnp.float32) + change).astype(jnp.bfloat16)

    if direct:
        for step in range(1, patch_n):
            refresh(step, res[step - 1])
    else:

        @pl.loop(1, patch_n)
        def _(step):
            refresh(step, res[0].at[me[0] ^ step])

    for h in range(heads):
        lanes = pl.ds(h * size, size)
        scores = lax.dot_general(
            q_all[:, lanes], k_all[:, lanes], (((1,), (1,)), ((), ())), preferred_element_type=jnp.float32
        ) * (1.0 / math.sqrt(size))
        powered = jnp.exp(scores - jnp.max(scores, axis=-1, keepdims=True))
        total = jnp.sum(powered, axis=-1, keepdims=True)
        summed = jnp.dot(powered.astype(jnp.bfloat16), v_all[:, lanes], preferred_element_type=jnp.float32)
        result = (summed / total).astype(jnp.bfloat16)
        for step in range(head_n):
            outs[step][:, lanes] = result[step * rows : (step + 1) * rows]


def join_kernel(count, me, *refs):
    width = refs[0].shape[1]
    for step in range(count):
        cols = pl.ds(pl.multiple_of((me[0] ^ step) * width, 128), width)
        refs[count][:, cols] = refs[step][...]


def local(
    head_n,
    patch_n,
    queries,
    keys,
    values,
    q_gain,
    k_gain,
    prev_keys,
    prev_values,
    res_keys,
    res_values,
    block_ids,
    scale_exps,
):
    bf16 = jnp.bfloat16
    heads = scale_exps.shape[1]
    width = prev_keys.shape[1]
    size = width // heads
    sent, block_len = res_keys.shape[:2]
    rows = queries.shape[0]
    fresh = sent * block_len
    tail = 16
    my_head = lax.axis_index("head").reshape(1)
    my_patch = lax.axis_index("patch").reshape(1)
    direct = patch_n <= DIRECT_PATCHES

    packed = pl.pallas_call(
        functools.partial(pack_kernel, sent, block_len, heads, size, tail),
        out_shape=jax.ShapeDtypeStruct((heads * 2 * fresh + tail, size), bf16),
        in_specs=[SM, SM, VM, VM],
        out_specs=VM,
        name="pack",
    )(block_ids, scale_exps, res_keys, res_values)
    if direct:
        residuals = [trade(packed, "patch", step, patch_n) for step in range(1, patch_n)]
    else:
        residuals = [lax.all_gather(packed, "patch", axis=0)]

    parts = pl.pallas_call(
        functools.partial(norm_kernel, head_n),
        out_shape=[jax.ShapeDtypeStruct((3 * rows, width), bf16)] * head_n,
        in_specs=[SM] + [VM] * 5,
        out_specs=[VM] * head_n,
        name="norm",
    )(my_head, queries, keys, values, q_gain.reshape(1, -1), k_gain.reshape(1, -1))
    parts = [parts[0]] + [trade(parts[step], "head", step, head_n) for step in range(1, head_n)]

    tok = rows * head_n
    total = tok * patch_n
    outs = pl.pallas_call(
        functools.partial(attend_kernel, head_n, patch_n, direct, sent, block_len, size),
        out_shape=[jax.ShapeDtypeStruct((rows, width), bf16)] * head_n,
        in_specs=[SM] + [VM] * (head_n + 2 + len(residuals)),
        out_specs=[VM] * head_n,
        scratch_shapes=[
            pltpu.VMEM((tok, width), bf16),
            pltpu.VMEM((total, width), bf16),
            pltpu.VMEM((total, width), bf16),
        ],
        compiler_params=pltpu.CompilerParams(vmem_limit_bytes=(16 if direct else 48) * 2**20),
        name="attend",
    )(my_patch, *parts, prev_keys, prev_values, *residuals)
    outs = [outs[0]] + [trade(outs[step], "head", step, head_n) for step in range(1, head_n)]
    return pl.pallas_call(
        functools.partial(join_kernel, head_n),
        out_shape=jax.ShapeDtypeStruct((rows, width * head_n), bf16),
        in_specs=[SM] + [VM] * head_n,
        out_specs=VM,
        name="join",
    )(my_head, *outs)


def solution(mesh):
    in_specs = (
        P(("groups", "patch", "head"), None),
        P(("groups", "patch", "head"), None),
        P(("groups", "patch", "head"), None),
        P(),
        P(),
        P("groups", "head"),
        P("groups", "head"),
        P(("groups", "patch"), None, "head"),
        P(("groups", "patch"), None, "head"),
        P(("groups", "patch")),
        P(("groups", "patch"), "head"),
    )
    out_specs = P(("groups", "patch", "head"), None)
    body = functools.partial(local, mesh.shape["head"], mesh.shape["patch"])
    return jax.shard_map(body, mesh=mesh, in_specs=in_specs, out_specs=out_specs, check_vma=False)
```

time: 86.8 us -> 31.2 us (0.36)
  blocking collectives: 52.8 us -> 0 us
  Pallas kernels: 0 us -> 6.88 us
  local copies, waits for them, and re-layouts: 9.55 us -> 5.14 us
  other arithmetic: 3.21 us -> 0 us
  waiting for transfers between devices: 6.68 us -> 9.41 us
  matrix products: 2.02 us -> 0 us
  starting transfers between devices: 11 us -> 9.35 us
  between operations: 0.93 us -> 0.04 us
    all_gather x3 -> x0, blocking collectives: 36.4 us -> none  [the longest x1 13.8 us: local(): residual_keys = lax.all_gather(res_keys, 'patch', axis=0, tiled=True)]
    all_to_all x3 -> x0, starting transfers between devices: 11 us -> none  [the longest x1 4.22 us: local(): lax.all_to_all(query_norm, 'head', split_axis=1, concat_axis=0, tiled=True)]
    ppermute x0 -> x9, waiting for transfers between devices: none -> 9.41 us  [trade(): return lax.ppermute(array, axis, [(i, i ^ step) for i in range(count)])]
    ppermute x0 -> x9, starting transfers between devices: none -> 9.35 us  [trade(): return lax.ppermute(array, axis, [(i, i ^ step) for i in range(count)])]
    unnamed x1 -> x0, blocking collectives: 9.07 us -> none
    all_to_all x1 -> x0, blocking collectives: 7.34 us -> none  [local(): lax.all_to_all(attended, 'head', split_axis=0, concat_axis=1, tiled=True)]
    pallas_call x0 -> x4, Pallas kernels: none -> 6.88 us  [the longest x1 2.04 us: local(): pl.pallas_call(functools.partial(norm_kernel, head_n), out_shape=[jax.Sha...]
    all_to_all x3 -> x0, waiting for transfers between devices: 6.68 us -> none  [the longest x1 3.71 us: local(): lax.all_to_all(key_norm, 'head', split_axis=1, concat_axis=0, tiled=True)]
  transfers between devices with their start and end apart: 3 -> 9, of which waited for: 2 -> 3; matrix products, arithmetic and copies ran while one was open for 9% -> 6% of each run, Pallas kernels for 0% -> 7%
where the time goes in v1:
time: 31.2 us; the launch traced here: 30.8 us
  waiting for transfers between devices  9.41 us (30%)
  starting transfers between devices  9.35 us (30%)
  Pallas kernels  6.88 us (22%)
  local copies, waits for them, and re-layouts  5.14 us (16%)
    ppermute x9, waiting for transfers between devices, trade(): return lax.ppermute(array, axis, [(i, i ^ step) for i in range(count)])  9.41 us
    ppermute x9, starting transfers between devices, trade(): return lax.ppermute(array, axis, [(i, i ^ step) for i in range(count)])  9.35 us
    unnamed x16, local copies, waits for them, and re-layouts  3.23 us
    pallas_call x1, Pallas kernels, local(): pl.pallas_call(functools.partial(norm_kernel, head_n), out_shape=[jax.Sha...  2.04 us
    pallas_call x1, Pallas kernels, local(): pl.pallas_call(functools.partial(attend_kernel, head_n, patch_n, direct,...  1.81 us
    pallas_call x1, Pallas kernels, local(): pl.pallas_call(functools.partial(pack_kernel, sent, block_len, heads, siz...  1.52 us
    pallas_call x1, Pallas kernels, local(): pl.pallas_call(functools.partial(join_kernel, head_n), out_shape=jax.Shap...  1.52 us
    reshape x1, local copies, waits for them, and re-layouts, local(): k_gain.reshape(1, -1)  1.31 us
  transfers between devices with their start and end apart: 9, of which 3 were waited for; matrix products, arithmetic and copies ran while one was open for 6% of the time, Pallas kernels for 7%

profile of v1, /device:TPU:0, one launch (start us, length us, event | category | flops | bytes accessed | tf_op | source)
XLA Modules:
  0.0 30.8 jit_solution(15786621543418327580)
XLA Ops:
  0.0 1.5 %pack.1 = bf16[336,128]{1,0:T(8,128)(2,1)} custom-call(s32[2]{0:T(128)} %ids.1, s32[2,5]{1,0:T(2,128)} %exps.1, bf16[2,16,640]{2,1,0:T(8,128)(2,1)} %res_k.1, bf16[2,16,640]{2,1,0:T(8,128)(2,1)} %res_v.1), custom_call_target="tpu_custom_call" | custom-call | tf_op jit(solution)/shard_map/pack/pallas_call | solution.py:150
  1.5 5.0 %collective-permute-start.5 = (bf16[336,128]{1,0:T(8,128)(2,1)}, bf16[336,128]{1,0:T(8,128)(2,1)S(1)}, u32[]{:S(2)}, u32[]{:S(2)}) collective-permute-start(bf16[336,128]{1,0:T(8,128)(2,1)} %pack.1), channel_id=1, source_target_pairs={{0,12},{4,8},{8,4},{12,0},{1,13},{5,9},{9,5},{13,1},{2,14},{6,10},... | collective-permute-start | bytes 258056 | tf_op jit(solution)/shard_map/ppermute | solution.py:18
  6.6 0.0 copy-done.7
  6.6 0.6 %reshape.14.qg_ref = f32[1,2560]{1,0:T(1,128)} reshape(f32[2560]{0:T(1024)S(1)} %copy-done.7) | data formatting | bytes 20480 | tf_op jit(solution)/shard_map/reshape | solution.py:168
  7.2 1.3 %reshape.15.kg_ref = f32[1,2560]{1,0:T(1,128)} reshape(f32[2560]{0:T(1024)} %param.15) | data formatting | bytes 20480 | tf_op jit(solution)/shard_map/reshape | solution.py:168
  8.5 2.0 %norm.1 = (bf16[96,640]{1,0:T(8,128)(2,1)}, bf16[96,640]{1,0:T(8,128)(2,1)}, bf16[96,640]{1,0:T(8,128)(2,1)}, bf16[96,640]{1,0:T(8,128)(2,1)}) custom-call(s32[1]{0:T(128)} %bitcast.me, bf16[32,2560]{1,0:T(8,128)(2,1)} %q_ref.1, bf16[32,2560]{1,0:T(8,128)(2,1)} %k_ref.1, bf16[32,2560]{1,0:T(8,128)(2,1)} %v_ref.1, f32[1,2560]{1,0:T(1,128)} %reshape.14.qg_ref, ...), custom_call_target="tpu_custom_call" | custom-call | tf_op jit(solution)/shard_map/norm/pallas_call | solution.py:162
  10.5 0.0 collective-permute-start
  10.5 1.5 %collective-permute-start.1 = (bf16[96,640]{1,0:T(8,128)(2,1)}, bf16[96,640]{1,0:T(8,128)(2,1)S(1)}, u32[]{:S(2)}, u32[]{:S(2)}) collective-permute-start(bf16[96,640]{1,0:T(8,128)(2,1)} %get-tuple-element.15), channel_id=1, source_target_pairs={{0,2},{1,3},{2,0},{3,1},{4,6},{5,7},{6,4},{7,5},{8,10},{9,11},{10,... | collective-permute-start | bytes 368648 | tf_op jit(solution)/shard_map/ppermute | solution.py:18
  12.0 0.4 %collective-permute-start.2 = (bf16[96,640]{1,0:T(8,128)(2,1)}, bf16[96,640]{1,0:T(8,128)(2,1)S(1)}, u32[]{:S(2)}, u32[]{:S(2)}) collective-permute-start(bf16[96,640]{1,0:T(8,128)(2,1)} %get-tuple-element.16), channel_id=1, source_target_pairs={{0,3},{1,2},{2,1},{3,0},{4,7},{5,6},{6,5},{7,4},{8,11},{9,10},{10,... | collective-permute-start | bytes 368648 | tf_op jit(solution)/shard_map/ppermute | solution.py:18
  12.4 0.0 collective-permute-start.4
  12.4 0.0 collective-permute-done.5.refs_8_
  12.4 0.6 %collective-permute-start.3 = (bf16[336,128]{1,0:T(8,128)(2,1)}, bf16[336,128]{1,0:T(8,128)(2,1)S(1)}, u32[]{:S(2)}, u32[]{:S(2)}) collective-permute-start(bf16[336,128]{1,0:T(8,128)(2,1)} %pack.1), channel_id=1, source_target_pairs={{0,4},{4,0},{8,12},{12,8},{1,5},{5,1},{9,13},{13,9},{2,6},{6,2},{1... | collective-permute-start | bytes 258056 | tf_op jit(solution)/shard_map/ppermute | solution.py:18
  13.0 6.2 %collective-permute-done.4.refs_7_ = bf16[336,128]{1,0:T(8,128)(2,1)S(1)} collective-permute-done((bf16[336,128]{1,0:T(8,128)(2,1)}, bf16[336,128]{1,0:T(8,128)(2,1)S(1)}, u32[]{:S(2)}, u32[]{:S(2)}) %collective-permute-start.4) | collective-permute-done | bytes 86048 | tf_op jit(solution)/shard_map/ppermute | solution.py:18
  19.2 0.0 collective-permute-done.3.refs_6_
  19.2 0.0 collective-permute-done.refs_1_
  19.2 0.0 collective-permute-done.1.refs_2_
  19.2 0.0 collective-permute-done.2.refs_3_
  19.2 0.0 copy-done
  19.2 0.0 copy-start.1
  19.2 1.1 %copy-done.1 = bf16[512,640]{1,0:T(8,128)(2,1)S(1)} copy-done((bf16[512,640]{1,0:T(8,128)(2,1)S(1)}, bf16[512,640]{1,0:T(8,128)(2,1)}, u32[]{:S(2)}) %copy-start.1) | copy-done | bytes 655384
  20.3 0.9 %copy-done.2 = bf16[96,640]{1,0:T(8,128)(2,1)S(1)} copy-done((bf16[96,640]{1,0:T(8,128)(2,1)S(1)}, bf16[96,640]{1,0:T(8,128)(2,1)}, u32[]{:S(2)}) %copy-start.2) | copy-done | bytes 122904
  21.2 1.8 %attend.1 = (bf16[32,640]{1,0:T(8,128)(2,1)S(1)}, bf16[32,640]{1,0:T(8,128)(2,1)S(1)}, bf16[32,640]{1,0:T(8,128)(2,1)S(1)}, bf16[32,640]{1,0:T(8,128)(2,1)S(1)}) custom-call(s32[1]{0:T(128)} %bitcast.1.me, bf16[96,640]{1,0:T(8,128)(2,1)S(1)} %copy-done.2, bf16[96,640]{1,0:T(8,128)(2,1)S(1)} %collective-permute-done.refs_1_, ...), custom_call_target="tpu_custom_call" | custom-call | tf_op jit(solution)/shard_map/attend/pallas_call | solution.py:173
  23.0 0.6 %copy-done.3 = bf16[32,640]{1,0:T(8,128)(2,1)} copy-done((bf16[32,640]{1,0:T(8,128)(2,1)}, bf16[32,640]{1,0:T(8,128)(2,1)S(1)}, u32[]{:S(2)}) %copy-start.3) | copy-done | bytes 40984
  23.6 0.0 collective-permute-start.6
  23.7 1.5 %collective-permute-start.7 = (bf16[32,640]{1,0:T(8,128)(2,1)S(1)}, bf16[32,640]{1,0:T(8,128)(2,1)S(1)}, u32[]{:S(2)}, u32[]{:S(2)}) collective-permute-start(bf16[32,640]{1,0:T(8,128)(2,1)S(1)} %get-tuple-element.19), channel_id=1, source_target_pairs={{0,2},{1,3},{2,0},{3,1},{4,6},{5,7},{6,4},{7,5},{8,10},{9,11},{10,... | collective-permute-start | bytes 122888 | tf_op jit(solution)/shard_map/ppermute | solution.py:18
  25.1 0.3 %collective-permute-start.8 = (bf16[32,640]{1,0:T(8,128)(2,1)S(1)}, bf16[32,640]{1,0:T(8,128)(2,1)S(1)}, u32[]{:S(2)}, u32[]{:S(2)}) collective-permute-start(bf16[32,640]{1,0:T(8,128)(2,1)S(1)} %get-tuple-element.20), channel_id=1, source_target_pairs={{0,3},{1,2},{2,1},{3,0},{4,7},{5,6},{6,5},{7,4},{8,11},{9,10},{10,... | collective-permute-start | bytes 122888 | tf_op jit(solution)/shard_map/ppermute | solution.py:18
  25.5 0.0 collective-permute-done.6.refs_1_
  25.5 2.2 %collective-permute-done.7.refs_2_ = bf16[32,640]{1,0:T(8,128)(2,1)S(1)} collective-permute-done((bf16[32,640]{1,0:T(8,128)(2,1)S(1)}, bf16[32,640]{1,0:T(8,128)(2,1)S(1)}, u32[]{:S(2)}, u32[]{:S(2)}) %collective-permute-start.7) | collective-permute-done | bytes 40992 | tf_op jit(solution)/shard_map/ppermute | solution.py:18
  27.7 1.0 %collective-permute-done.8.refs_3_ = bf16[32,640]{1,0:T(8,128)(2,1)S(1)} collective-permute-done((bf16[32,640]{1,0:T(8,128)(2,1)S(1)}, bf16[32,640]{1,0:T(8,128)(2,1)S(1)}, u32[]{:S(2)}, u32[]{:S(2)}) %collective-permute-start.8) | collective-permute-done | bytes 40992 | tf_op jit(solution)/shard_map/ppermute | solution.py:18
  28.7 0.0 copy-done.5
  28.7 0.6 %copy-done.6 = bf16[32,640]{1,0:T(8,128)(2,1)} copy-done((bf16[32,640]{1,0:T(8,128)(2,1)}, bf16[32,640]{1,0:T(8,128)(2,1)S(1)}, u32[]{:S(2)}) %copy-start.6) | copy-done | bytes 40984
  29.3 1.5 %join.1 = bf16[32,2560]{1,0:T(8,128)(2,1)} custom-call(s32[1]{0:T(128)} %bitcast.me, bf16[32,640]{1,0:T(8,128)(2,1)} %copy-done.3, bf16[32,640]{1,0:T(8,128)(2,1)} %copy-done.4, bf16[32,640]{1,0:T(8,128)(2,1)} %copy-done.5, bf16[32,640]{1,0:T(8,128)(2,1)} %copy-done.6), custom_call_target="tpu_custom_call" | custom-call | tf_op jit(solution)/shard_map/join/pallas_call | solution.py:187
  (8 shorter events, 0.0 us)
Async XLA Ops:
  0.0 6.6 %copy-start.7 = (f32[2560]{0:T(1024)S(1)}, f32[2560]{0:T(1024)}, u32[]{:S(2)}) copy-start(f32[2560]{0:T(1024)} %param.14) | copy-start | bytes 30724
  0.0 19.2 %copy-start = (bf16[512,640]{1,0:T(8,128)(2,1)S(1)}, bf16[512,640]{1,0:T(8,128)(2,1)}, u32[]{:S(2)}) copy-start(bf16[512,640]{1,0:T(8,128)(2,1)} %refs_4_.1) | copy-start | bytes 1966084
  1.5 10.9 %collective-permute-start.5 = (bf16[336,128]{1,0:T(8,128)(2,1)}, bf16[336,128]{1,0:T(8,128)(2,1)S(1)}, u32[]{:S(2)}, u32[]{:S(2)}) collective-permute-start(bf16[336,128]{1,0:T(8,128)(2,1)} %pack.1), channel_id=1, source_target_pairs={{0,12},{4,8},{8,4},{12,0},{1,13},{5,9},{9,5},{13,1},{2,14},{6,10},... | collective-permute-start | bytes 258056 | tf_op jit(solution)/shard_map/ppermute | solution.py:18
  10.5 8.7 %collective-permute-start = (bf16[96,640]{1,0:T(8,128)(2,1)}, bf16[96,640]{1,0:T(8,128)(2,1)S(1)}, u32[]{:S(2)}, u32[]{:S(2)}) collective-permute-start(bf16[96,640]{1,0:T(8,128)(2,1)} %get-tuple-element.14), channel_id=1, source_target_pairs={{0,1},{1,0},{2,3},{3,2},{4,5},{5,4},{6,7},{7,6},{8,9},{9,8},{10,11... | collective-permute-start | bytes 368648 | tf_op jit(solution)/shard_map/ppermute | solution.py:18
  10.5 8.7 %collective-permute-start.1 = (bf16[96,640]{1,0:T(8,128)(2,1)}, bf16[96,640]{1,0:T(8,128)(2,1)S(1)}, u32[]{:S(2)}, u32[]{:S(2)}) collective-permute-start(bf16[96,640]{1,0:T(8,128)(2,1)} %get-tuple-element.15), channel_id=1, source_target_pairs={{0,2},{1,3},{2,0},{3,1},{4,6},{5,7},{6,4},{7,5},{8,10},{9,11},{10,... | collective-permute-start | bytes 368648 | tf_op jit(solution)/shard_map/ppermute | solution.py:18
  12.0 7.2 %collective-permute-start.2 = (bf16[96,640]{1,0:T(8,128)(2,1)}, bf16[96,640]{1,0:T(8,128)(2,1)S(1)}, u32[]{:S(2)}, u32[]{:S(2)}) collective-permute-start(bf16[96,640]{1,0:T(8,128)(2,1)} %get-tuple-element.16), channel_id=1, source_target_pairs={{0,3},{1,2},{2,1},{3,0},{4,7},{5,6},{6,5},{7,4},{8,11},{9,10},{10,... | collective-permute-start | bytes 368648 | tf_op jit(solution)/shard_map/ppermute | solution.py:18
  12.4 6.8 %collective-permute-start.4 = (bf16[336,128]{1,0:T(8,128)(2,1)}, bf16[336,128]{1,0:T(8,128)(2,1)S(1)}, u32[]{:S(2)}, u32[]{:S(2)}) collective-permute-start(bf16[336,128]{1,0:T(8,128)(2,1)} %pack.1), channel_id=1, source_target_pairs={{0,8},{4,12},{8,0},{12,4},{1,9},{5,13},{9,1},{13,5},{2,10},{6,14},... | collective-permute-start | bytes 258056 | tf_op jit(solution)/shard_map/ppermute | solution.py:18
  12.4 6.8 %collective-permute-start.3 = (bf16[336,128]{1,0:T(8,128)(2,1)}, bf16[336,128]{1,0:T(8,128)(2,1)S(1)}, u32[]{:S(2)}, u32[]{:S(2)}) collective-permute-start(bf16[336,128]{1,0:T(8,128)(2,1)} %pack.1), channel_id=1, source_target_pairs={{0,4},{4,0},{8,12},{12,8},{1,5},{5,1},{9,13},{13,9},{2,6},{6,2},{1... | collective-permute-start | bytes 258056 | tf_op jit(solution)/shard_map/ppermute | solution.py:18
  19.2 1.1 %copy-start.1 = (bf16[512,640]{1,0:T(8,128)(2,1)S(1)}, bf16[512,640]{1,0:T(8,128)(2,1)}, u32[]{:S(2)}) copy-start(bf16[512,640]{1,0:T(8,128)(2,1)} %refs_5_.1) | copy-start | bytes 1966084
  20.3 0.9 %copy-start.2 = (bf16[96,640]{1,0:T(8,128)(2,1)S(1)}, bf16[96,640]{1,0:T(8,128)(2,1)}, u32[]{:S(2)}) copy-start(bf16[96,640]{1,0:T(8,128)(2,1)} %get-tuple-element.13.refs_0_) | copy-start | bytes 368644
  23.0 0.6 %copy-start.3 = (bf16[32,640]{1,0:T(8,128)(2,1)}, bf16[32,640]{1,0:T(8,128)(2,1)S(1)}, u32[]{:S(2)}) copy-start(bf16[32,640]{1,0:T(8,128)(2,1)S(1)} %get-tuple-element.17.refs_0_) | copy-start | bytes 122884
  23.6 1.9 %collective-permute-start.6 = (bf16[32,640]{1,0:T(8,128)(2,1)S(1)}, bf16[32,640]{1,0:T(8,128)(2,1)S(1)}, u32[]{:S(2)}, u32[]{:S(2)}) collective-permute-start(bf16[32,640]{1,0:T(8,128)(2,1)S(1)} %get-tuple-element.18), channel_id=1, source_target_pairs={{0,1},{1,0},{2,3},{3,2},{4,5},{5,4},{6,7},{7,6},{8,9},{9,8},{10,11... | collective-permute-start | bytes 122888 | tf_op jit(solution)/shard_map/ppermute | solution.py:18
  23.7 4.0 %collective-permute-start.7 = (bf16[32,640]{1,0:T(8,128)(2,1)S(1)}, bf16[32,640]{1,0:T(8,128)(2,1)S(1)}, u32[]{:S(2)}, u32[]{:S(2)}) collective-permute-start(bf16[32,640]{1,0:T(8,128)(2,1)S(1)} %get-tuple-element.19), channel_id=1, source_target_pairs={{0,2},{1,3},{2,0},{3,1},{4,6},{5,7},{6,4},{7,5},{8,10},{9,11},{10,... | collective-permute-start | bytes 122888 | tf_op jit(solution)/shard_map/ppermute | solution.py:18
  25.1 3.6 %collective-permute-start.8 = (bf16[32,640]{1,0:T(8,128)(2,1)S(1)}, bf16[32,640]{1,0:T(8,128)(2,1)S(1)}, u32[]{:S(2)}, u32[]{:S(2)}) collective-permute-start(bf16[32,640]{1,0:T(8,128)(2,1)S(1)} %get-tuple-element.20), channel_id=1, source_target_pairs={{0,3},{1,2},{2,1},{3,0},{4,7},{5,6},{6,5},{7,4},{8,11},{9,10},{10,... | collective-permute-start | bytes 122888 | tf_op jit(solution)/shard_map/ppermute | solution.py:18
  25.5 3.2 %copy-start.4 = (bf16[32,640]{1,0:T(8,128)(2,1)}, bf16[32,640]{1,0:T(8,128)(2,1)S(1)}, u32[]{:S(2)}) copy-start(bf16[32,640]{1,0:T(8,128)(2,1)S(1)} %collective-permute-done.6.refs_1_) | copy-start | bytes 122884
  27.7 1.0 %copy-start.5 = (bf16[32,640]{1,0:T(8,128)(2,1)}, bf16[32,640]{1,0:T(8,128)(2,1)S(1)}, u32[]{:S(2)}) copy-start(bf16[32,640]{1,0:T(8,128)(2,1)S(1)} %collective-permute-done.7.refs_2_) | copy-start | bytes 122884
  28.7 0.6 %copy-start.6 = (bf16[32,640]{1,0:T(8,128)(2,1)}, bf16[32,640]{1,0:T(8,128)(2,1)S(1)}, u32[]{:S(2)}) copy-start(bf16[32,640]{1,0:T(8,128)(2,1)S(1)} %collective-permute-done.8.refs_3_) | copy-start | bytes 122884

commit v2 on v1

--- a/solution.py
+++ b/solution.py
@@ -9,7 +9,6 @@
 from jax.sharding import PartitionSpec as P
 
 epsilon = 1e-06
-DIRECT_PATCHES = 8
 VM = pl.BlockSpec(memory_space=pltpu.VMEM)
 SM = pl.BlockSpec(memory_space=pltpu.SMEM)
 
@@ -18,7 +17,7 @@
     return lax.ppermute(array, axis, [(i, i ^ step) for i in range(count)])
 
 
-def pack_kernel(sent, block_len, heads, size, tail, ids, exps, res_k, res_v, out):
+def pack(sent, block_len, heads, size, tail, ids, exps, res_k, res_v, out):
     rows = sent * block_len
     for h in range(heads):
         for r in range(sent):
@@ -35,21 +34,37 @@
     out[pl.ds(heads * 2 * rows, tail), :] = numbers.astype(jnp.bfloat16)
 
 
-def norm_kernel(count, me, q_ref, k_ref, v_ref, qg_ref, kg_ref, *outs):
+def prepare_kernel(count, sent, block_len, heads, size, tail, n_in, me, *refs):
+    inputs, out, outs = refs[:n_in], refs[n_in], refs[n_in + 1 : n_in + 1 + count]
+    held, sems = refs[n_in + 1 + count : -1], refs[-1]
+    copies = [pltpu.make_async_copy(a, b, sems.at[i]) for i, (a, b) in enumerate(zip(inputs, held, strict=True))]
+    for copy in copies:
+        copy.start()
+    ids, exps, res_k, res_v, q_ref, qg_ref, k_ref, kg_ref, v_ref = held
+    for copy in copies[:4]:
+        copy.wait()
+    pack(sent, block_len, heads, size, tail, ids, exps, res_k, res_v, out)
     rows, width = q_ref.shape[0], q_ref.shape[1] // count
-
-    def inverse(ref):
+    columns = [pl.ds(pl.multiple_of((me[0] ^ step) * width, 128), width) for step in range(count)]
+    for at, (ref, gain) in enumerate(((q_ref, qg_ref), (k_ref, kg_ref))):
+        copies[4 + 2 * at].wait()
+        copies[5 + 2 * at].wait()
         x = ref[...].astype(jnp.float32)
-        return lax.rsqrt(jnp.mean(x * x, axis=-1, keepdims=True) + epsilon)
-
-    q_inv, k_inv = inverse(q_ref), inverse(k_ref)
-    for step in range(count):
-        cols = pl.ds(pl.multiple_of((me[0] ^ step) * width, 128), width)
-        q = q_ref[:, cols].astype(jnp.float32) * q_inv * qg_ref[:, cols]
-        k = k_ref[:, cols].astype(jnp.float32) * k_inv * kg_ref[:, cols]
-        outs[step][pl.ds(0, rows), :] = q.astype(jnp.bfloat16)
-        outs[step][pl.ds(rows, rows), :] = k.astype(jnp.bfloat16)
+        inverse = lax.rsqrt(jnp.mean(x * x, axis=-1, keepdims=True) + epsilon)
+        for step, cols in enumerate(columns):
+            normal = ref[:, cols].astype(jnp.float32) * inverse * gain[cols]
+            outs[step][pl.ds(at * rows, rows), :] = normal.astype(jnp.bfloat16)
+    copies[8].wait()
+    for step, cols in enumerate(columns):
         outs[step][pl.ds(2 * rows, rows), :] = v_ref[:, cols]
+
+
+def stage_kernel(k_ref, v_ref, k_out, v_out, sems):
+    copies = [pltpu.make_async_copy(k_ref, k_out, sems.at[0]), pltpu.make_async_copy(v_ref, v_out, sems.at[1])]
+    for copy in copies:
+        copy.start()
+    for copy in copies:
+        copy.wait()
 
 
 def attend_kernel(head_n, patch_n, direct, sent, block_len, size, me, *refs):
@@ -145,28 +160,42 @@
     tail = 16
     my_head = lax.axis_index("head").reshape(1)
     my_patch = lax.axis_index("patch").reshape(1)
-    direct = patch_n <= DIRECT_PATCHES
-
-    packed = pl.pallas_call(
-        functools.partial(pack_kernel, sent, block_len, heads, size, tail),
-        out_shape=jax.ShapeDtypeStruct((heads * 2 * fresh + tail, size), bf16),
-        in_specs=[SM, SM, VM, VM],
-        out_specs=VM,
-        name="pack",
-    )(block_ids, scale_exps, res_keys, res_values)
-    if direct:
-        residuals = [trade(packed, "patch", step, patch_n) for step in range(1, patch_n)]
+    direct = patch_n == 4
+
+    small = pltpu.CompilerParams(vmem_limit_bytes=8 * 2**20)
+    hbm = pl.BlockSpec(memory_space=pltpu.HBM)
+    in_hbm = functools.partial(pltpu.with_memory_space_constraint, memory_space=pltpu.HBM)
+    inputs = (block_ids, scale_exps, res_keys, res_values, queries, q_gain, keys, k_gain, values)
+    packed, *parts = pl.pallas_call(
+        functools.partial(prepare_kernel, head_n, sent, block_len, heads, size, tail, len(inputs)),
+        out_shape=[jax.ShapeDtypeStruct((heads * 2 * fresh + tail, size), bf16)]
+        + [jax.ShapeDtypeStruct((3 * rows, width), bf16)] * head_n,
+        in_specs=[SM] + [hbm] * len(inputs),
+        out_specs=[VM] * (head_n + 1),
+        scratch_shapes=[pltpu.SMEM(x.shape, x.dtype) for x in inputs[:2]]
+        + [pltpu.VMEM(x.shape, x.dtype) for x in inputs[2:]]
+        + [pltpu.SemaphoreType.DMA((len(inputs),))],
+        compiler_params=small,
+        name="prepare",
+    )(my_head, *[in_hbm(x) for x in inputs])
+    prev_keys, prev_values = pl.pallas_call(
+        stage_kernel,
+        out_shape=[jax.ShapeDtypeStruct(prev_keys.shape, bf16)] * 2,
+        in_specs=[hbm] * 2,
+        out_specs=[VM] * 2,
+        scratch_shapes=[pltpu.SemaphoreType.DMA((2,))],
+        compiler_params=pltpu.CompilerParams(vmem_limit_bytes=(8 if patch_n == 4 else 16) * 2**20),
+        cost_estimate=pl.CostEstimate(flops=0, bytes_accessed=4 * prev_keys.size, transcendentals=0),
+        name="stage",
+    )(in_hbm(prev_keys), in_hbm(prev_values))
+    if patch_n == 4:
+        far = trade(packed, "patch", 2, patch_n)
+        parts = [parts[0]] + [trade(parts[step], "head", step, head_n) for step in range(1, head_n)]
+        near = trade(packed, "patch", 1, patch_n)
+        residuals = [near, far, trade(far, "patch", 1, patch_n)]
     else:
+        parts = [parts[0]] + [trade(parts[step], "head", step, head_n) for step in range(1, head_n)]
         residuals = [lax.all_gather(packed, "patch", axis=0)]
-
-    parts = pl.pallas_call(
-        functools.partial(norm_kernel, head_n),
-        out_shape=[jax.ShapeDtypeStruct((3 * rows, width), bf16)] * head_n,
-        in_specs=[SM] + [VM] * 5,
-        out_specs=[VM] * head_n,
-        name="norm",
-    )(my_head, queries, keys, values, q_gain.reshape(1, -1), k_gain.reshape(1, -1))
-    parts = [parts[0]] + [trade(parts[step], "head", step, head_n) for step in range(1, head_n)]
 
     tok = rows * head_n
     total = tok * patch_n
@@ -180,7 +209,7 @@
             pltpu.VMEM((total, width), bf16),
             pltpu.VMEM((total, width), bf16),
         ],
-        compiler_params=pltpu.CompilerParams(vmem_limit_bytes=(16 if direct else 48) * 2**20),
+        compiler_params=pltpu.CompilerParams(vmem_limit_bytes=(8 if direct else 48) * 2**20),
         name="attend",
     )(my_patch, *parts, prev_keys, prev_values, *residuals)
     outs = [outs[0]] + [trade(outs[step], "head", step, head_n) for step in range(1, head_n)]
@@ -189,6 +218,7 @@
         out_shape=jax.ShapeDtypeStruct((rows, width * head_n), bf16),
         in_specs=[SM] + [VM] * head_n,
         out_specs=VM,
+        compiler_params=small,
         name="join",
     )(my_head, *outs)
 

time: 31.2 us -> 22.2 us (0.71)
  local copies, waits for them, and re-layouts: 5.14 us -> 0 us
  waiting for transfers between devices: 9.41 us -> 6.69 us
  Pallas kernels: 6.88 us -> 5.12 us
  starting transfers between devices: 9.35 us -> 10.2 us
    unnamed x16 -> x0, local copies, waits for them, and re-layouts: 3.23 us -> none
    ppermute x9, waiting for transfers between devices: 9.41 us -> 6.69 us  [trade(): return lax.ppermute(array, axis, [(i, i ^ step) for i in range(count)])]
    reshape x2 -> x0, local copies, waits for them, and re-layouts: 1.91 us -> none  [the longest x1 1.31 us: local(): k_gain.reshape(1, -1)]
    pallas_call x2, Pallas kernels: 3.56 us -> 2.64 us  [the longest x1 1.34 us: local(): pl.pallas_call(functools.partial(prepare_kernel, head_n, sent, block_len,...]
    ppermute x9, starting transfers between devices: 9.35 us -> 10.2 us  [trade(): return lax.ppermute(array, axis, [(i, i ^ step) for i in range(count)])]
    pallas_call x1, Pallas kernels: 1.52 us -> 0.68 us  [local(): pl.pallas_call(functools.partial(join_kernel, head_n), out_shape=jax.Shap...]
  transfers between devices with their start and end apart: 9 -> 9, of which waited for: 3 -> 6; matrix products, arithmetic and copies ran while one was open for 6% -> 0% of each run, Pallas kernels for 7% -> 6%
where the time goes in v2:
time: 22.2 us; the launch traced here: 22.1 us
  starting transfers between devices  10.2 us (46%)
  waiting for transfers between devices  6.69 us (30%)
  Pallas kernels  5.12 us (23%)
    ppermute x9, starting transfers between devices, trade(): return lax.ppermute(array, axis, [(i, i ^ step) for i in range(count)])  10.2 us
    ppermute x9, waiting for transfers between devices, trade(): return lax.ppermute(array, axis, [(i, i ^ step) for i in range(count)])  6.69 us
    pallas_call x1, Pallas kernels, local(): pl.pallas_call(functools.partial(attend_kernel, head_n, patch_n, direct,...  1.8 us
    pallas_call x1, Pallas kernels, local(): pl.pallas_call(functools.partial(prepare_kernel, head_n, sent, block_len,...  1.34 us
    pallas_call x1, Pallas kernels, local(): pl.pallas_call(stage_kernel, out_shape=[jax.ShapeDtypeStruct(prev_keys.sh...  1.3 us
    pallas_call x1, Pallas kernels, local(): pl.pallas_call(functools.partial(join_kernel, head_n), out_shape=jax.Shap...  0.68 us
  transfers between devices with their start and end apart: 9, of which 6 were waited for; matrix products, arithmetic and copies ran while one was open for 0% of the time, Pallas kernels for 6%

profile of v2, /device:TPU:0, one launch (start us, length us, event | category | flops | bytes accessed | tf_op | source)
XLA Modules:
  0.0 22.1 jit_solution(15021615259032331087)
XLA Ops:
  0.0 1.3 %prepare.1 = (bf16[336,128]{1,0:T(8,128)(2,1)S(1)}, bf16[96,640]{1,0:T(8,128)(2,1)S(1)}, bf16[96,640]{1,0:T(8,128)(2,1)S(1)}, bf16[96,640]{1,0:T(8,128)(2,1)S(1)}, bf16[96,640]{1,0:T(8,128)(2,1)S(1)}) custom-call(s32[1]{0:T(128)} %bitcast.me, s32[2]{0:T(128)} %refs_0_.1, s32[2,5]{1,0:T(2,128)} %refs_1_.1, bf16[2,16,640]{2,1,0:T(8,128)(2,1)} %refs_2_.1, ...), custom_call_target="tpu_custom_call" | custom-call | tf_op jit(solution)/shard_map/prepare/pallas_call | solution.py:169
  1.3 4.1 %collective-permute-start.4 = (bf16[336,128]{1,0:T(8,128)(2,1)S(1)}, bf16[336,128]{1,0:T(8,128)(2,1)S(1)}, u32[]{:S(2)}, u32[]{:S(2)}) collective-permute-start(bf16[336,128]{1,0:T(8,128)(2,1)S(1)} %get-tuple-element.22), channel_id=1, source_target_pairs={{0,8},{4,12},{8,0},{12,4},{1,9},{5,13},{9,1},{13,5},{2,10},{6,14},... | collective-permute-start | bytes 258056 | tf_op jit(solution)/shard_map/ppermute | solution.py:17
  5.5 0.0 collective-permute-start
  5.5 1.5 %collective-permute-start.1 = (bf16[96,640]{1,0:T(8,128)(2,1)S(1)}, bf16[96,640]{1,0:T(8,128)(2,1)S(1)}, u32[]{:S(2)}, u32[]{:S(2)}) collective-permute-start(bf16[96,640]{1,0:T(8,128)(2,1)S(1)} %get-tuple-element.18), channel_id=1, source_target_pairs={{0,2},{1,3},{2,0},{3,1},{4,6},{5,7},{6,4},{7,5},{8,10},{9,11},{10,... | collective-permute-start | bytes 368648 | tf_op jit(solution)/shard_map/ppermute | solution.py:17
  6.9 0.4 %collective-permute-start.2 = (bf16[96,640]{1,0:T(8,128)(2,1)S(1)}, bf16[96,640]{1,0:T(8,128)(2,1)S(1)}, u32[]{:S(2)}, u32[]{:S(2)}) collective-permute-start(bf16[96,640]{1,0:T(8,128)(2,1)S(1)} %get-tuple-element.19), channel_id=1, source_target_pairs={{0,3},{1,2},{2,1},{3,0},{4,7},{5,6},{6,5},{7,4},{8,11},{9,10},{10,... | collective-permute-start | bytes 368648 | tf_op jit(solution)/shard_map/ppermute | solution.py:17
  7.3 1.6 %collective-permute-start.3 = (bf16[336,128]{1,0:T(8,128)(2,1)S(1)}, bf16[336,128]{1,0:T(8,128)(2,1)S(1)}, u32[]{:S(2)}, u32[]{:S(2)}) collective-permute-start(bf16[336,128]{1,0:T(8,128)(2,1)S(1)} %get-tuple-element.22), channel_id=1, source_target_pairs={{0,4},{4,0},{8,12},{12,8},{1,5},{5,1},{9,13},{13,9},{2,6},{6,2},{1... | collective-permute-start | bytes 258056 | tf_op jit(solution)/shard_map/ppermute | solution.py:17
  8.9 0.9 %collective-permute-done.4.refs_7_ = bf16[336,128]{1,0:T(8,128)(2,1)S(1)} collective-permute-done((bf16[336,128]{1,0:T(8,128)(2,1)S(1)}, bf16[336,128]{1,0:T(8,128)(2,1)S(1)}, u32[]{:S(2)}, u32[]{:S(2)}) %collective-permute-start.4) | collective-permute-done | bytes 86048 | tf_op jit(solution)/shard_map/ppermute | solution.py:17
  9.8 0.8 %collective-permute-start.5 = (bf16[336,128]{1,0:T(8,128)(2,1)S(1)}, bf16[336,128]{1,0:T(8,128)(2,1)S(1)}, u32[]{:S(2)}, u32[]{:S(2)}) collective-permute-start(bf16[336,128]{1,0:T(8,128)(2,1)S(1)} %collective-permute-done.4.refs_7_), channel_id=1, source_target_pairs={{0,4},{4,0},{8,12},{12,8},{1,5},{5,1},{9,13},{13,9},{2,6},{6,2},{1... | collective-permute-start | bytes 258056 | tf_op jit(solution)/shard_map/ppermute | solution.py:17
  10.6 1.3 %stage.1 = (bf16[512,640]{1,0:T(8,128)(2,1)S(1)}, bf16[512,640]{1,0:T(8,128)(2,1)S(1)}) custom-call(bf16[512,640]{1,0:T(8,128)(2,1)} %k_ref.1, bf16[512,640]{1,0:T(8,128)(2,1)} %v_ref.1), custom_call_target="tpu_custom_call" | custom-call | bytes 1310720 | tf_op jit(solution)/shard_map/stage/pallas_call | solution.py:181
  11.9 0.7 %collective-permute-done.3.refs_6_ = bf16[336,128]{1,0:T(8,128)(2,1)S(1)} collective-permute-done((bf16[336,128]{1,0:T(8,128)(2,1)S(1)}, bf16[336,128]{1,0:T(8,128)(2,1)S(1)}, u32[]{:S(2)}, u32[]{:S(2)}) %collective-permute-start.3) | collective-permute-done | bytes 86048 | tf_op jit(solution)/shard_map/ppermute | solution.py:17
  12.6 0.0 collective-permute-done.refs_1_
  12.6 0.0 collective-permute-done.1.refs_2_
  12.6 0.8 %collective-permute-done.2.refs_3_ = bf16[96,640]{1,0:T(8,128)(2,1)S(1)} collective-permute-done((bf16[96,640]{1,0:T(8,128)(2,1)S(1)}, bf16[96,640]{1,0:T(8,128)(2,1)S(1)}, u32[]{:S(2)}, u32[]{:S(2)}) %collective-permute-start.2) | collective-permute-done | bytes 122912 | tf_op jit(solution)/shard_map/ppermute | solution.py:17
  13.4 0.9 %collective-permute-done.5.refs_8_ = bf16[336,128]{1,0:T(8,128)(2,1)S(1)} collective-permute-done((bf16[336,128]{1,0:T(8,128)(2,1)S(1)}, bf16[336,128]{1,0:T(8,128)(2,1)S(1)}, u32[]{:S(2)}, u32[]{:S(2)}) %collective-permute-start.5) | collective-permute-done | bytes 86048 | tf_op jit(solution)/shard_map/ppermute | solution.py:17
  14.3 1.8 %attend.1 = (bf16[32,640]{1,0:T(8,128)(2,1)S(1)}, bf16[32,640]{1,0:T(8,128)(2,1)S(1)}, bf16[32,640]{1,0:T(8,128)(2,1)S(1)}, bf16[32,640]{1,0:T(8,128)(2,1)S(1)}) custom-call(s32[1]{0:T(128)} %bitcast.1.me, bf16[96,640]{1,0:T(8,128)(2,1)S(1)} %get-tuple-element.16.refs_0_, bf16[96,640]{1,0:T(8,128)(2,1)S(1)} %collective-permute-done.refs_1_, ...), custom_call_target="tpu_custom_call" | custom-call | tf_op jit(solution)/shard_map/attend/pallas_call | solution.py:202
  16.1 0.1 collective-permute-start.6
  16.2 1.7 %collective-permute-start.7 = (bf16[32,640]{1,0:T(8,128)(2,1)S(1)}, bf16[32,640]{1,0:T(8,128)(2,1)S(1)}, u32[]{:S(2)}, u32[]{:S(2)}) collective-permute-start(bf16[32,640]{1,0:T(8,128)(2,1)S(1)} %get-tuple-element.25), channel_id=1, source_target_pairs={{0,2},{1,3},{2,0},{3,1},{4,6},{5,7},{6,4},{7,5},{8,10},{9,11},{10,... | collective-permute-start | bytes 122888 | tf_op jit(solution)/shard_map/ppermute | solution.py:17
  17.9 0.2 collective-permute-start.8
  18.0 0.0 collective-permute-done.6.refs_1_
  18.1 2.2 %collective-permute-done.7.refs_2_ = bf16[32,640]{1,0:T(8,128)(2,1)S(1)} collective-permute-done((bf16[32,640]{1,0:T(8,128)(2,1)S(1)}, bf16[32,640]{1,0:T(8,128)(2,1)S(1)}, u32[]{:S(2)}, u32[]{:S(2)}) %collective-permute-start.7) | collective-permute-done | bytes 40992 | tf_op jit(solution)/shard_map/ppermute | solution.py:17
  20.3 1.2 %collective-permute-done.8.refs_3_ = bf16[32,640]{1,0:T(8,128)(2,1)S(1)} collective-permute-done((bf16[32,640]{1,0:T(8,128)(2,1)S(1)}, bf16[32,640]{1,0:T(8,128)(2,1)S(1)}, u32[]{:S(2)}, u32[]{:S(2)}) %collective-permute-start.8) | collective-permute-done | bytes 40992 | tf_op jit(solution)/shard_map/ppermute | solution.py:17
  21.4 0.7 %join.1 = bf16[32,2560]{1,0:T(8,128)(2,1)} custom-call(s32[1]{0:T(128)} %bitcast.me, bf16[32,640]{1,0:T(8,128)(2,1)S(1)} %get-tuple-element.23.refs_0_, bf16[32,640]{1,0:T(8,128)(2,1)S(1)} %collective-permute-done.6.refs_1_, bf16[32,640]{1,0:T(8,128)(2,1)S(1)} %collective-permute-done.7.refs_2_, bf16[32,640]{1,0:T(8,128)(2,1)S(1)} %collective-permute-done.8.refs_3_), custom_call_target="tpu_custom_call" | custom-call | tf_op jit(solution)/shard_map/join/pallas_call | solution.py:216
Async XLA Ops:
  1.3 8.5 %collective-permute-start.4 = (bf16[336,128]{1,0:T(8,128)(2,1)S(1)}, bf16[336,128]{1,0:T(8,128)(2,1)S(1)}, u32[]{:S(2)}, u32[]{:S(2)}) collective-permute-start(bf16[336,128]{1,0:T(8,128)(2,1)S(1)} %get-tuple-element.22), channel_id=1, source_target_pairs={{0,8},{4,12},{8,0},{12,4},{1,9},{5,13},{9,1},{13,5},{2,10},{6,14},... | collective-permute-start | bytes 258056 | tf_op jit(solution)/shard_map/ppermute | solution.py:17
  5.5 7.2 %collective-permute-start = (bf16[96,640]{1,0:T(8,128)(2,1)S(1)}, bf16[96,640]{1,0:T(8,128)(2,1)S(1)}, u32[]{:S(2)}, u32[]{:S(2)}) collective-permute-start(bf16[96,640]{1,0:T(8,128)(2,1)S(1)} %get-tuple-element.17), channel_id=1, source_target_pairs={{0,1},{1,0},{2,3},{3,2},{4,5},{5,4},{6,7},{7,6},{8,9},{9,8},{10,11... | collective-permute-start | bytes 368648 | tf_op jit(solution)/shard_map/ppermute | solution.py:17
  5.5 7.2 %collective-permute-start.1 = (bf16[96,640]{1,0:T(8,128)(2,1)S(1)}, bf16[96,640]{1,0:T(8,128)(2,1)S(1)}, u32[]{:S(2)}, u32[]{:S(2)}) collective-permute-start(bf16[96,640]{1,0:T(8,128)(2,1)S(1)} %get-tuple-element.18), channel_id=1, source_target_pairs={{0,2},{1,3},{2,0},{3,1},{4,6},{5,7},{6,4},{7,5},{8,10},{9,11},{10,... | collective-permute-start | bytes 368648 | tf_op jit(solution)/shard_map/ppermute | solution.py:17
  6.9 6.5 %collective-permute-start.2 = (bf16[96,640]{1,0:T(8,128)(2,1)S(1)}, bf16[96,640]{1,0:T(8,128)(2,1)S(1)}, u32[]{:S(2)}, u32[]{:S(2)}) collective-permute-start(bf16[96,640]{1,0:T(8,128)(2,1)S(1)} %get-tuple-element.19), channel_id=1, source_target_pairs={{0,3},{1,2},{2,1},{3,0},{4,7},{5,6},{6,5},{7,4},{8,11},{9,10},{10,... | collective-permute-start | bytes 368648 | tf_op jit(solution)/shard_map/ppermute | solution.py:17
  7.3 5.3 %collective-permute-start.3 = (bf16[336,128]{1,0:T(8,128)(2,1)S(1)}, bf16[336,128]{1,0:T(8,128)(2,1)S(1)}, u32[]{:S(2)}, u32[]{:S(2)}) collective-permute-start(bf16[336,128]{1,0:T(8,128)(2,1)S(1)} %get-tuple-element.22), channel_id=1, source_target_pairs={{0,4},{4,0},{8,12},{12,8},{1,5},{5,1},{9,13},{13,9},{2,6},{6,2},{1... | collective-permute-start | bytes 258056 | tf_op jit(solution)/shard_map/ppermute | solution.py:17
  9.8 4.5 %collective-permute-start.5 = (bf16[336,128]{1,0:T(8,128)(2,1)S(1)}, bf16[336,128]{1,0:T(8,128)(2,1)S(1)}, u32[]{:S(2)}, u32[]{:S(2)}) collective-permute-start(bf16[336,128]{1,0:T(8,128)(2,1)S(1)} %collective-permute-done.4.refs_7_), channel_id=1, source_target_pairs={{0,4},{4,0},{8,12},{12,8},{1,5},{5,1},{9,13},{13,9},{2,6},{6,2},{1... | collective-permute-start | bytes 258056 | tf_op jit(solution)/shard_map/ppermute | solution.py:17
  16.1 1.9 %collective-permute-start.6 = (bf16[32,640]{1,0:T(8,128)(2,1)S(1)}, bf16[32,640]{1,0:T(8,128)(2,1)S(1)}, u32[]{:S(2)}, u32[]{:S(2)}) collective-permute-start(bf16[32,640]{1,0:T(8,128)(2,1)S(1)} %get-tuple-element.24), channel_id=1, source_target_pairs={{0,1},{1,0},{2,3},{3,2},{4,5},{5,4},{6,7},{7,6},{8,9},{9,8},{10,11... | collective-permute-start | bytes 122888 | tf_op jit(solution)/shard_map/ppermute | solution.py:17
  16.2 4.1 %collective-permute-start.7 = (bf16[32,640]{1,0:T(8,128)(2,1)S(1)}, bf16[32,640]{1,0:T(8,128)(2,1)S(1)}, u32[]{:S(2)}, u32[]{:S(2)}) collective-permute-start(bf16[32,640]{1,0:T(8,128)(2,1)S(1)} %get-tuple-element.25), channel_id=1, source_target_pairs={{0,2},{1,3},{2,0},{3,1},{4,6},{5,7},{6,4},{7,5},{8,10},{9,11},{10,... | collective-permute-start | bytes 122888 | tf_op jit(solution)/shard_map/ppermute | solution.py:17
  17.9 3.5 %collective-permute-start.8 = (bf16[32,640]{1,0:T(8,128)(2,1)S(1)}, bf16[32,640]{1,0:T(8,128)(2,1)S(1)}, u32[]{:S(2)}, u32[]{:S(2)}) collective-permute-start(bf16[32,640]{1,0:T(8,128)(2,1)S(1)} %get-tuple-element.26), channel_id=1, source_target_pairs={{0,3},{1,2},{2,1},{3,0},{4,7},{5,6},{6,5},{7,4},{8,11},{9,10},{10,... | collective-permute-start | bytes 122888 | tf_op jit(solution)/shard_map/ppermute | solution.py:17

commit v3 on v2

v3 whole, which is shorter than its diff:
```python
import functools
import math

import jax
import jax.numpy as jnp
from jax import lax
from jax.experimental import pallas as pl
from jax.experimental.pallas import tpu as pltpu
from jax.sharding import PartitionSpec as P

epsilon = 1e-06
tail = 16
VM = pl.BlockSpec(memory_space=pltpu.VMEM)
SM = pl.BlockSpec(memory_space=pltpu.SMEM)
HB = pl.BlockSpec(memory_space=pltpu.HBM)
in_hbm = functools.partial(pltpu.with_memory_space_constraint, memory_space=pltpu.HBM)


def trade(array, axis, step, count):
    return lax.ppermute(array, axis, [(i, i ^ step) for i in range(count)])


def order_of(count):
    return [*range(2, count), *range(min(2, count))]


def in_turn(refs):
    turned = dict(zip(order_of(len(refs)), refs, strict=True))
    return [turned[step] for step in range(len(refs))]


def start_all(pairs, sems):
    copies = [pltpu.make_async_copy(a, b, sems.at[i]) for i, (a, b) in enumerate(pairs)]
    for copy in copies:
        copy.start()
    return copies


def prepare_kernel(count, n_in, me, *refs):
    inputs, both, outs = refs[:n_in], refs[n_in], refs[n_in + 1 : n_in + 1 + count]
    held, sems = refs[n_in + 1 + count : -1], refs[-1]
    copies = start_all(zip(inputs, held, strict=True), sems)
    ids, exps, res_k, res_v, q_ref, qg_ref, k_ref, kg_ref, v_ref = held

    sent, block_len = res_k.shape[:2]
    heads = exps.shape[1]
    size = res_k.shape[2] // heads
    after = heads * sent * block_len + tail
    for copy in copies[:4]:
        copy.wait()
    for h in range(heads):
        for r in range(sent):
            power = (1 << (exps[r, h] + 16)).astype(jnp.float32) * (1.0 / 65536.0)
            lanes = pl.ds(h * size, size)
            at = (h * sent + r) * block_len
            k = (res_k[r, :, lanes].astype(jnp.float32) * power).astype(jnp.bfloat16)
            v = (res_v[r, :, lanes].astype(jnp.float32) * power).astype(jnp.bfloat16)
            both[pl.ds(at, block_len), :] = k
            both[pl.ds(after + at, block_len), :] = v
    lane = lax.broadcasted_iota(jnp.int32, (tail, size), 1) // block_len
    numbers = jnp.zeros((tail, size), jnp.float32)
    for r in range(sent):
        numbers = jnp.where(lane == r, ids[r].astype(jnp.float32), numbers)
    both[pl.ds(after - tail, tail), :] = numbers.astype(jnp.bfloat16)

    rows, width = q_ref.shape[0], q_ref.shape[1] // count
    columns = [pl.ds(pl.multiple_of((me[0] ^ step) * width, 128), width) for step in range(count)]
    for at, (ref, gain) in enumerate(((q_ref, qg_ref), (k_ref, kg_ref))):
        copies[4 + 2 * at].wait()
        copies[5 + 2 * at].wait()
        x = ref[...].astype(jnp.float32)
        inverse = lax.rsqrt(jnp.mean(x * x, axis=-1, keepdims=True) + epsilon)
        for step, cols in enumerate(columns):
            normal = ref[:, cols].astype(jnp.float32) * inverse * gain[cols]
            outs[step][pl.ds(at * rows, rows), :] = normal.astype(jnp.bfloat16)
    copies[8].wait()
    for step, cols in enumerate(columns):
        outs[step][pl.ds(2 * rows, rows), :] = v_ref[:, cols]


def chooser(tok, fresh, block_len, packed_k, rows_k):
    row = lax.broadcasted_iota(jnp.int32, (tok, fresh), 0)
    col = lax.broadcasted_iota(jnp.int32, (tok, fresh), 1)
    numbers = packed_k[pl.ds(rows_k, tail), :].astype(jnp.float32)[0:1, :fresh]
    return jnp.logical_and(
        row % block_len == col % block_len, (row // block_len).astype(jnp.float32) == numbers
    ).astype(jnp.bfloat16)


def refresh(chosen, old, source, new, target, residual, first):
    fresh = chosen.shape[1]
    size = residual.shape[1]
    for h in range(new.shape[1] // size):
        lanes = pl.ds(h * size, size)
        change = jnp.dot(
            chosen, residual[pl.ds(first + h * fresh, fresh), :], preferred_element_type=jnp.float32
        )
        new[target, lanes] = (old[source, lanes].astype(jnp.float32) + change).astype(jnp.bfloat16)


def stage_kernel(steps, early, tok, fresh, block_len, n_res, me, k_ref, v_ref, *refs):
    res, (k_out, v_out, sems) = refs[:n_res], refs[n_res:]
    pairs = []
    for place, step in enumerate(steps):
        source = pl.ds(pl.multiple_of((me[0] ^ step) * tok, 128), tok)
        target = pl.ds(place * tok, tok)
        pairs += [(k_ref.at[source], k_out.at[target]), (v_ref.at[source], v_out.at[target])]
    copies = start_all(pairs, sems)
    rows_k = k_out.shape[1] // res[0].shape[-1] * fresh

    def one(place, packed):
        rows = place * tok
        rows = pl.ds(rows if isinstance(place, int) else pl.multiple_of(rows, 128), tok)
        chosen = chooser(tok, fresh, block_len, packed, rows_k)
        refresh(chosen, k_out, rows, k_out, rows, packed, 0)
        refresh(chosen, v_out, rows, v_out, rows, packed, rows_k + tail)

    for copy in copies:
        copy.wait()
    if early:
        for place in range(early):
            one(place, res[place])
    else:

        @pl.loop(1, len(steps) + 1)
        def _(step):
            one(step - 1, res[0].at[me[0] ^ step])


def scored(q, keys):
    return lax.dot_general(
        q, keys, (((1,), (1,)), ((), ())), preferred_element_type=jnp.float32
    ) * (math.log2(math.e) / math.sqrt(q.shape[1]))


def score_kernel(count, n_now, ahead, block_len, fresh, size, *refs):
    (k_st, v_st), now, parts = refs[:2], refs[2 : 2 + n_now], in_turn(refs[2 + n_now : 2 + n_now + count])
    q_all, v_own, scores, k_own = refs[2 + n_now + count :]
    rows = parts[0].shape[0] // 3
    tok = rows * count
    heads = parts[0].shape[1] // size
    for place, packed in enumerate(now):
        chosen = chooser(tok, fresh, block_len, packed, heads * fresh)
        source, target = pl.ds(ahead + place * tok, tok), pl.ds((1 + place) * tok, tok)
        refresh(chosen, k_st, source, k_own, target, packed, 0)
        refresh(chosen, v_st, source, v_own, target, packed, heads * fresh + tail)
    for step in range(count):
        q_all[pl.ds(step * rows, rows), :] = parts[step][pl.ds(0, rows), :]
        k_own[pl.ds(step * rows, rows), :] = parts[step][pl.ds(rows, rows), :]
        v_own[pl.ds(step * rows, rows), :] = parts[step][pl.ds(2 * rows, rows), :]
    for h in range(heads):
        lanes = pl.ds(h * size, size)
        scores[h, :, pl.ds(0, ahead)] = scored(q_all[:, lanes], k_st[pl.ds(0, ahead), lanes])
        scores[h, :, pl.ds(ahead, k_own.shape[0])] = scored(q_all[:, lanes], k_own[:, lanes])


def finish_kernel(count, n_late, ahead, block_len, fresh, size, *refs):
    (k_st, v_st, q_all, v_own, scores), late = refs[:5], refs[5 : 5 + n_late]
    outs, (k_new, v_new) = refs[5 + n_late : -2], refs[-2:]
    tok = q_all.shape[0]
    rows = tok // count
    heads = q_all.shape[1] // size
    for packed in late:
        chosen = chooser(tok, fresh, block_len, packed, heads * fresh)
        source, target = pl.ds(k_st.shape[0] - tok, tok), pl.ds(0, tok)
        refresh(chosen, k_st, source, k_new, target, packed, 0)
        refresh(chosen, v_st, source, v_new, target, packed, heads * fresh + tail)
    columns = [pl.ds(h * size, size) for h in range(heads)]
    together = heads if late else 1
    for first in range(0, heads, together):
        group = range(first, first + together)
        cut = {h: [scores[h, :, pl.ds(0, ahead)], scores[h, :, pl.ds(ahead, v_own.shape[0])]] for h in group}
        held = {h: [v_st[pl.ds(0, ahead), columns[h]], v_own[:, columns[h]]] for h in group}
        if late:
            for h in group:
                cut[h].append(scored(q_all[:, columns[h]], k_new[:, columns[h]]))
                held[h].append(v_new[:, columns[h]])
        peaks = {h: row_fold(jnp.maximum, jnp.max, cut[h]) for h in group}
        powered, summed = {}, {}
        for h in group:
            powered[h] = [jnp.exp2(part - peaks[h]) for part in cut[h]]
            summed[h] = jnp.dot(
                jnp.concatenate([part.astype(jnp.bfloat16) for part in powered[h]], axis=1),
                jnp.concatenate(held[h], axis=0),
                preferred_element_type=jnp.float32,
            )
        totals = {h: row_fold(jnp.add, jnp.sum, powered[h]) for h in group}
        for h in group:
            result = (summed[h] / totals[h]).astype(jnp.bfloat16)
            for step in range(count):
                outs[step][:, columns[h]] = result[step * rows : (step + 1) * rows]


def row_fold(both, along, parts):
    blocks = [part[:, at : at + 128] for part in parts for at in range(0, part.shape[1], 128)]
    return along(functools.reduce(both, blocks), axis=-1, keepdims=True)


def join_kernel(count, me, *refs):
    parts, out = in_turn(refs[:count]), refs[count]
    width = parts[0].shape[1]
    for step in range(count):
        out[:, pl.ds(pl.multiple_of((me[0] ^ step) * width, 128), width)] = parts[step][...]


def local(
    head_n,
    patch_n,
    queries,
    keys,
    values,
    q_gain,
    k_gain,
    prev_keys,
    prev_values,
    res_keys,
    res_values,
    block_ids,
    scale_exps,
):
    bf16 = jnp.bfloat16
    heads = scale_exps.shape[1]
    width = prev_keys.shape[1]
    size = width // heads
    sent, block_len = res_keys.shape[:2]
    rows = queries.shape[0]
    tok = rows * head_n
    fresh = sent * block_len
    my_head = lax.axis_index("head").reshape(1)
    my_patch = lax.axis_index("patch").reshape(1)
    four = patch_n == 4
    grant = pltpu.CompilerParams(vmem_limit_bytes=8 * 2**20)
    larger = grant if four else pltpu.CompilerParams(vmem_limit_bytes=24 * 2**20)

    def shape(*dims):
        return jax.ShapeDtypeStruct(dims, bf16)

    inputs = (block_ids, scale_exps, res_keys, res_values, queries, q_gain, keys, k_gain, values)
    both, *parts = pl.pallas_call(
        functools.partial(prepare_kernel, head_n, len(inputs)),
        out_shape=[shape(2 * heads * fresh + tail, size)] + [shape(3 * rows, width)] * head_n,
        in_specs=[SM] + [HB] * len(inputs),
        out_specs=[VM] * (head_n + 1),
        scratch_shapes=[pltpu.SMEM(x.shape, x.dtype) for x in inputs[:2]]
        + [pltpu.VMEM(x.shape, x.dtype) for x in inputs[2:]]
        + [pltpu.SemaphoreType.DMA((len(inputs),))],
        compiler_params=grant,
        name="prepare",
    )(my_head, *[in_hbm(x) for x in inputs])

    if four:
        near = trade(both, "patch", 1, patch_n)
        far = trade(both, "patch", 2, patch_n)
        residuals = [far]
        steps, late = [2, 1, 3], [near]
    else:
        residuals = [lax.all_gather(both, "patch", axis=0)]
        steps, late = range(1, patch_n), []
    order = order_of(head_n)
    parts = [trade(parts[step], "head", step, head_n) if step else parts[0] for step in range(head_n)]
    now = late
    late = [trade(far, "patch", 1, patch_n)] if four else []

    others = (patch_n - 1) * tok
    stale_k, stale_v = pl.pallas_call(
        functools.partial(stage_kernel, steps, 1 if four else 0, tok, fresh, block_len, len(residuals)),
        out_shape=[shape(others, width)] * 2,
        in_specs=[SM] + [HB] * 2 + [VM] * len(residuals),
        out_specs=[VM] * 2,
        scratch_shapes=[pltpu.SemaphoreType.DMA((2 * (patch_n - 1),))],
        compiler_params=larger,
        name="stage",
    )(my_patch, in_hbm(prev_keys), in_hbm(prev_values), *residuals)

    ahead = others - (len(now) + len(late)) * tok
    own = (1 + len(now)) * tok
    kept = jax.ShapeDtypeStruct((heads, tok, ahead + own), jnp.float32)
    q_all, v_own, scores = pl.pallas_call(
        functools.partial(score_kernel, head_n, len(now), ahead, block_len, fresh, size),
        out_shape=[shape(tok, width), shape(own, width), kept],
        in_specs=[VM] * (head_n + 2 + len(now)),
        out_specs=[VM] * 3,
        scratch_shapes=[pltpu.VMEM((own, width), bf16)],
        compiler_params=larger,
        name="score",
    )(stale_k, stale_v, *now, *[parts[step] for step in order])
    outs = pl.pallas_call(
        functools.partial(finish_kernel, head_n, len(late), ahead, block_len, fresh, size),
        out_shape=[shape(rows, width)] * head_n,
        in_specs=[VM] * (5 + len(late)),
        out_specs=[VM] * head_n,
        scratch_shapes=[pltpu.VMEM((tok, width), bf16)] * 2,
        compiler_params=larger,
        name="finish",
    )(stale_k, stale_v, q_all, v_own, scores, *late)
    outs = [trade(outs[step], "head", step, head_n) if step else outs[0] for step in range(head_n)]
    return pl.pallas_call(
        functools.partial(join_kernel, head_n),
        out_shape=shape(rows, width * head_n),
        in_specs=[SM] + [VM] * head_n,
        out_specs=VM,
        compiler_params=grant,
        name="join",
    )(my_head, *[outs[step] for step in order])


def solution(mesh):
    in_specs = (
        P(("groups", "patch", "head"), None),
        P(("groups", "patch", "head"), None),
        P(("groups", "patch", "head"), None),
        P(),
        P(),
        P("groups", "head"),
        P("groups", "head"),
        P(("groups", "patch"), None, "head"),
        P(("groups", "patch"), None, "head"),
        P(("groups", "patch")),
        P(("groups", "patch"), "head"),
    )
    out_specs = P(("groups", "patch", "head"), None)
    body = functools.partial(local, mesh.shape["head"], mesh.shape["patch"])
    return jax.shard_map(body, mesh=mesh, in_specs=in_specs, out_specs=out_specs, check_vma=False)
```

time: 22.2 us -> 21 us (0.946)
  waiting for transfers between devices: 6.69 us -> 5.2 us
  starting transfers between devices: 10.2 us -> 10.8 us
  Pallas kernels: 5.12 us -> 4.83 us
    ppermute x9, waiting for transfers between devices: 6.69 us -> 5.2 us  [trade(): return lax.ppermute(array, axis, [(i, i ^ step) for i in range(count)])]
    ppermute x9, starting transfers between devices: 10.2 us -> 10.8 us  [trade(): return lax.ppermute(array, axis, [(i, i ^ step) for i in range(count)])]
    pallas_call x4 -> x5, Pallas kernels: 5.12 us -> 4.83 us  [the longest x1 1.56 us: local(): pl.pallas_call(functools.partial(stage_kernel, steps, 1 if four else 0, t...]
  transfers between devices with their start and end apart: 9 -> 9, of which waited for: 6 -> 5; matrix products, arithmetic and copies ran while one was open for 0% -> 0% of each run, Pallas kernels for 6% -> 10%
where the time goes in v3:
time: 21 us; the launch traced here: 20.9 us
  starting transfers between devices  10.8 us (51%)
  waiting for transfers between devices  5.2 us (25%)
  Pallas kernels  4.83 us (23%)
    ppermute x9, starting transfers between devices, trade(): return lax.ppermute(array, axis, [(i, i ^ step) for i in range(count)])  10.8 us
    ppermute x9, waiting for transfers between devices, trade(): return lax.ppermute(array, axis, [(i, i ^ step) for i in range(count)])  5.2 us
    pallas_call x1, Pallas kernels, local(): pl.pallas_call(functools.partial(stage_kernel, steps, 1 if four else 0, t...  1.56 us
    pallas_call x1, Pallas kernels, local(): pl.pallas_call(functools.partial(prepare_kernel, head_n, len(inputs)), ou...  1.34 us
    pallas_call x1, Pallas kernels, local(): pl.pallas_call(functools.partial(finish_kernel, head_n, len(late), ahead,...  0.73 us
    pallas_call x1, Pallas kernels, local(): pl.pallas_call(functools.partial(join_kernel, head_n), out_shape=shape(ro...  0.68 us
    pallas_call x1, Pallas kernels, local(): pl.pallas_call(functools.partial(score_kernel, head_n, len(now), ahead, b...  0.51 us
  transfers between devices with their start and end apart: 9, of which 5 were waited for; matrix products, arithmetic and copies ran while one was open for 0% of the time, Pallas kernels for 10%

profile of v3, /device:TPU:0, one launch (start us, length us, event | category | flops | bytes accessed | tf_op | source)
XLA Modules:
  0.0 20.9 jit_solution(9362365320689367660)
XLA Ops:
  0.0 1.3 %prepare.1 = (bf16[336,128]{1,0:T(8,128)(2,1)S(1)}, bf16[96,640]{1,0:T(8,128)(2,1)S(1)}, bf16[96,640]{1,0:T(8,128)(2,1)S(1)}, bf16[96,640]{1,0:T(8,128)(2,1)S(1)}, bf16[96,640]{1,0:T(8,128)(2,1)S(1)}) custom-call(s32[1]{0:T(128)} %bitcast.me, s32[2]{0:T(128)} %refs_0_.1, s32[2,5]{1,0:T(2,128)} %refs_1_.1, bf16[2,16,640]{2,1,0:T(8,128)(2,1)} %refs_2_.1, ...), custom_call_target="tpu_custom_call" | custom-call | tf_op jit(solution)/shard_map/prepare/pallas_call | solution.py:239
  1.3 4.1 %collective-permute-start = (bf16[336,128]{1,0:T(8,128)(2,1)S(1)}, bf16[336,128]{1,0:T(8,128)(2,1)S(1)}, u32[]{:S(2)}, u32[]{:S(2)}) collective-permute-start(bf16[336,128]{1,0:T(8,128)(2,1)S(1)} %get-tuple-element.19), channel_id=1, source_target_pairs={{0,8},{4,12},{8,0},{12,4},{1,9},{5,13},{9,1},{13,5},{2,10},{6,14},... | collective-permute-start | bytes 258056 | tf_op jit(solution)/shard_map/ppermute | solution.py:20
  5.5 1.5 %collective-permute-start.2 = (bf16[96,640]{1,0:T(8,128)(2,1)S(1)}, bf16[96,640]{1,0:T(8,128)(2,1)S(1)}, u32[]{:S(2)}, u32[]{:S(2)}) collective-permute-start(bf16[96,640]{1,0:T(8,128)(2,1)S(1)} %get-tuple-element.22), channel_id=1, source_target_pairs={{0,2},{1,3},{2,0},{3,1},{4,6},{5,7},{6,4},{7,5},{8,10},{9,11},{10,... | collective-permute-start | bytes 368648 | tf_op jit(solution)/shard_map/ppermute | solution.py:20
  6.9 0.0 collective-permute-start.3
  6.9 0.6 %collective-permute-start.4 = (bf16[96,640]{1,0:T(8,128)(2,1)S(1)}, bf16[96,640]{1,0:T(8,128)(2,1)S(1)}, u32[]{:S(2)}, u32[]{:S(2)}) collective-permute-start(bf16[96,640]{1,0:T(8,128)(2,1)S(1)} %get-tuple-element.25), channel_id=1, source_target_pairs={{0,1},{1,0},{2,3},{3,2},{4,5},{5,4},{6,7},{7,6},{8,9},{9,8},{10,11... | collective-permute-start | bytes 368648 | tf_op jit(solution)/shard_map/ppermute | solution.py:20
  7.6 1.6 %collective-permute-start.1 = (bf16[336,128]{1,0:T(8,128)(2,1)S(1)}, bf16[336,128]{1,0:T(8,128)(2,1)S(1)}, u32[]{:S(2)}, u32[]{:S(2)}) collective-permute-start(bf16[336,128]{1,0:T(8,128)(2,1)S(1)} %get-tuple-element.19), channel_id=1, source_target_pairs={{0,4},{4,0},{8,12},{12,8},{1,5},{5,1},{9,13},{13,9},{2,6},{6,2},{1... | collective-permute-start | bytes 258056 | tf_op jit(solution)/shard_map/ppermute | solution.py:20
  9.2 0.7 %collective-permute-done.refs_0_ = bf16[336,128]{1,0:T(8,128)(2,1)S(1)} collective-permute-done((bf16[336,128]{1,0:T(8,128)(2,1)S(1)}, bf16[336,128]{1,0:T(8,128)(2,1)S(1)}, u32[]{:S(2)}, u32[]{:S(2)}) %collective-permute-start) | collective-permute-done | bytes 86048 | tf_op jit(solution)/shard_map/ppermute | solution.py:20
  9.8 0.8 %collective-permute-start.5 = (bf16[336,128]{1,0:T(8,128)(2,1)S(1)}, bf16[336,128]{1,0:T(8,128)(2,1)S(1)}, u32[]{:S(2)}, u32[]{:S(2)}) collective-permute-start(bf16[336,128]{1,0:T(8,128)(2,1)S(1)} %collective-permute-done.refs_0_), channel_id=1, source_target_pairs={{0,4},{4,0},{8,12},{12,8},{1,5},{5,1},{9,13},{13,9},{2,6},{6,2},{1... | collective-permute-start | bytes 258056 | tf_op jit(solution)/shard_map/ppermute | solution.py:20
  10.6 1.6 %stage.1 = (bf16[384,640]{1,0:T(8,128)(2,1)S(1)}, bf16[384,640]{1,0:T(8,128)(2,1)S(1)}) custom-call(s32[1]{0:T(128)} %bitcast.1.me, bf16[512,640]{1,0:T(8,128)(2,1)} %k_ref.1, bf16[512,640]{1,0:T(8,128)(2,1)} %v_ref.1, bf16[336,128]{1,0:T(8,128)(2,1)S(1)} %collective-permute-done.refs_0_), custom_call_target="tpu_custom_call" | custom-call | tf_op jit(solution)/shard_map/stage/pallas_call | solution.py:265
  12.2 0.5 %collective-permute-done.1.refs_2_ = bf16[336,128]{1,0:T(8,128)(2,1)S(1)} collective-permute-done((bf16[336,128]{1,0:T(8,128)(2,1)S(1)}, bf16[336,128]{1,0:T(8,128)(2,1)S(1)}, u32[]{:S(2)}, u32[]{:S(2)}) %collective-permute-start.1) | collective-permute-done | bytes 86048 | tf_op jit(solution)/shard_map/ppermute | solution.py:20
  12.7 0.0 collective-permute-done.2.refs_3_
  12.7 0.0 collective-permute-done.3.refs_4_
  12.7 0.0 collective-permute-done.4.refs_6_
  12.7 0.5 %score.1 = (bf16[128,640]{1,0:T(8,128)(2,1)S(1)}, bf16[256,640]{1,0:T(8,128)(2,1)S(1)}, f32[5,128,384]{2,1,0:T(8,128)S(1)}) custom-call(bf16[384,640]{1,0:T(8,128)(2,1)S(1)} %get-tuple-element.20.refs_0_, bf16[384,640]{1,0:T(8,128)(2,1)S(1)} %get-tuple-element.21.refs_1_, bf16[336,128]{1,0:T(8,128)(2,1)S(1)} %collective-permute-done.1.refs_2_, ...), custom_call_target="tpu_custom_call" | custom-call | tf_op jit(solution)/shard_map/score/pallas_call | solution.py:278
  13.2 1.1 %collective-permute-done.5.refs_5_ = bf16[336,128]{1,0:T(8,128)(2,1)S(1)} collective-permute-done((bf16[336,128]{1,0:T(8,128)(2,1)S(1)}, bf16[336,128]{1,0:T(8,128)(2,1)S(1)}, u32[]{:S(2)}, u32[]{:S(2)}) %collective-permute-start.5) | collective-permute-done | bytes 86048 | tf_op jit(solution)/shard_map/ppermute | solution.py:20
  14.3 0.7 %finish.1 = (bf16[32,640]{1,0:T(8,128)(2,1)S(1)}, bf16[32,640]{1,0:T(8,128)(2,1)S(1)}, bf16[32,640]{1,0:T(8,128)(2,1)S(1)}, bf16[32,640]{1,0:T(8,128)(2,1)S(1)}) custom-call(bf16[384,640]{1,0:T(8,128)(2,1)S(1)} %get-tuple-element.20.refs_0_, bf16[384,640]{1,0:T(8,128)(2,1)S(1)} %get-tuple-element.21.refs_1_, bf16[128,640]{1,0:T(8,128)(2,1)S(1)} %get-tuple-element.26.refs_2_, ...), custom_call_target="tpu_custom_call" | custom-call | tf_op jit(solution)/shard_map/finish/pallas_call | solution.py:287
  15.0 1.7 %collective-permute-start.6 = (bf16[32,640]{1,0:T(8,128)(2,1)S(1)}, bf16[32,640]{1,0:T(8,128)(2,1)S(1)}, u32[]{:S(2)}, u32[]{:S(2)}) collective-permute-start(bf16[32,640]{1,0:T(8,128)(2,1)S(1)} %get-tuple-element.29), channel_id=1, source_target_pairs={{0,2},{1,3},{2,0},{3,1},{4,6},{5,7},{6,4},{7,5},{8,10},{9,11},{10,... | collective-permute-start | bytes 122888 | tf_op jit(solution)/shard_map/ppermute | solution.py:20
  16.7 0.0 collective-permute-start.7
  16.7 0.5 %collective-permute-start.8 = (bf16[32,640]{1,0:T(8,128)(2,1)S(1)}, bf16[32,640]{1,0:T(8,128)(2,1)S(1)}, u32[]{:S(2)}, u32[]{:S(2)}) collective-permute-start(bf16[32,640]{1,0:T(8,128)(2,1)S(1)} %get-tuple-element.32), channel_id=1, source_target_pairs={{0,1},{1,0},{2,3},{3,2},{4,5},{5,4},{6,7},{7,6},{8,9},{9,8},{10,11... | collective-permute-start | bytes 122888 | tf_op jit(solution)/shard_map/ppermute | solution.py:20
  17.3 1.9 %collective-permute-done.6.refs_0_ = bf16[32,640]{1,0:T(8,128)(2,1)S(1)} collective-permute-done((bf16[32,640]{1,0:T(8,128)(2,1)S(1)}, bf16[32,640]{1,0:T(8,128)(2,1)S(1)}, u32[]{:S(2)}, u32[]{:S(2)}) %collective-permute-start.6) | collective-permute-done | bytes 40992 | tf_op jit(solution)/shard_map/ppermute | solution.py:20
  19.1 1.1 %collective-permute-done.7.refs_1_ = bf16[32,640]{1,0:T(8,128)(2,1)S(1)} collective-permute-done((bf16[32,640]{1,0:T(8,128)(2,1)S(1)}, bf16[32,640]{1,0:T(8,128)(2,1)S(1)}, u32[]{:S(2)}, u32[]{:S(2)}) %collective-permute-start.7) | collective-permute-done | bytes 40992 | tf_op jit(solution)/shard_map/ppermute | solution.py:20
  20.2 0.0 collective-permute-done.8.refs_3_
  20.2 0.7 %join.1 = bf16[32,2560]{1,0:T(8,128)(2,1)} custom-call(s32[1]{0:T(128)} %bitcast.me, bf16[32,640]{1,0:T(8,128)(2,1)S(1)} %collective-permute-done.6.refs_0_, bf16[32,640]{1,0:T(8,128)(2,1)S(1)} %collective-permute-done.7.refs_1_, bf16[32,640]{1,0:T(8,128)(2,1)S(1)} %get-tuple-element.31.refs_2_, bf16[32,640]{1,0:T(8,128)(2,1)S(1)} %collective-permute-done.8.refs_3_), custom_call_target="tpu_custom_call" | custom-call | tf_op jit(solution)/shard_map/join/pallas_call | solution.py:297
Async XLA Ops:
  1.3 8.5 %collective-permute-start = (bf16[336,128]{1,0:T(8,128)(2,1)S(1)}, bf16[336,128]{1,0:T(8,128)(2,1)S(1)}, u32[]{:S(2)}, u32[]{:S(2)}) collective-permute-start(bf16[336,128]{1,0:T(8,128)(2,1)S(1)} %get-tuple-element.19), channel_id=1, source_target_pairs={{0,8},{4,12},{8,0},{12,4},{1,9},{5,13},{9,1},{13,5},{2,10},{6,14},... | collective-permute-start | bytes 258056 | tf_op jit(solution)/shard_map/ppermute | solution.py:20
  5.5 7.2 %collective-permute-start.2 = (bf16[96,640]{1,0:T(8,128)(2,1)S(1)}, bf16[96,640]{1,0:T(8,128)(2,1)S(1)}, u32[]{:S(2)}, u32[]{:S(2)}) collective-permute-start(bf16[96,640]{1,0:T(8,128)(2,1)S(1)} %get-tuple-element.22), channel_id=1, source_target_pairs={{0,2},{1,3},{2,0},{3,1},{4,6},{5,7},{6,4},{7,5},{8,10},{9,11},{10,... | collective-permute-start | bytes 368648 | tf_op jit(solution)/shard_map/ppermute | solution.py:20
  6.9 5.7 %collective-permute-start.3 = (bf16[96,640]{1,0:T(8,128)(2,1)S(1)}, bf16[96,640]{1,0:T(8,128)(2,1)S(1)}, u32[]{:S(2)}, u32[]{:S(2)}) collective-permute-start(bf16[96,640]{1,0:T(8,128)(2,1)S(1)} %get-tuple-element.23), channel_id=1, source_target_pairs={{0,3},{1,2},{2,1},{3,0},{4,7},{5,6},{6,5},{7,4},{8,11},{9,10},{10,... | collective-permute-start | bytes 368648 | tf_op jit(solution)/shard_map/ppermute | solution.py:20
  6.9 5.7 %collective-permute-start.4 = (bf16[96,640]{1,0:T(8,128)(2,1)S(1)}, bf16[96,640]{1,0:T(8,128)(2,1)S(1)}, u32[]{:S(2)}, u32[]{:S(2)}) collective-permute-start(bf16[96,640]{1,0:T(8,128)(2,1)S(1)} %get-tuple-element.25), channel_id=1, source_target_pairs={{0,1},{1,0},{2,3},{3,2},{4,5},{5,4},{6,7},{7,6},{8,9},{9,8},{10,11... | collective-permute-start | bytes 368648 | tf_op jit(solution)/shard_map/ppermute | solution.py:20
  7.6 5.1 %collective-permute-start.1 = (bf16[336,128]{1,0:T(8,128)(2,1)S(1)}, bf16[336,128]{1,0:T(8,128)(2,1)S(1)}, u32[]{:S(2)}, u32[]{:S(2)}) collective-permute-start(bf16[336,128]{1,0:T(8,128)(2,1)S(1)} %get-tuple-element.19), channel_id=1, source_target_pairs={{0,4},{4,0},{8,12},{12,8},{1,5},{5,1},{9,13},{13,9},{2,6},{6,2},{1... | collective-permute-start | bytes 258056 | tf_op jit(solution)/shard_map/ppermute | solution.py:20
  9.8 4.5 %collective-permute-start.5 = (bf16[336,128]{1,0:T(8,128)(2,1)S(1)}, bf16[336,128]{1,0:T(8,128)(2,1)S(1)}, u32[]{:S(2)}, u32[]{:S(2)}) collective-permute-start(bf16[336,128]{1,0:T(8,128)(2,1)S(1)} %collective-permute-done.refs_0_), channel_id=1, source_target_pairs={{0,4},{4,0},{8,12},{12,8},{1,5},{5,1},{9,13},{13,9},{2,6},{6,2},{1... | collective-permute-start | bytes 258056 | tf_op jit(solution)/shard_map/ppermute | solution.py:20
  15.0 4.1 %collective-permute-start.6 = (bf16[32,640]{1,0:T(8,128)(2,1)S(1)}, bf16[32,640]{1,0:T(8,128)(2,1)S(1)}, u32[]{:S(2)}, u32[]{:S(2)}) collective-permute-start(bf16[32,640]{1,0:T(8,128)(2,1)S(1)} %get-tuple-element.29), channel_id=1, source_target_pairs={{0,2},{1,3},{2,0},{3,1},{4,6},{5,7},{6,4},{7,5},{8,10},{9,11},{10,... | collective-permute-start | bytes 122888 | tf_op jit(solution)/shard_map/ppermute | solution.py:20
  16.7 3.4 %collective-permute-start.7 = (bf16[32,640]{1,0:T(8,128)(2,1)S(1)}, bf16[32,640]{1,0:T(8,128)(2,1)S(1)}, u32[]{:S(2)}, u32[]{:S(2)}) collective-permute-start(bf16[32,640]{1,0:T(8,128)(2,1)S(1)} %get-tuple-element.30), channel_id=1, source_target_pairs={{0,3},{1,2},{2,1},{3,0},{4,7},{5,6},{6,5},{7,4},{8,11},{9,10},{10,... | collective-permute-start | bytes 122888 | tf_op jit(solution)/shard_map/ppermute | solution.py:20
  16.7 3.4 %collective-permute-start.8 = (bf16[32,640]{1,0:T(8,128)(2,1)S(1)}, bf16[32,640]{1,0:T(8,128)(2,1)S(1)}, u32[]{:S(2)}, u32[]{:S(2)}) collective-permute-start(bf16[32,640]{1,0:T(8,128)(2,1)S(1)} %get-tuple-element.32), channel_id=1, source_target_pairs={{0,1},{1,0},{2,3},{3,2},{4,5},{5,4},{6,7},{7,6},{8,9},{9,8},{10,11... | collective-permute-start | bytes 122888 | tf_op jit(solution)/shard_map/ppermute | solution.py:20

commit v4 on v3

--- a/solution.py
+++ b/solution.py
@@ -20,12 +20,16 @@
     return lax.ppermute(array, axis, [(i, i ^ step) for i in range(count)])
 
 
-def order_of(count):
+def tokens_in(count):
     return [*range(2, count), *range(min(2, count))]
 
 
-def in_turn(refs):
-    turned = dict(zip(order_of(len(refs)), refs, strict=True))
+def tokens_out(count):
+    return list(reversed(range(count)))
+
+
+def in_turn(refs, order):
+    turned = dict(zip(order(len(refs)), refs, strict=True))
     return [turned[step] for step in range(len(refs))]
 
 
@@ -134,7 +138,7 @@
 
 
 def score_kernel(count, n_now, ahead, block_len, fresh, size, *refs):
-    (k_st, v_st), now, parts = refs[:2], refs[2 : 2 + n_now], in_turn(refs[2 + n_now : 2 + n_now + count])
+    (k_st, v_st), now, parts = refs[:2], refs[2 : 2 + n_now], in_turn(refs[2 + n_now : 2 + n_now + count], tokens_in)
     q_all, v_own, scores, k_own = refs[2 + n_now + count :]
     rows = parts[0].shape[0] // 3
     tok = rows * count
@@ -197,7 +201,7 @@
 
 
 def join_kernel(count, me, *refs):
-    parts, out = in_turn(refs[:count]), refs[count]
+    parts, out = in_turn(refs[:count], tokens_out), refs[count]
     width = parts[0].shape[1]
     for step in range(count):
         out[:, pl.ds(pl.multiple_of((me[0] ^ step) * width, 128), width)] = parts[step][...]
@@ -256,7 +260,6 @@
     else:
         residuals = [lax.all_gather(both, "patch", axis=0)]
         steps, late = range(1, patch_n), []
-    order = order_of(head_n)
     parts = [trade(parts[step], "head", step, head_n) if step else parts[0] for step in range(head_n)]
     now = late
     late = [trade(far, "patch", 1, patch_n)] if four else []
@@ -283,7 +286,7 @@
         scratch_shapes=[pltpu.VMEM((own, width), bf16)],
         compiler_params=larger,
         name="score",
-    )(stale_k, stale_v, *now, *[parts[step] for step in order])
+    )(stale_k, stale_v, *now, *[parts[step] for step in tokens_in(head_n)])
     outs = pl.pallas_call(
         functools.partial(finish_kernel, head_n, len(late), ahead, block_len, fresh, size),
         out_shape=[shape(rows, width)] * head_n,
@@ -301,7 +304,7 @@
         out_specs=VM,
         compiler_params=grant,
         name="join",
-    )(my_head, *[outs[step] for step in order])
+    )(my_head, *[outs[step] for step in tokens_out(head_n)])
 
 
 def solution(mesh):

time: 21 us -> 20.3 us (0.967)
  waiting for transfers between devices: 5.2 us -> 4.71 us
  starting transfers between devices: 10.8 us -> 10.5 us
    ppermute x9, waiting for transfers between devices: 5.2 us -> 4.71 us  [trade(): return lax.ppermute(array, axis, [(i, i ^ step) for i in range(count)])]
    ppermute x9, starting transfers between devices: 10.8 us -> 10.5 us  [trade(): return lax.ppermute(array, axis, [(i, i ^ step) for i in range(count)])]
where the time goes in v4:
time: 20.3 us; the launch traced here: 20.1 us
  starting transfers between devices  10.5 us (52%)
  Pallas kernels  4.83 us (24%)
  waiting for transfers between devices  4.71 us (23%)
    ppermute x9, starting transfers between devices, trade(): return lax.ppermute(array, axis, [(i, i ^ step) for i in range(count)])  10.5 us
    ppermute x9, waiting for transfers between devices, trade(): return lax.ppermute(array, axis, [(i, i ^ step) for i in range(count)])  4.71 us
    pallas_call x1, Pallas kernels, local(): pl.pallas_call(functools.partial(stage_kernel, steps, 1 if four else 0, t...  1.56 us
    pallas_call x1, Pallas kernels, local(): pl.pallas_call(functools.partial(prepare_kernel, head_n, len(inputs)), ou...  1.34 us
    pallas_call x1, Pallas kernels, local(): pl.pallas_call(functools.partial(finish_kernel, head_n, len(late), ahead,...  0.73 us
    pallas_call x1, Pallas kernels, local(): pl.pallas_call(functools.partial(join_kernel, head_n), out_shape=shape(ro...  0.68 us
    pallas_call x1, Pallas kernels, local(): pl.pallas_call(functools.partial(score_kernel, head_n, len(now), ahead, b...  0.51 us
  transfers between devices with their start and end apart: 9, of which 5 were waited for; matrix products, arithmetic and copies ran while one was open for 0% of the time, Pallas kernels for 10%

profile of v4, /device:TPU:0, one launch (start us, length us, event | category | flops | bytes accessed | tf_op | source)
XLA Modules:
  0.0 20.1 jit_solution(18011330844605692870)
XLA Ops:
  0.0 1.3 %prepare.1 = (bf16[336,128]{1,0:T(8,128)(2,1)S(1)}, bf16[96,640]{1,0:T(8,128)(2,1)S(1)}, bf16[96,640]{1,0:T(8,128)(2,1)S(1)}, bf16[96,640]{1,0:T(8,128)(2,1)S(1)}, bf16[96,640]{1,0:T(8,128)(2,1)S(1)}) custom-call(s32[1]{0:T(128)} %bitcast.me, s32[2]{0:T(128)} %refs_0_.1, s32[2,5]{1,0:T(2,128)} %refs_1_.1, bf16[2,16,640]{2,1,0:T(8,128)(2,1)} %refs_2_.1, ...), custom_call_target="tpu_custom_call" | custom-call | tf_op jit(solution)/shard_map/prepare/pallas_call | solution.py:243
  1.3 4.1 %collective-permute-start = (bf16[336,128]{1,0:T(8,128)(2,1)S(1)}, bf16[336,128]{1,0:T(8,128)(2,1)S(1)}, u32[]{:S(2)}, u32[]{:S(2)}) collective-permute-start(bf16[336,128]{1,0:T(8,128)(2,1)S(1)} %get-tuple-element.19), channel_id=1, source_target_pairs={{0,8},{4,12},{8,0},{12,4},{1,9},{5,13},{9,1},{13,5},{2,10},{6,14},... | collective-permute-start | bytes 258056 | tf_op jit(solution)/shard_map/ppermute | solution.py:20
  5.5 1.5 %collective-permute-start.2 = (bf16[96,640]{1,0:T(8,128)(2,1)S(1)}, bf16[96,640]{1,0:T(8,128)(2,1)S(1)}, u32[]{:S(2)}, u32[]{:S(2)}) collective-permute-start(bf16[96,640]{1,0:T(8,128)(2,1)S(1)} %get-tuple-element.22), channel_id=1, source_target_pairs={{0,2},{1,3},{2,0},{3,1},{4,6},{5,7},{6,4},{7,5},{8,10},{9,11},{10,... | collective-permute-start | bytes 368648 | tf_op jit(solution)/shard_map/ppermute | solution.py:20
  6.9 0.0 collective-permute-start.3
  6.9 0.6 %collective-permute-start.4 = (bf16[96,640]{1,0:T(8,128)(2,1)S(1)}, bf16[96,640]{1,0:T(8,128)(2,1)S(1)}, u32[]{:S(2)}, u32[]{:S(2)}) collective-permute-start(bf16[96,640]{1,0:T(8,128)(2,1)S(1)} %get-tuple-element.25), channel_id=1, source_target_pairs={{0,1},{1,0},{2,3},{3,2},{4,5},{5,4},{6,7},{7,6},{8,9},{9,8},{10,11... | collective-permute-start | bytes 368648 | tf_op jit(solution)/shard_map/ppermute | solution.py:20
  7.6 1.6 %collective-permute-start.1 = (bf16[336,128]{1,0:T(8,128)(2,1)S(1)}, bf16[336,128]{1,0:T(8,128)(2,1)S(1)}, u32[]{:S(2)}, u32[]{:S(2)}) collective-permute-start(bf16[336,128]{1,0:T(8,128)(2,1)S(1)} %get-tuple-element.19), channel_id=1, source_target_pairs={{0,4},{4,0},{8,12},{12,8},{1,5},{5,1},{9,13},{13,9},{2,6},{6,2},{1... | collective-permute-start | bytes 258056 | tf_op jit(solution)/shard_map/ppermute | solution.py:20
  9.2 0.7 %collective-permute-done.refs_0_ = bf16[336,128]{1,0:T(8,128)(2,1)S(1)} collective-permute-done((bf16[336,128]{1,0:T(8,128)(2,1)S(1)}, bf16[336,128]{1,0:T(8,128)(2,1)S(1)}, u32[]{:S(2)}, u32[]{:S(2)}) %collective-permute-start) | collective-permute-done | bytes 86048 | tf_op jit(solution)/shard_map/ppermute | solution.py:20
  9.8 0.8 %collective-permute-start.5 = (bf16[336,128]{1,0:T(8,128)(2,1)S(1)}, bf16[336,128]{1,0:T(8,128)(2,1)S(1)}, u32[]{:S(2)}, u32[]{:S(2)}) collective-permute-start(bf16[336,128]{1,0:T(8,128)(2,1)S(1)} %collective-permute-done.refs_0_), channel_id=1, source_target_pairs={{0,4},{4,0},{8,12},{12,8},{1,5},{5,1},{9,13},{13,9},{2,6},{6,2},{1... | collective-permute-start | bytes 258056 | tf_op jit(solution)/shard_map/ppermute | solution.py:20
  10.6 1.6 %stage.1 = (bf16[384,640]{1,0:T(8,128)(2,1)S(1)}, bf16[384,640]{1,0:T(8,128)(2,1)S(1)}) custom-call(s32[1]{0:T(128)} %bitcast.1.me, bf16[512,640]{1,0:T(8,128)(2,1)} %k_ref.1, bf16[512,640]{1,0:T(8,128)(2,1)} %v_ref.1, bf16[336,128]{1,0:T(8,128)(2,1)S(1)} %collective-permute-done.refs_0_), custom_call_target="tpu_custom_call" | custom-call | tf_op jit(solution)/shard_map/stage/pallas_call | solution.py:268
  12.2 0.5 %collective-permute-done.1.refs_2_ = bf16[336,128]{1,0:T(8,128)(2,1)S(1)} collective-permute-done((bf16[336,128]{1,0:T(8,128)(2,1)S(1)}, bf16[336,128]{1,0:T(8,128)(2,1)S(1)}, u32[]{:S(2)}, u32[]{:S(2)}) %collective-permute-start.1) | collective-permute-done | bytes 86048 | tf_op jit(solution)/shard_map/ppermute | solution.py:20
  12.7 0.0 collective-permute-done.2.refs_3_
  12.7 0.0 collective-permute-done.3.refs_4_
  12.7 0.0 collective-permute-done.4.refs_6_
  12.7 0.5 %score.1 = (bf16[128,640]{1,0:T(8,128)(2,1)S(1)}, bf16[256,640]{1,0:T(8,128)(2,1)S(1)}, f32[5,128,384]{2,1,0:T(8,128)S(1)}) custom-call(bf16[384,640]{1,0:T(8,128)(2,1)S(1)} %get-tuple-element.20.refs_0_, bf16[384,640]{1,0:T(8,128)(2,1)S(1)} %get-tuple-element.21.refs_1_, bf16[336,128]{1,0:T(8,128)(2,1)S(1)} %collective-permute-done.1.refs_2_, ...), custom_call_target="tpu_custom_call" | custom-call | tf_op jit(solution)/shard_map/score/pallas_call | solution.py:281
  13.2 1.1 %collective-permute-done.5.refs_5_ = bf16[336,128]{1,0:T(8,128)(2,1)S(1)} collective-permute-done((bf16[336,128]{1,0:T(8,128)(2,1)S(1)}, bf16[336,128]{1,0:T(8,128)(2,1)S(1)}, u32[]{:S(2)}, u32[]{:S(2)}) %collective-permute-start.5) | collective-permute-done | bytes 86048 | tf_op jit(solution)/shard_map/ppermute | solution.py:20
  14.3 0.7 %finish.1 = (bf16[32,640]{1,0:T(8,128)(2,1)S(1)}, bf16[32,640]{1,0:T(8,128)(2,1)S(1)}, bf16[32,640]{1,0:T(8,128)(2,1)S(1)}, bf16[32,640]{1,0:T(8,128)(2,1)S(1)}) custom-call(bf16[384,640]{1,0:T(8,128)(2,1)S(1)} %get-tuple-element.20.refs_0_, bf16[384,640]{1,0:T(8,128)(2,1)S(1)} %get-tuple-element.21.refs_1_, bf16[128,640]{1,0:T(8,128)(2,1)S(1)} %get-tuple-element.26.refs_2_, ...), custom_call_target="tpu_custom_call" | custom-call | tf_op jit(solution)/shard_map/finish/pallas_call | solution.py:290
  15.0 0.2 collective-permute-start.6
  15.2 1.6 %collective-permute-start.7 = (bf16[32,640]{1,0:T(8,128)(2,1)S(1)}, bf16[32,640]{1,0:T(8,128)(2,1)S(1)}, u32[]{:S(2)}, u32[]{:S(2)}) collective-permute-start(bf16[32,640]{1,0:T(8,128)(2,1)S(1)} %get-tuple-element.30), channel_id=1, source_target_pairs={{0,2},{1,3},{2,0},{3,1},{4,6},{5,7},{6,4},{7,5},{8,10},{9,11},{10,... | collective-permute-start | bytes 122888 | tf_op jit(solution)/shard_map/ppermute | solution.py:20
  16.8 0.2 collective-permute-start.8
  17.0 1.8 %collective-permute-done.6.refs_0_ = bf16[32,640]{1,0:T(8,128)(2,1)S(1)} collective-permute-done((bf16[32,640]{1,0:T(8,128)(2,1)S(1)}, bf16[32,640]{1,0:T(8,128)(2,1)S(1)}, u32[]{:S(2)}, u32[]{:S(2)}) %collective-permute-start.6) | collective-permute-done | bytes 40992 | tf_op jit(solution)/shard_map/ppermute | solution.py:20
  18.8 0.6 %collective-permute-done.7.refs_1_ = bf16[32,640]{1,0:T(8,128)(2,1)S(1)} collective-permute-done((bf16[32,640]{1,0:T(8,128)(2,1)S(1)}, bf16[32,640]{1,0:T(8,128)(2,1)S(1)}, u32[]{:S(2)}, u32[]{:S(2)}) %collective-permute-start.7) | collective-permute-done | bytes 40992 | tf_op jit(solution)/shard_map/ppermute | solution.py:20
  19.4 0.0 collective-permute-done.8.refs_2_
  19.4 0.7 %join.1 = bf16[32,2560]{1,0:T(8,128)(2,1)} custom-call(s32[1]{0:T(128)} %bitcast.me, bf16[32,640]{1,0:T(8,128)(2,1)S(1)} %collective-permute-done.6.refs_0_, bf16[32,640]{1,0:T(8,128)(2,1)S(1)} %collective-permute-done.7.refs_1_, bf16[32,640]{1,0:T(8,128)(2,1)S(1)} %collective-permute-done.8.refs_2_, bf16[32,640]{1,0:T(8,128)(2,1)S(1)} %get-tuple-element.32.refs_3_), custom_call_target="tpu_custom_call" | custom-call | tf_op jit(solution)/shard_map/join/pallas_call | solution.py:300
Async XLA Ops:
  1.3 8.5 %collective-permute-start = (bf16[336,128]{1,0:T(8,128)(2,1)S(1)}, bf16[336,128]{1,0:T(8,128)(2,1)S(1)}, u32[]{:S(2)}, u32[]{:S(2)}) collective-permute-start(bf16[336,128]{1,0:T(8,128)(2,1)S(1)} %get-tuple-element.19), channel_id=1, source_target_pairs={{0,8},{4,12},{8,0},{12,4},{1,9},{5,13},{9,1},{13,5},{2,10},{6,14},... | collective-permute-start | bytes 258056 | tf_op jit(solution)/shard_map/ppermute | solution.py:20
  5.5 7.2 %collective-permute-start.2 = (bf16[96,640]{1,0:T(8,128)(2,1)S(1)}, bf16[96,640]{1,0:T(8,128)(2,1)S(1)}, u32[]{:S(2)}, u32[]{:S(2)}) collective-permute-start(bf16[96,640]{1,0:T(8,128)(2,1)S(1)} %get-tuple-element.22), channel_id=1, source_target_pairs={{0,2},{1,3},{2,0},{3,1},{4,6},{5,7},{6,4},{7,5},{8,10},{9,11},{10,... | collective-permute-start | bytes 368648 | tf_op jit(solution)/shard_map/ppermute | solution.py:20
  6.9 5.7 %collective-permute-start.3 = (bf16[96,640]{1,0:T(8,128)(2,1)S(1)}, bf16[96,640]{1,0:T(8,128)(2,1)S(1)}, u32[]{:S(2)}, u32[]{:S(2)}) collective-permute-start(bf16[96,640]{1,0:T(8,128)(2,1)S(1)} %get-tuple-element.23), channel_id=1, source_target_pairs={{0,3},{1,2},{2,1},{3,0},{4,7},{5,6},{6,5},{7,4},{8,11},{9,10},{10,... | collective-permute-start | bytes 368648 | tf_op jit(solution)/shard_map/ppermute | solution.py:20
  6.9 5.7 %collective-permute-start.4 = (bf16[96,640]{1,0:T(8,128)(2,1)S(1)}, bf16[96,640]{1,0:T(8,128)(2,1)S(1)}, u32[]{:S(2)}, u32[]{:S(2)}) collective-permute-start(bf16[96,640]{1,0:T(8,128)(2,1)S(1)} %get-tuple-element.25), channel_id=1, source_target_pairs={{0,1},{1,0},{2,3},{3,2},{4,5},{5,4},{6,7},{7,6},{8,9},{9,8},{10,11... | collective-permute-start | bytes 368648 | tf_op jit(solution)/shard_map/ppermute | solution.py:20
  7.6 5.1 %collective-permute-start.1 = (bf16[336,128]{1,0:T(8,128)(2,1)S(1)}, bf16[336,128]{1,0:T(8,128)(2,1)S(1)}, u32[]{:S(2)}, u32[]{:S(2)}) collective-permute-start(bf16[336,128]{1,0:T(8,128)(2,1)S(1)} %get-tuple-element.19), channel_id=1, source_target_pairs={{0,4},{4,0},{8,12},{12,8},{1,5},{5,1},{9,13},{13,9},{2,6},{6,2},{1... | collective-permute-start | bytes 258056 | tf_op jit(solution)/shard_map/ppermute | solution.py:20
  9.8 4.5 %collective-permute-start.5 = (bf16[336,128]{1,0:T(8,128)(2,1)S(1)}, bf16[336,128]{1,0:T(8,128)(2,1)S(1)}, u32[]{:S(2)}, u32[]{:S(2)}) collective-permute-start(bf16[336,128]{1,0:T(8,128)(2,1)S(1)} %collective-permute-done.refs_0_), channel_id=1, source_target_pairs={{0,4},{4,0},{8,12},{12,8},{1,5},{5,1},{9,13},{13,9},{2,6},{6,2},{1... | collective-permute-start | bytes 258056 | tf_op jit(solution)/shard_map/ppermute | solution.py:20
  15.0 3.7 %collective-permute-start.6 = (bf16[32,640]{1,0:T(8,128)(2,1)S(1)}, bf16[32,640]{1,0:T(8,128)(2,1)S(1)}, u32[]{:S(2)}, u32[]{:S(2)}) collective-permute-start(bf16[32,640]{1,0:T(8,128)(2,1)S(1)} %get-tuple-element.29), channel_id=1, source_target_pairs={{0,3},{1,2},{2,1},{3,0},{4,7},{5,6},{6,5},{7,4},{8,11},{9,10},{10,... | collective-permute-start | bytes 122888 | tf_op jit(solution)/shard_map/ppermute | solution.py:20
  15.2 4.2 %collective-permute-start.7 = (bf16[32,640]{1,0:T(8,128)(2,1)S(1)}, bf16[32,640]{1,0:T(8,128)(2,1)S(1)}, u32[]{:S(2)}, u32[]{:S(2)}) collective-permute-start(bf16[32,640]{1,0:T(8,128)(2,1)S(1)} %get-tuple-element.30), channel_id=1, source_target_pairs={{0,2},{1,3},{2,0},{3,1},{4,6},{5,7},{6,4},{7,5},{8,10},{9,11},{10,... | collective-permute-start | bytes 122888 | tf_op jit(solution)/shard_map/ppermute | solution.py:20
  16.8 2.6 %collective-permute-start.8 = (bf16[32,640]{1,0:T(8,128)(2,1)S(1)}, bf16[32,640]{1,0:T(8,128)(2,1)S(1)}, u32[]{:S(2)}, u32[]{:S(2)}) collective-permute-start(bf16[32,640]{1,0:T(8,128)(2,1)S(1)} %get-tuple-element.31), channel_id=1, source_target_pairs={{0,1},{1,0},{2,3},{3,2},{4,5},{5,4},{6,7},{7,6},{8,9},{9,8},{10,11... | collective-permute-start | bytes 122888 | tf_op jit(solution)/shard_map/ppermute | solution.py:20

commit v5 on v4

--- a/solution.py
+++ b/solution.py
@@ -43,7 +43,18 @@
 def prepare_kernel(count, n_in, me, *refs):
     inputs, both, outs = refs[:n_in], refs[n_in], refs[n_in + 1 : n_in + 1 + count]
     held, sems = refs[n_in + 1 + count : -1], refs[-1]
-    copies = start_all(zip(inputs, held, strict=True), sems)
+    copies = []
+    for at, (source, target) in enumerate(zip(inputs, held, strict=True)):
+        whole = pltpu.make_async_copy(source, target, sems.at[at])
+        copies.append(whole)
+        if at < 4 or len(source.shape) == 1 or source.shape[0] % 32:
+            whole.start()
+            continue
+        high, wide = source.shape[0] // 2, source.shape[1] // 2
+        for top in (0, high):
+            for left in (0, wide):
+                where = (pl.ds(top, high), pl.ds(left, wide))
+                pltpu.make_async_copy(source.at[where], target.at[where], sems.at[at]).start()
     ids, exps, res_k, res_v, q_ref, qg_ref, k_ref, kg_ref, v_ref = held
 
     sent, block_len = res_k.shape[:2]
@@ -158,26 +169,28 @@
         scores[h, :, pl.ds(ahead, k_own.shape[0])] = scored(q_all[:, lanes], k_own[:, lanes])
 
 
-def finish_kernel(count, n_late, ahead, block_len, fresh, size, *refs):
+def finish_kernel(steps, n_late, n_given, rows, ahead, block_len, fresh, size, *refs):
     (k_st, v_st, q_all, v_own, scores), late = refs[:5], refs[5 : 5 + n_late]
-    outs, (k_new, v_new) = refs[5 + n_late : -2], refs[-2:]
+    given = refs[5 + n_late : 5 + n_late + n_given]
+    outs = refs[5 + n_late + n_given :]
     tok = q_all.shape[0]
-    rows = tok // count
     heads = q_all.shape[1] // size
+    k_new, v_new = given or outs[len(steps) :] or (None, None)
     for packed in late:
         chosen = chooser(tok, fresh, block_len, packed, heads * fresh)
         source, target = pl.ds(k_st.shape[0] - tok, tok), pl.ds(0, tok)
         refresh(chosen, k_st, source, k_new, target, packed, 0)
         refresh(chosen, v_st, source, v_new, target, packed, heads * fresh + tail)
+    span = pl.ds(steps[0] * rows, len(steps) * rows)
     columns = [pl.ds(h * size, size) for h in range(heads)]
-    together = heads if late else 1
+    together = heads if k_new is not None else 1
     for first in range(0, heads, together):
         group = range(first, first + together)
-        cut = {h: [scores[h, :, pl.ds(0, ahead)], scores[h, :, pl.ds(ahead, v_own.shape[0])]] for h in group}
+        cut = {h: [scores[h, span, pl.ds(0, ahead)], scores[h, span, pl.ds(ahead, v_own.shape[0])]] for h in group}
         held = {h: [v_st[pl.ds(0, ahead), columns[h]], v_own[:, columns[h]]] for h in group}
-        if late:
+        if k_new is not None:
             for h in group:
-                cut[h].append(scored(q_all[:, columns[h]], k_new[:, columns[h]]))
+                cut[h].append(scored(q_all[span, columns[h]], k_new[:, columns[h]]))
                 held[h].append(v_new[:, columns[h]])
         peaks = {h: row_fold(jnp.maximum, jnp.max, cut[h]) for h in group}
         powered, summed = {}, {}
@@ -191,8 +204,8 @@
         totals = {h: row_fold(jnp.add, jnp.sum, powered[h]) for h in group}
         for h in group:
             result = (summed[h] / totals[h]).astype(jnp.bfloat16)
-            for step in range(count):
-                outs[step][:, columns[h]] = result[step * rows : (step + 1) * rows]
+            for place in range(len(steps)):
+                outs[place][:, columns[h]] = result[place * rows : (place + 1) * rows]
 
 
 def row_fold(both, along, parts):
@@ -287,15 +300,20 @@
         compiler_params=larger,
         name="score",
     )(stale_k, stale_v, *now, *[parts[step] for step in tokens_in(head_n)])
-    outs = pl.pallas_call(
-        functools.partial(finish_kernel, head_n, len(late), ahead, block_len, fresh, size),
-        out_shape=[shape(rows, width)] * head_n,
-        in_specs=[VM] * (5 + len(late)),
-        out_specs=[VM] * head_n,
-        scratch_shapes=[pltpu.VMEM((tok, width), bf16)] * 2,
-        compiler_params=larger,
-        name="finish",
-    )(stale_k, stale_v, q_all, v_own, scores, *late)
+    done, given = {}, []
+    for steps in (range(2, head_n), range(min(2, head_n))):
+        fresh_late = [] if given else late
+        finished = pl.pallas_call(
+            functools.partial(finish_kernel, steps, len(fresh_late), len(given), rows, ahead, block_len, fresh, size),
+            out_shape=[shape(rows, width)] * len(steps) + [shape(tok, width)] * (2 * len(fresh_late)),
+            in_specs=[VM] * (5 + len(fresh_late) + len(given)),
+            out_specs=[VM] * (len(steps) + 2 * len(fresh_late)),
+            compiler_params=larger,
+            name="finish",
+        )(stale_k, stale_v, q_all, v_own, scores, *fresh_late, *given)
+        done.update(zip(steps, finished))
+        given = given or finished[len(steps) :]
+    outs = [done[step] for step in range(head_n)]
     outs = [trade(outs[step], "head", step, head_n) if step else outs[0] for step in range(head_n)]
     return pl.pallas_call(
         functools.partial(join_kernel, head_n),

time: 20.3 us -> 20.1 us (level)
  waiting for transfers between devices: 4.71 us -> 4.14 us
  Pallas kernels: 4.83 us -> 5.15 us
    ppermute x9, waiting for transfers between devices: 4.71 us -> 4.14 us  [trade(): return lax.ppermute(array, axis, [(i, i ^ step) for i in range(count)])]
    pallas_call x1 -> x2, Pallas kernels: 0.73 us -> 1.13 us  [local(): pl.pallas_call(functools.partial(finish_kernel, steps, len(fresh_late), l...]
  transfers between devices with their start and end apart: 9 -> 9, of which waited for: 5 -> 5; matrix products, arithmetic and copies ran while one was open for 0% -> 0% of each run, Pallas kernels for 10% -> 13%
where the time goes in v5:
time: 20.1 us; the launch traced here: 19.9 us
  starting transfers between devices  10.6 us (53%)
  Pallas kernels  5.15 us (26%)
  waiting for transfers between devices  4.14 us (21%)
    ppermute x9, starting transfers between devices, trade(): return lax.ppermute(array, axis, [(i, i ^ step) for i in range(count)])  10.6 us
    ppermute x9, waiting for transfers between devices, trade(): return lax.ppermute(array, axis, [(i, i ^ step) for i in range(count)])  4.14 us
    pallas_call x1, Pallas kernels, local(): pl.pallas_call(functools.partial(stage_kernel, steps, 1 if four else 0, t...  1.56 us
    pallas_call x1, Pallas kernels, local(): pl.pallas_call(functools.partial(prepare_kernel, head_n, len(inputs)), ou...  1.25 us
    pallas_call x2, Pallas kernels, local(): pl.pallas_call(functools.partial(finish_kernel, steps, len(fresh_late), l...  1.13 us
    pallas_call x1, Pallas kernels, local(): pl.pallas_call(functools.partial(join_kernel, head_n), out_shape=shape(ro...  0.68 us
    pallas_call x1, Pallas kernels, local(): pl.pallas_call(functools.partial(score_kernel, head_n, len(now), ahead, b...  0.51 us
  transfers between devices with their start and end apart: 9, of which 5 were waited for; matrix products, arithmetic and copies ran while one was open for 0% of the time, Pallas kernels for 13%

profile of v5, /device:TPU:0, one launch (start us, length us, event | category | flops | bytes accessed | tf_op | source)
XLA Modules:
  0.0 19.9 jit_solution(2122761628034795755)
XLA Ops:
  0.0 1.3 %prepare.1 = (bf16[336,128]{1,0:T(8,128)(2,1)S(1)}, bf16[96,640]{1,0:T(8,128)(2,1)S(1)}, bf16[96,640]{1,0:T(8,128)(2,1)S(1)}, bf16[96,640]{1,0:T(8,128)(2,1)S(1)}, bf16[96,640]{1,0:T(8,128)(2,1)S(1)}) custom-call(s32[1]{0:T(128)} %bitcast.me, s32[2]{0:T(128)} %refs_0_.1, s32[2,5]{1,0:T(2,128)} %refs_1_.1, bf16[2,16,640]{2,1,0:T(8,128)(2,1)} %refs_2_.1, ...), custom_call_target="tpu_custom_call" | custom-call | tf_op jit(solution)/shard_map/prepare/pallas_call | solution.py:256
  1.3 4.1 %collective-permute-start = (bf16[336,128]{1,0:T(8,128)(2,1)S(1)}, bf16[336,128]{1,0:T(8,128)(2,1)S(1)}, u32[]{:S(2)}, u32[]{:S(2)}) collective-permute-start(bf16[336,128]{1,0:T(8,128)(2,1)S(1)} %get-tuple-element.21), channel_id=1, source_target_pairs={{0,8},{4,12},{8,0},{12,4},{1,9},{5,13},{9,1},{13,5},{2,10},{6,14},... | collective-permute-start | bytes 258056 | tf_op jit(solution)/shard_map/ppermute | solution.py:20
  5.4 1.5 %collective-permute-start.2 = (bf16[96,640]{1,0:T(8,128)(2,1)S(1)}, bf16[96,640]{1,0:T(8,128)(2,1)S(1)}, u32[]{:S(2)}, u32[]{:S(2)}) collective-permute-start(bf16[96,640]{1,0:T(8,128)(2,1)S(1)} %get-tuple-element.24), channel_id=1, source_target_pairs={{0,2},{1,3},{2,0},{3,1},{4,6},{5,7},{6,4},{7,5},{8,10},{9,11},{10,... | collective-permute-start | bytes 368648 | tf_op jit(solution)/shard_map/ppermute | solution.py:20
  6.9 0.0 collective-permute-start.3
  6.9 0.6 %collective-permute-start.4 = (bf16[96,640]{1,0:T(8,128)(2,1)S(1)}, bf16[96,640]{1,0:T(8,128)(2,1)S(1)}, u32[]{:S(2)}, u32[]{:S(2)}) collective-permute-start(bf16[96,640]{1,0:T(8,128)(2,1)S(1)} %get-tuple-element.27), channel_id=1, source_target_pairs={{0,1},{1,0},{2,3},{3,2},{4,5},{5,4},{6,7},{7,6},{8,9},{9,8},{10,11... | collective-permute-start | bytes 368648 | tf_op jit(solution)/shard_map/ppermute | solution.py:20
  7.5 1.6 %collective-permute-start.1 = (bf16[336,128]{1,0:T(8,128)(2,1)S(1)}, bf16[336,128]{1,0:T(8,128)(2,1)S(1)}, u32[]{:S(2)}, u32[]{:S(2)}) collective-permute-start(bf16[336,128]{1,0:T(8,128)(2,1)S(1)} %get-tuple-element.21), channel_id=1, source_target_pairs={{0,4},{4,0},{8,12},{12,8},{1,5},{5,1},{9,13},{13,9},{2,6},{6,2},{1... | collective-permute-start | bytes 258056 | tf_op jit(solution)/shard_map/ppermute | solution.py:20
  9.1 0.7 %collective-permute-done.refs_0_ = bf16[336,128]{1,0:T(8,128)(2,1)S(1)} collective-permute-done((bf16[336,128]{1,0:T(8,128)(2,1)S(1)}, bf16[336,128]{1,0:T(8,128)(2,1)S(1)}, u32[]{:S(2)}, u32[]{:S(2)}) %collective-permute-start) | collective-permute-done | bytes 86048 | tf_op jit(solution)/shard_map/ppermute | solution.py:20
  9.7 0.8 %collective-permute-start.5 = (bf16[336,128]{1,0:T(8,128)(2,1)S(1)}, bf16[336,128]{1,0:T(8,128)(2,1)S(1)}, u32[]{:S(2)}, u32[]{:S(2)}) collective-permute-start(bf16[336,128]{1,0:T(8,128)(2,1)S(1)} %collective-permute-done.refs_0_), channel_id=1, source_target_pairs={{0,4},{4,0},{8,12},{12,8},{1,5},{5,1},{9,13},{13,9},{2,6},{6,2},{1... | collective-permute-start | bytes 258056 | tf_op jit(solution)/shard_map/ppermute | solution.py:20
  10.5 1.6 %stage.1 = (bf16[384,640]{1,0:T(8,128)(2,1)S(1)}, bf16[384,640]{1,0:T(8,128)(2,1)S(1)}) custom-call(s32[1]{0:T(128)} %bitcast.1.me, bf16[512,640]{1,0:T(8,128)(2,1)} %k_ref.1, bf16[512,640]{1,0:T(8,128)(2,1)} %v_ref.1, bf16[336,128]{1,0:T(8,128)(2,1)S(1)} %collective-permute-done.refs_0_), custom_call_target="tpu_custom_call" | custom-call | tf_op jit(solution)/shard_map/stage/pallas_call | solution.py:281
  12.1 0.5 %collective-permute-done.1.refs_2_ = bf16[336,128]{1,0:T(8,128)(2,1)S(1)} collective-permute-done((bf16[336,128]{1,0:T(8,128)(2,1)S(1)}, bf16[336,128]{1,0:T(8,128)(2,1)S(1)}, u32[]{:S(2)}, u32[]{:S(2)}) %collective-permute-start.1) | collective-permute-done | bytes 86048 | tf_op jit(solution)/shard_map/ppermute | solution.py:20
  12.6 0.0 collective-permute-done.2.refs_3_
  12.6 0.0 collective-permute-done.3.refs_4_
  12.6 0.0 collective-permute-done.4.refs_6_
  12.6 0.5 %score.1 = (bf16[128,640]{1,0:T(8,128)(2,1)S(1)}, bf16[256,640]{1,0:T(8,128)(2,1)S(1)}, f32[5,128,384]{2,1,0:T(8,128)S(1)}) custom-call(bf16[384,640]{1,0:T(8,128)(2,1)S(1)} %get-tuple-element.22.refs_0_, bf16[384,640]{1,0:T(8,128)(2,1)S(1)} %get-tuple-element.23.refs_1_, bf16[336,128]{1,0:T(8,128)(2,1)S(1)} %collective-permute-done.1.refs_2_, ...), custom_call_target="tpu_custom_call" | custom-call | tf_op jit(solution)/shard_map/score/pallas_call | solution.py:294
  13.1 1.1 %collective-permute-done.5.refs_5_ = bf16[336,128]{1,0:T(8,128)(2,1)S(1)} collective-permute-done((bf16[336,128]{1,0:T(8,128)(2,1)S(1)}, bf16[336,128]{1,0:T(8,128)(2,1)S(1)}, u32[]{:S(2)}, u32[]{:S(2)}) %collective-permute-start.5) | collective-permute-done | bytes 86048 | tf_op jit(solution)/shard_map/ppermute | solution.py:20
  14.2 0.6 %finish.2 = (bf16[32,640]{1,0:T(8,128)(2,1)S(1)}, bf16[32,640]{1,0:T(8,128)(2,1)S(1)}, bf16[128,640]{1,0:T(8,128)(2,1)S(1)}, bf16[128,640]{1,0:T(8,128)(2,1)S(1)}) custom-call(bf16[384,640]{1,0:T(8,128)(2,1)S(1)} %get-tuple-element.22.refs_0_, bf16[384,640]{1,0:T(8,128)(2,1)S(1)} %get-tuple-element.23.refs_1_, ...), custom_call_target="tpu_custom_call" | custom-call | tf_op jit(solution)/shard_map/finish/pallas_call | solution.py:306
  14.9 0.2 collective-permute-start.6
  15.0 1.6 %collective-permute-start.7 = (bf16[32,640]{1,0:T(8,128)(2,1)S(1)}, bf16[32,640]{1,0:T(8,128)(2,1)S(1)}, u32[]{:S(2)}, u32[]{:S(2)}) collective-permute-start(bf16[32,640]{1,0:T(8,128)(2,1)S(1)} %get-tuple-element.32), channel_id=1, source_target_pairs={{0,2},{1,3},{2,0},{3,1},{4,6},{5,7},{6,4},{7,5},{8,10},{9,11},{10,... | collective-permute-start | bytes 122888 | tf_op jit(solution)/shard_map/ppermute | solution.py:20
  16.6 0.5 %finish.3 = (bf16[32,640]{1,0:T(8,128)(2,1)S(1)}, bf16[32,640]{1,0:T(8,128)(2,1)S(1)}) custom-call(bf16[384,640]{1,0:T(8,128)(2,1)S(1)} %get-tuple-element.22.refs_0_, bf16[384,640]{1,0:T(8,128)(2,1)S(1)} %get-tuple-element.23.refs_1_, bf16[128,640]{1,0:T(8,128)(2,1)S(1)} %get-tuple-element.28.refs_2_, bf16[256,640]{1,0:T(8,128)(2,1)S(1)} %get-tuple-element.29.refs_3_, ...), custom_call_target="tpu_custom_call" | custom-call | tf_op jit(solution)/shard_map/finish/pallas_call | solution.py:306
  17.1 0.2 %collective-permute-start.8 = (bf16[32,640]{1,0:T(8,128)(2,1)S(1)}, bf16[32,640]{1,0:T(8,128)(2,1)S(1)}, u32[]{:S(2)}, u32[]{:S(2)}) collective-permute-start(bf16[32,640]{1,0:T(8,128)(2,1)S(1)} %get-tuple-element.35), channel_id=1, source_target_pairs={{0,1},{1,0},{2,3},{3,2},{4,5},{5,4},{6,7},{7,6},{8,9},{9,8},{10,11... | collective-permute-start | bytes 122888 | tf_op jit(solution)/shard_map/ppermute | solution.py:20
  17.4 1.2 %collective-permute-done.6.refs_0_ = bf16[32,640]{1,0:T(8,128)(2,1)S(1)} collective-permute-done((bf16[32,640]{1,0:T(8,128)(2,1)S(1)}, bf16[32,640]{1,0:T(8,128)(2,1)S(1)}, u32[]{:S(2)}, u32[]{:S(2)}) %collective-permute-start.6) | collective-permute-done | bytes 40992 | tf_op jit(solution)/shard_map/ppermute | solution.py:20
  18.6 0.6 %collective-permute-done.7.refs_1_ = bf16[32,640]{1,0:T(8,128)(2,1)S(1)} collective-permute-done((bf16[32,640]{1,0:T(8,128)(2,1)S(1)}, bf16[32,640]{1,0:T(8,128)(2,1)S(1)}, u32[]{:S(2)}, u32[]{:S(2)}) %collective-permute-start.7) | collective-permute-done | bytes 40992 | tf_op jit(solution)/shard_map/ppermute | solution.py:20
  19.2 0.0 collective-permute-done.8.refs_2_
  19.2 0.7 %join.1 = bf16[32,2560]{1,0:T(8,128)(2,1)} custom-call(s32[1]{0:T(128)} %bitcast.me, bf16[32,640]{1,0:T(8,128)(2,1)S(1)} %collective-permute-done.6.refs_0_, bf16[32,640]{1,0:T(8,128)(2,1)S(1)} %collective-permute-done.7.refs_1_, bf16[32,640]{1,0:T(8,128)(2,1)S(1)} %collective-permute-done.8.refs_2_, bf16[32,640]{1,0:T(8,128)(2,1)S(1)} %get-tuple-element.36.refs_3_), custom_call_target="tpu_custom_call" | custom-call | tf_op jit(solution)/shard_map/join/pallas_call | solution.py:318
Async XLA Ops:
  1.3 8.5 %collective-permute-start = (bf16[336,128]{1,0:T(8,128)(2,1)S(1)}, bf16[336,128]{1,0:T(8,128)(2,1)S(1)}, u32[]{:S(2)}, u32[]{:S(2)}) collective-permute-start(bf16[336,128]{1,0:T(8,128)(2,1)S(1)} %get-tuple-element.21), channel_id=1, source_target_pairs={{0,8},{4,12},{8,0},{12,4},{1,9},{5,13},{9,1},{13,5},{2,10},{6,14},... | collective-permute-start | bytes 258056 | tf_op jit(solution)/shard_map/ppermute | solution.py:20
  5.4 7.2 %collective-permute-start.2 = (bf16[96,640]{1,0:T(8,128)(2,1)S(1)}, bf16[96,640]{1,0:T(8,128)(2,1)S(1)}, u32[]{:S(2)}, u32[]{:S(2)}) collective-permute-start(bf16[96,640]{1,0:T(8,128)(2,1)S(1)} %get-tuple-element.24), channel_id=1, source_target_pairs={{0,2},{1,3},{2,0},{3,1},{4,6},{5,7},{6,4},{7,5},{8,10},{9,11},{10,... | collective-permute-start | bytes 368648 | tf_op jit(solution)/shard_map/ppermute | solution.py:20
  6.9 5.7 %collective-permute-start.3 = (bf16[96,640]{1,0:T(8,128)(2,1)S(1)}, bf16[96,640]{1,0:T(8,128)(2,1)S(1)}, u32[]{:S(2)}, u32[]{:S(2)}) collective-permute-start(bf16[96,640]{1,0:T(8,128)(2,1)S(1)} %get-tuple-element.25), channel_id=1, source_target_pairs={{0,3},{1,2},{2,1},{3,0},{4,7},{5,6},{6,5},{7,4},{8,11},{9,10},{10,... | collective-permute-start | bytes 368648 | tf_op jit(solution)/shard_map/ppermute | solution.py:20
  6.9 5.7 %collective-permute-start.4 = (bf16[96,640]{1,0:T(8,128)(2,1)S(1)}, bf16[96,640]{1,0:T(8,128)(2,1)S(1)}, u32[]{:S(2)}, u32[]{:S(2)}) collective-permute-start(bf16[96,640]{1,0:T(8,128)(2,1)S(1)} %get-tuple-element.27), channel_id=1, source_target_pairs={{0,1},{1,0},{2,3},{3,2},{4,5},{5,4},{6,7},{7,6},{8,9},{9,8},{10,11... | collective-permute-start | bytes 368648 | tf_op jit(solution)/shard_map/ppermute | solution.py:20
  7.5 5.1 %collective-permute-start.1 = (bf16[336,128]{1,0:T(8,128)(2,1)S(1)}, bf16[336,128]{1,0:T(8,128)(2,1)S(1)}, u32[]{:S(2)}, u32[]{:S(2)}) collective-permute-start(bf16[336,128]{1,0:T(8,128)(2,1)S(1)} %get-tuple-element.21), channel_id=1, source_target_pairs={{0,4},{4,0},{8,12},{12,8},{1,5},{5,1},{9,13},{13,9},{2,6},{6,2},{1... | collective-permute-start | bytes 258056 | tf_op jit(solution)/shard_map/ppermute | solution.py:20
  9.7 4.5 %collective-permute-start.5 = (bf16[336,128]{1,0:T(8,128)(2,1)S(1)}, bf16[336,128]{1,0:T(8,128)(2,1)S(1)}, u32[]{:S(2)}, u32[]{:S(2)}) collective-permute-start(bf16[336,128]{1,0:T(8,128)(2,1)S(1)} %collective-permute-done.refs_0_), channel_id=1, source_target_pairs={{0,4},{4,0},{8,12},{12,8},{1,5},{5,1},{9,13},{13,9},{2,6},{6,2},{1... | collective-permute-start | bytes 258056 | tf_op jit(solution)/shard_map/ppermute | solution.py:20
  14.9 3.7 %collective-permute-start.6 = (bf16[32,640]{1,0:T(8,128)(2,1)S(1)}, bf16[32,640]{1,0:T(8,128)(2,1)S(1)}, u32[]{:S(2)}, u32[]{:S(2)}) collective-permute-start(bf16[32,640]{1,0:T(8,128)(2,1)S(1)} %get-tuple-element.31), channel_id=1, source_target_pairs={{0,3},{1,2},{2,1},{3,0},{4,7},{5,6},{6,5},{7,4},{8,11},{9,10},{10,... | collective-permute-start | bytes 122888 | tf_op jit(solution)/shard_map/ppermute | solution.py:20
  15.0 4.2 %collective-permute-start.7 = (bf16[32,640]{1,0:T(8,128)(2,1)S(1)}, bf16[32,640]{1,0:T(8,128)(2,1)S(1)}, u32[]{:S(2)}, u32[]{:S(2)}) collective-permute-start(bf16[32,640]{1,0:T(8,128)(2,1)S(1)} %get-tuple-element.32), channel_id=1, source_target_pairs={{0,2},{1,3},{2,0},{3,1},{4,6},{5,7},{6,4},{7,5},{8,10},{9,11},{10,... | collective-permute-start | bytes 122888 | tf_op jit(solution)/shard_map/ppermute | solution.py:20
  17.1 2.1 %collective-permute-start.8 = (bf16[32,640]{1,0:T(8,128)(2,1)S(1)}, bf16[32,640]{1,0:T(8,128)(2,1)S(1)}, u32[]{:S(2)}, u32[]{:S(2)}) collective-permute-start(bf16[32,640]{1,0:T(8,128)(2,1)S(1)} %get-tuple-element.35), channel_id=1, source_target_pairs={{0,1},{1,0},{2,3},{3,2},{4,5},{5,4},{6,7},{7,6},{8,9},{9,8},{10,11... | collective-permute-start | bytes 122888 | tf_op jit(solution)/shard_map/ppermute | solution.py:20

commit v6 on v5

--- a/solution.py
+++ b/solution.py
@@ -148,17 +148,24 @@
     ) * (math.log2(math.e) / math.sqrt(q.shape[1]))
 
 
+def near_kernel(tok, block_len, fresh, size, k_st, v_st, packed, *refs):
+    k_out, v_out = refs[-2:]
+    rows_k = k_st.shape[1] // size * fresh
+    chosen = chooser(tok, fresh, block_len, packed, rows_k)
+    refresh(chosen, k_st, pl.ds(tok, tok), k_out, pl.ds(0, tok), packed, 0)
+    refresh(chosen, v_st, pl.ds(tok, tok), v_out, pl.ds(0, tok), packed, rows_k + tail)
+
+
 def score_kernel(count, n_now, ahead, block_len, fresh, size, *refs):
     (k_st, v_st), now, parts = refs[:2], refs[2 : 2 + n_now], in_turn(refs[2 + n_now : 2 + n_now + count], tokens_in)
     q_all, v_own, scores, k_own = refs[2 + n_now + count :]
+    near = pl.ds(parts[0].shape[0] // 3 * count, parts[0].shape[0] // 3 * count)
     rows = parts[0].shape[0] // 3
     tok = rows * count
     heads = parts[0].shape[1] // size
-    for place, packed in enumerate(now):
-        chosen = chooser(tok, fresh, block_len, packed, heads * fresh)
-        source, target = pl.ds(ahead + place * tok, tok), pl.ds((1 + place) * tok, tok)
-        refresh(chosen, k_st, source, k_own, target, packed, 0)
-        refresh(chosen, v_st, source, v_own, target, packed, heads * fresh + tail)
+    if now:
+        k_own[near, :] = now[0][...]
+        v_own[near, :] = now[1][...]
     for step in range(count):
         q_all[pl.ds(step * rows, rows), :] = parts[step][pl.ds(0, rows), :]
         k_own[pl.ds(step * rows, rows), :] = parts[step][pl.ds(rows, rows), :]
@@ -288,8 +295,18 @@
         name="stage",
     )(my_patch, in_hbm(prev_keys), in_hbm(prev_values), *residuals)
 
-    ahead = others - (len(now) + len(late)) * tok
-    own = (1 + len(now)) * tok
+    ahead = others - 2 * tok if four else others
+    own = (2 if four else 1) * tok
+    if now:
+        now = pl.pallas_call(
+            functools.partial(near_kernel, tok, block_len, fresh, size),
+            out_shape=[shape(tok, width)] * 2,
+            in_specs=[VM] * (1 + head_n),
+            out_specs=[VM] * 2,
+            compiler_params=grant,
+            cost_estimate=pl.CostEstimate(flops=500000000, bytes_accessed=0, transcendentals=0),
+            name="near",
+        )(stale_k, stale_v, *now, *parts[2:])
     kept = jax.ShapeDtypeStruct((heads, tok, ahead + own), jnp.float32)
     q_all, v_own, scores = pl.pallas_call(
         functools.partial(score_kernel, head_n, len(now), ahead, block_len, fresh, size),

time: 20.1 us -> 20.1 us (level)
  starting transfers between devices: 10.6 us -> 10.3 us
  waiting for transfers between devices: 4.14 us -> 4.35 us
    ppermute x9, starting transfers between devices: 10.6 us -> 10.3 us  [trade(): return lax.ppermute(array, axis, [(i, i ^ step) for i in range(count)])]
    pallas_call x0 -> x1, Pallas kernels: none -> 0.22 us  [local(): pl.pallas_call(functools.partial(near_kernel, tok, block_len, fresh, size...]
    ppermute x9, waiting for transfers between devices: 4.14 us -> 4.35 us  [trade(): return lax.ppermute(array, axis, [(i, i ^ step) for i in range(count)])]
  transfers between devices with their start and end apart: 9 -> 9, of which waited for: 5 -> 6; matrix products, arithmetic and copies ran while one was open for 0% -> 0% of each run, Pallas kernels for 13% -> 13%
where the time goes in v6:
time: 20.1 us; the launch traced here: 19.9 us
  starting transfers between devices  10.3 us (51%)
  Pallas kernels  5.22 us (26%)
  waiting for transfers between devices  4.35 us (22%)
    ppermute x9, starting transfers between devices, trade(): return lax.ppermute(array, axis, [(i, i ^ step) for i in range(count)])  10.3 us
    ppermute x9, waiting for transfers between devices, trade(): return lax.ppermute(array, axis, [(i, i ^ step) for i in range(count)])  4.35 us
    pallas_call x1, Pallas kernels, local(): pl.pallas_call(functools.partial(stage_kernel, steps, 1 if four else 0, t...  1.57 us
    pallas_call x1, Pallas kernels, local(): pl.pallas_call(functools.partial(prepare_kernel, head_n, len(inputs)), ou...  1.25 us
    pallas_call x2, Pallas kernels, local(): pl.pallas_call(functools.partial(finish_kernel, steps, len(fresh_late), l...  1.13 us
    pallas_call x1, Pallas kernels, local(): pl.pallas_call(functools.partial(join_kernel, head_n), out_shape=shape(ro...  0.68 us
  transfers between devices with their start and end apart: 9, of which 6 were waited for; matrix products, arithmetic and copies ran while one was open for 0% of the time, Pallas kernels for 13%

profile of v6, /device:TPU:0, one launch (start us, length us, event | category | flops | bytes accessed | tf_op | source)
XLA Modules:
  0.0 19.9 jit_solution(6995900945200217192)
XLA Ops:
  0.0 1.3 %prepare.1 = (bf16[336,128]{1,0:T(8,128)(2,1)S(1)}, bf16[96,640]{1,0:T(8,128)(2,1)S(1)}, bf16[96,640]{1,0:T(8,128)(2,1)S(1)}, bf16[96,640]{1,0:T(8,128)(2,1)S(1)}, bf16[96,640]{1,0:T(8,128)(2,1)S(1)}) custom-call(s32[1]{0:T(128)} %bitcast.me, s32[2]{0:T(128)} %refs_0_.1, s32[2,5]{1,0:T(2,128)} %refs_1_.1, bf16[2,16,640]{2,1,0:T(8,128)(2,1)} %refs_2_.1, ...), custom_call_target="tpu_custom_call" | custom-call | tf_op jit(solution)/shard_map/prepare/pallas_call | solution.py:263
  1.3 4.1 %collective-permute-start = (bf16[336,128]{1,0:T(8,128)(2,1)S(1)}, bf16[336,128]{1,0:T(8,128)(2,1)S(1)}, u32[]{:S(2)}, u32[]{:S(2)}) collective-permute-start(bf16[336,128]{1,0:T(8,128)(2,1)S(1)} %get-tuple-element.23), channel_id=1, source_target_pairs={{0,8},{4,12},{8,0},{12,4},{1,9},{5,13},{9,1},{13,5},{2,10},{6,14},... | collective-permute-start | bytes 258056 | tf_op jit(solution)/shard_map/ppermute | solution.py:20
  5.4 1.5 %collective-permute-start.2 = (bf16[96,640]{1,0:T(8,128)(2,1)S(1)}, bf16[96,640]{1,0:T(8,128)(2,1)S(1)}, u32[]{:S(2)}, u32[]{:S(2)}) collective-permute-start(bf16[96,640]{1,0:T(8,128)(2,1)S(1)} %get-tuple-element.26), channel_id=1, source_target_pairs={{0,2},{1,3},{2,0},{3,1},{4,6},{5,7},{6,4},{7,5},{8,10},{9,11},{10,... | collective-permute-start | bytes 368648 | tf_op jit(solution)/shard_map/ppermute | solution.py:20
  6.9 0.0 collective-permute-start.3
  6.9 1.6 %collective-permute-start.1 = (bf16[336,128]{1,0:T(8,128)(2,1)S(1)}, bf16[336,128]{1,0:T(8,128)(2,1)S(1)}, u32[]{:S(2)}, u32[]{:S(2)}) collective-permute-start(bf16[336,128]{1,0:T(8,128)(2,1)S(1)} %get-tuple-element.23), channel_id=1, source_target_pairs={{0,4},{4,0},{8,12},{12,8},{1,5},{5,1},{9,13},{13,9},{2,6},{6,2},{1... | collective-permute-start | bytes 258056 | tf_op jit(solution)/shard_map/ppermute | solution.py:20
  8.4 0.4 %collective-permute-start.4 = (bf16[96,640]{1,0:T(8,128)(2,1)S(1)}, bf16[96,640]{1,0:T(8,128)(2,1)S(1)}, u32[]{:S(2)}, u32[]{:S(2)}) collective-permute-start(bf16[96,640]{1,0:T(8,128)(2,1)S(1)} %get-tuple-element.31), channel_id=1, source_target_pairs={{0,1},{1,0},{2,3},{3,2},{4,5},{5,4},{6,7},{7,6},{8,9},{9,8},{10,11... | collective-permute-start | bytes 368648 | tf_op jit(solution)/shard_map/ppermute | solution.py:20
  8.8 0.9 %collective-permute-done.refs_0_ = bf16[336,128]{1,0:T(8,128)(2,1)S(1)} collective-permute-done((bf16[336,128]{1,0:T(8,128)(2,1)S(1)}, bf16[336,128]{1,0:T(8,128)(2,1)S(1)}, u32[]{:S(2)}, u32[]{:S(2)}) %collective-permute-start) | collective-permute-done | bytes 86048 | tf_op jit(solution)/shard_map/ppermute | solution.py:20
  9.7 0.8 %collective-permute-start.5 = (bf16[336,128]{1,0:T(8,128)(2,1)S(1)}, bf16[336,128]{1,0:T(8,128)(2,1)S(1)}, u32[]{:S(2)}, u32[]{:S(2)}) collective-permute-start(bf16[336,128]{1,0:T(8,128)(2,1)S(1)} %collective-permute-done.refs_0_), channel_id=1, source_target_pairs={{0,4},{4,0},{8,12},{12,8},{1,5},{5,1},{9,13},{13,9},{2,6},{6,2},{1... | collective-permute-start | bytes 258056 | tf_op jit(solution)/shard_map/ppermute | solution.py:20
  10.5 1.6 %stage.1 = (bf16[384,640]{1,0:T(8,128)(2,1)S(1)}, bf16[384,640]{1,0:T(8,128)(2,1)S(1)}) custom-call(s32[1]{0:T(128)} %bitcast.1.me, bf16[512,640]{1,0:T(8,128)(2,1)} %k_ref.1, bf16[512,640]{1,0:T(8,128)(2,1)} %v_ref.1, bf16[336,128]{1,0:T(8,128)(2,1)S(1)} %collective-permute-done.refs_0_), custom_call_target="tpu_custom_call" | custom-call | tf_op jit(solution)/shard_map/stage/pallas_call | solution.py:288
  12.1 0.2 collective-permute-done.1.packed
  12.3 0.0 collective-permute-done.2.refs_0_.refs_4_
  12.3 0.2 collective-permute-done.3.refs_1_.refs_5_
  12.5 0.2 %near.1 = (bf16[128,640]{1,0:T(8,128)(2,1)S(1)}, bf16[128,640]{1,0:T(8,128)(2,1)S(1)}) custom-call(bf16[384,640]{1,0:T(8,128)(2,1)S(1)} %get-tuple-element.24.k_st.refs_0_, bf16[384,640]{1,0:T(8,128)(2,1)S(1)} %get-tuple-element.25.v_st.refs_1_, bf16[336,128]{1,0:T(8,128)(2,1)S(1)} %collective-permute-done.1.packed, ...), custom_call_target="tpu_custom_call" | custom-call | flops 500000000 | tf_op jit(solution)/shard_map/near/pallas_call | solution.py:301
  12.7 0.0 collective-permute-done.4.refs_7_
  12.7 0.4 %score.1 = (bf16[128,640]{1,0:T(8,128)(2,1)S(1)}, bf16[256,640]{1,0:T(8,128)(2,1)S(1)}, f32[5,128,384]{2,1,0:T(8,128)S(1)}) custom-call(bf16[384,640]{1,0:T(8,128)(2,1)S(1)} %get-tuple-element.24.k_st.refs_0_, bf16[384,640]{1,0:T(8,128)(2,1)S(1)} %get-tuple-element.25.v_st.refs_1_, bf16[128,640]{1,0:T(8,128)(2,1)S(1)} %get-tuple-element.28.refs_2_, ...), custom_call_target="tpu_custom_call" | custom-call | tf_op jit(solution)/shard_map/score/pallas_call | solution.py:311
  13.1 1.2 %collective-permute-done.5.refs_5_ = bf16[336,128]{1,0:T(8,128)(2,1)S(1)} collective-permute-done((bf16[336,128]{1,0:T(8,128)(2,1)S(1)}, bf16[336,128]{1,0:T(8,128)(2,1)S(1)}, u32[]{:S(2)}, u32[]{:S(2)}) %collective-permute-start.5) | collective-permute-done | bytes 86048 | tf_op jit(solution)/shard_map/ppermute | solution.py:20
  14.2 0.6 %finish.2 = (bf16[32,640]{1,0:T(8,128)(2,1)S(1)}, bf16[32,640]{1,0:T(8,128)(2,1)S(1)}, bf16[128,640]{1,0:T(8,128)(2,1)S(1)}, bf16[128,640]{1,0:T(8,128)(2,1)S(1)}) custom-call(bf16[384,640]{1,0:T(8,128)(2,1)S(1)} %get-tuple-element.24.k_st.refs_0_, bf16[384,640]{1,0:T(8,128)(2,1)S(1)} %get-tuple-element.25.v_st.refs_1_, ...), custom_call_target="tpu_custom_call" | custom-call | tf_op jit(solution)/shard_map/finish/pallas_call | solution.py:323
  14.9 0.2 %collective-permute-start.6 = (bf16[32,640]{1,0:T(8,128)(2,1)S(1)}, bf16[32,640]{1,0:T(8,128)(2,1)S(1)}, u32[]{:S(2)}, u32[]{:S(2)}) collective-permute-start(bf16[32,640]{1,0:T(8,128)(2,1)S(1)} %get-tuple-element.35), channel_id=1, source_target_pairs={{0,3},{1,2},{2,1},{3,0},{4,7},{5,6},{6,5},{7,4},{8,11},{9,10},{10,... | collective-permute-start | bytes 122888 | tf_op jit(solution)/shard_map/ppermute | solution.py:20
  15.1 1.6 %collective-permute-start.7 = (bf16[32,640]{1,0:T(8,128)(2,1)S(1)}, bf16[32,640]{1,0:T(8,128)(2,1)S(1)}, u32[]{:S(2)}, u32[]{:S(2)}) collective-permute-start(bf16[32,640]{1,0:T(8,128)(2,1)S(1)} %get-tuple-element.36), channel_id=1, source_target_pairs={{0,2},{1,3},{2,0},{3,1},{4,6},{5,7},{6,4},{7,5},{8,10},{9,11},{10,... | collective-permute-start | bytes 122888 | tf_op jit(solution)/shard_map/ppermute | solution.py:20
  16.6 0.5 %finish.3 = (bf16[32,640]{1,0:T(8,128)(2,1)S(1)}, bf16[32,640]{1,0:T(8,128)(2,1)S(1)}) custom-call(bf16[384,640]{1,0:T(8,128)(2,1)S(1)} %get-tuple-element.24.k_st.refs_0_, bf16[384,640]{1,0:T(8,128)(2,1)S(1)} %get-tuple-element.25.v_st.refs_1_, bf16[128,640]{1,0:T(8,128)(2,1)S(1)} %get-tuple-element.32.refs_2_, ...), custom_call_target="tpu_custom_call" | custom-call | tf_op jit(solution)/shard_map/finish/pallas_call | solution.py:323
  17.1 0.2 %collective-permute-start.8 = (bf16[32,640]{1,0:T(8,128)(2,1)S(1)}, bf16[32,640]{1,0:T(8,128)(2,1)S(1)}, u32[]{:S(2)}, u32[]{:S(2)}) collective-permute-start(bf16[32,640]{1,0:T(8,128)(2,1)S(1)} %get-tuple-element.39), channel_id=1, source_target_pairs={{0,1},{1,0},{2,3},{3,2},{4,5},{5,4},{6,7},{7,6},{8,9},{9,8},{10,11... | collective-permute-start | bytes 122888 | tf_op jit(solution)/shard_map/ppermute | solution.py:20
  17.4 1.2 %collective-permute-done.6.refs_0_ = bf16[32,640]{1,0:T(8,128)(2,1)S(1)} collective-permute-done((bf16[32,640]{1,0:T(8,128)(2,1)S(1)}, bf16[32,640]{1,0:T(8,128)(2,1)S(1)}, u32[]{:S(2)}, u32[]{:S(2)}) %collective-permute-start.6) | collective-permute-done | bytes 40992 | tf_op jit(solution)/shard_map/ppermute | solution.py:20
  18.6 0.6 %collective-permute-done.7.refs_1_ = bf16[32,640]{1,0:T(8,128)(2,1)S(1)} collective-permute-done((bf16[32,640]{1,0:T(8,128)(2,1)S(1)}, bf16[32,640]{1,0:T(8,128)(2,1)S(1)}, u32[]{:S(2)}, u32[]{:S(2)}) %collective-permute-start.7) | collective-permute-done | bytes 40992 | tf_op jit(solution)/shard_map/ppermute | solution.py:20
  19.2 0.0 collective-permute-done.8.refs_2_
  19.2 0.7 %join.1 = bf16[32,2560]{1,0:T(8,128)(2,1)} custom-call(s32[1]{0:T(128)} %bitcast.me, bf16[32,640]{1,0:T(8,128)(2,1)S(1)} %collective-permute-done.6.refs_0_, bf16[32,640]{1,0:T(8,128)(2,1)S(1)} %collective-permute-done.7.refs_1_, bf16[32,640]{1,0:T(8,128)(2,1)S(1)} %collective-permute-done.8.refs_2_, bf16[32,640]{1,0:T(8,128)(2,1)S(1)} %get-tuple-element.40.refs_3_), custom_call_target="tpu_custom_call" | custom-call | tf_op jit(solution)/shard_map/join/pallas_call | solution.py:335
Async XLA Ops:
  1.3 8.5 %collective-permute-start = (bf16[336,128]{1,0:T(8,128)(2,1)S(1)}, bf16[336,128]{1,0:T(8,128)(2,1)S(1)}, u32[]{:S(2)}, u32[]{:S(2)}) collective-permute-start(bf16[336,128]{1,0:T(8,128)(2,1)S(1)} %get-tuple-element.23), channel_id=1, source_target_pairs={{0,8},{4,12},{8,0},{12,4},{1,9},{5,13},{9,1},{13,5},{2,10},{6,14},... | collective-permute-start | bytes 258056 | tf_op jit(solution)/shard_map/ppermute | solution.py:20
  5.4 6.9 %collective-permute-start.2 = (bf16[96,640]{1,0:T(8,128)(2,1)S(1)}, bf16[96,640]{1,0:T(8,128)(2,1)S(1)}, u32[]{:S(2)}, u32[]{:S(2)}) collective-permute-start(bf16[96,640]{1,0:T(8,128)(2,1)S(1)} %get-tuple-element.26), channel_id=1, source_target_pairs={{0,2},{1,3},{2,0},{3,1},{4,6},{5,7},{6,4},{7,5},{8,10},{9,11},{10,... | collective-permute-start | bytes 368648 | tf_op jit(solution)/shard_map/ppermute | solution.py:20
  6.9 5.6 %collective-permute-start.3 = (bf16[96,640]{1,0:T(8,128)(2,1)S(1)}, bf16[96,640]{1,0:T(8,128)(2,1)S(1)}, u32[]{:S(2)}, u32[]{:S(2)}) collective-permute-start(bf16[96,640]{1,0:T(8,128)(2,1)S(1)} %get-tuple-element.27), channel_id=1, source_target_pairs={{0,3},{1,2},{2,1},{3,0},{4,7},{5,6},{6,5},{7,4},{8,11},{9,10},{10,... | collective-permute-start | bytes 368648 | tf_op jit(solution)/shard_map/ppermute | solution.py:20
  6.9 5.4 %collective-permute-start.1 = (bf16[336,128]{1,0:T(8,128)(2,1)S(1)}, bf16[336,128]{1,0:T(8,128)(2,1)S(1)}, u32[]{:S(2)}, u32[]{:S(2)}) collective-permute-start(bf16[336,128]{1,0:T(8,128)(2,1)S(1)} %get-tuple-element.23), channel_id=1, source_target_pairs={{0,4},{4,0},{8,12},{12,8},{1,5},{5,1},{9,13},{13,9},{2,6},{6,2},{1... | collective-permute-start | bytes 258056 | tf_op jit(solution)/shard_map/ppermute | solution.py:20
  8.4 4.3 %collective-permute-start.4 = (bf16[96,640]{1,0:T(8,128)(2,1)S(1)}, bf16[96,640]{1,0:T(8,128)(2,1)S(1)}, u32[]{:S(2)}, u32[]{:S(2)}) collective-permute-start(bf16[96,640]{1,0:T(8,128)(2,1)S(1)} %get-tuple-element.31), channel_id=1, source_target_pairs={{0,1},{1,0},{2,3},{3,2},{4,5},{5,4},{6,7},{7,6},{8,9},{9,8},{10,11... | collective-permute-start | bytes 368648 | tf_op jit(solution)/shard_map/ppermute | solution.py:20
  9.7 4.5 %collective-permute-start.5 = (bf16[336,128]{1,0:T(8,128)(2,1)S(1)}, bf16[336,128]{1,0:T(8,128)(2,1)S(1)}, u32[]{:S(2)}, u32[]{:S(2)}) collective-permute-start(bf16[336,128]{1,0:T(8,128)(2,1)S(1)} %collective-permute-done.refs_0_), channel_id=1, source_target_pairs={{0,4},{4,0},{8,12},{12,8},{1,5},{5,1},{9,13},{13,9},{2,6},{6,2},{1... | collective-permute-start | bytes 258056 | tf_op jit(solution)/shard_map/ppermute | solution.py:20
  14.9 3.7 %collective-permute-start.6 = (bf16[32,640]{1,0:T(8,128)(2,1)S(1)}, bf16[32,640]{1,0:T(8,128)(2,1)S(1)}, u32[]{:S(2)}, u32[]{:S(2)}) collective-permute-start(bf16[32,640]{1,0:T(8,128)(2,1)S(1)} %get-tuple-element.35), channel_id=1, source_target_pairs={{0,3},{1,2},{2,1},{3,0},{4,7},{5,6},{6,5},{7,4},{8,11},{9,10},{10,... | collective-permute-start | bytes 122888 | tf_op jit(solution)/shard_map/ppermute | solution.py:20
  15.1 4.1 %collective-permute-start.7 = (bf16[32,640]{1,0:T(8,128)(2,1)S(1)}, bf16[32,640]{1,0:T(8,128)(2,1)S(1)}, u32[]{:S(2)}, u32[]{:S(2)}) collective-permute-start(bf16[32,640]{1,0:T(8,128)(2,1)S(1)} %get-tuple-element.36), channel_id=1, source_target_pairs={{0,2},{1,3},{2,0},{3,1},{4,6},{5,7},{6,4},{7,5},{8,10},{9,11},{10,... | collective-permute-start | bytes 122888 | tf_op jit(solution)/shard_map/ppermute | solution.py:20
  17.1 2.1 %collective-permute-start.8 = (bf16[32,640]{1,0:T(8,128)(2,1)S(1)}, bf16[32,640]{1,0:T(8,128)(2,1)S(1)}, u32[]{:S(2)}, u32[]{:S(2)}) collective-permute-start(bf16[32,640]{1,0:T(8,128)(2,1)S(1)} %get-tuple-element.39), channel_id=1, source_target_pairs={{0,1},{1,0},{2,3},{3,2},{4,5},{5,4},{6,7},{7,6},{8,9},{9,8},{10,11... | collective-permute-start | bytes 122888 | tf_op jit(solution)/shard_map/ppermute | solution.py:20

commit v7 on v6

--- a/solution.py
+++ b/solution.py
@@ -20,12 +20,17 @@
     return lax.ppermute(array, axis, [(i, i ^ step) for i in range(count)])
 
 
+def cross(array, even, odd, patch_n, head_n):
+    pairs = [(p * head_n + h, (p ^ (odd if h % 2 else even)) * head_n + h) for p in range(patch_n) for h in range(head_n)]
+    return lax.ppermute(array, ("patch", "head"), pairs)
+
+
 def tokens_in(count):
     return [*range(2, count), *range(min(2, count))]
 
 
 def tokens_out(count):
-    return list(reversed(range(count)))
+    return [*range(2, count), *range(min(2, count))]
 
 
 def in_turn(refs, order):
@@ -113,9 +118,12 @@
         new[target, lanes] = (old[source, lanes].astype(jnp.float32) + change).astype(jnp.bfloat16)
 
 
-def stage_kernel(steps, early, tok, fresh, block_len, n_res, me, k_ref, v_ref, *refs):
+def stage_kernel(steps, early, tok, fresh, block_len, n_res, me, my_head, k_ref, v_ref, *refs):
     res, (k_out, v_out, sems) = refs[:n_res], refs[n_res:]
     pairs = []
+    if early:
+        first = 2 - my_head[0] % 2
+        steps = [first, 3 - first, 3]
     for place, step in enumerate(steps):
         source = pl.ds(pl.multiple_of((me[0] ^ step) * tok, 128), tok)
         target = pl.ds(place * tok, tok)
@@ -273,27 +281,27 @@
     )(my_head, *[in_hbm(x) for x in inputs])
 
     if four:
-        near = trade(both, "patch", 1, patch_n)
-        far = trade(both, "patch", 2, patch_n)
-        residuals = [far]
-        steps, late = [2, 1, 3], [near]
+        first = cross(both, 2, 1, patch_n, head_n)
+        second = cross(both, 1, 2, patch_n, head_n)
+        residuals = [first]
+        steps, late = [0, 0, 0], [second]
     else:
         residuals = [lax.all_gather(both, "patch", axis=0)]
         steps, late = range(1, patch_n), []
     parts = [trade(parts[step], "head", step, head_n) if step else parts[0] for step in range(head_n)]
     now = late
-    late = [trade(far, "patch", 1, patch_n)] if four else []
+    late = [cross(first, 1, 2, patch_n, head_n)] if four else []
 
     others = (patch_n - 1) * tok
     stale_k, stale_v = pl.pallas_call(
         functools.partial(stage_kernel, steps, 1 if four else 0, tok, fresh, block_len, len(residuals)),
         out_shape=[shape(others, width)] * 2,
-        in_specs=[SM] + [HB] * 2 + [VM] * len(residuals),
+        in_specs=[SM] * 2 + [HB] * 2 + [VM] * len(residuals),
         out_specs=[VM] * 2,
         scratch_shapes=[pltpu.SemaphoreType.DMA((2 * (patch_n - 1),))],
         compiler_params=larger,
         name="stage",
-    )(my_patch, in_hbm(prev_keys), in_hbm(prev_values), *residuals)
+    )(my_patch, my_head, in_hbm(prev_keys), in_hbm(prev_values), *residuals)
 
     ahead = others - 2 * tok if four else others
     own = (2 if four else 1) * tok

time: 20.1 us -> 20.3 us (level)
  the two profiles are of different devices: /device:TPU:0 before, /device:TPU:1 now
where the time goes in v7:
time: 20.3 us; the launch traced here: 20.1 us
  starting transfers between devices  10.2 us (50%)
  Pallas kernels  5.22 us (26%)
  waiting for transfers between devices  4.67 us (23%)
    ppermute x6, starting transfers between devices, trade(): return lax.ppermute(array, axis, [(i, i ^ step) for i in range(count)])  7.03 us
    ppermute x6, waiting for transfers between devices, trade(): return lax.ppermute(array, axis, [(i, i ^ step) for i in range(count)])  3.28 us
    ppermute x3, starting transfers between devices, cross(): return lax.ppermute(array, ('patch', 'head'), pairs)  3.12 us
    pallas_call x1, Pallas kernels, local(): pl.pallas_call(functools.partial(stage_kernel, steps, 1 if four else 0, t...  1.56 us
    ppermute x3, waiting for transfers between devices, cross(): return lax.ppermute(array, ('patch', 'head'), pairs)  1.39 us
    pallas_call x1, Pallas kernels, local(): pl.pallas_call(functools.partial(prepare_kernel, head_n, len(inputs)), ou...  1.25 us
    pallas_call x2, Pallas kernels, local(): pl.pallas_call(functools.partial(finish_kernel, steps, len(fresh_late), l...  1.13 us
    pallas_call x1, Pallas kernels, local(): pl.pallas_call(functools.partial(join_kernel, head_n), out_shape=shape(ro...  0.68 us
  transfers between devices with their start and end apart: 9, of which 5 were waited for; matrix products, arithmetic and copies ran while one was open for 0% of the time, Pallas kernels for 13%

profile of v7, /device:TPU:1, one launch (start us, length us, event | category | flops | bytes accessed | tf_op | source)
XLA Modules:
  0.0 20.1 jit_solution(17572885854731770428)
XLA Ops:
  0.0 1.2 %prepare.1 = (bf16[336,128]{1,0:T(8,128)(2,1)S(1)}, bf16[96,640]{1,0:T(8,128)(2,1)S(1)}, bf16[96,640]{1,0:T(8,128)(2,1)S(1)}, bf16[96,640]{1,0:T(8,128)(2,1)S(1)}, bf16[96,640]{1,0:T(8,128)(2,1)S(1)}) custom-call(s32[1]{0:T(128)} %bitcast.me.my_head, s32[2]{0:T(128)} %refs_0_.1, s32[2,5]{1,0:T(2,128)} %refs_1_.1, bf16[2,16,640]{2,1,0:T(8,128)(2,1)} %refs_2_.1, ...), custom_call_target="tpu_custom_call" | custom-call | tf_op jit(solution)/shard_map/prepare/pallas_call | solution.py:271
  1.3 2.2 %collective-permute-start = (bf16[336,128]{1,0:T(8,128)(2,1)S(1)}, bf16[336,128]{1,0:T(8,128)(2,1)S(1)}, u32[]{:S(2)}, u32[]{:S(2)}) collective-permute-start(bf16[336,128]{1,0:T(8,128)(2,1)S(1)} %get-tuple-element.23), channel_id=1, source_target_pairs={{0,8},{1,5},{2,10},{3,7},{4,12},{5,1},{6,14},{7,3},{8,0},{9,13},{1... | collective-permute-start | bytes 258056 | tf_op jit(solution)/shard_map/ppermute | solution.py:25
  3.4 1.2 %collective-permute-start.2 = (bf16[96,640]{1,0:T(8,128)(2,1)S(1)}, bf16[96,640]{1,0:T(8,128)(2,1)S(1)}, u32[]{:S(2)}, u32[]{:S(2)}) collective-permute-start(bf16[96,640]{1,0:T(8,128)(2,1)S(1)} %get-tuple-element.26), channel_id=1, source_target_pairs={{0,2},{1,3},{2,0},{3,1},{4,6},{5,7},{6,4},{7,5},{8,10},{9,11},{10,... | collective-permute-start | bytes 368648 | tf_op jit(solution)/shard_map/ppermute | solution.py:20
  4.7 2.4 %collective-permute-start.3 = (bf16[96,640]{1,0:T(8,128)(2,1)S(1)}, bf16[96,640]{1,0:T(8,128)(2,1)S(1)}, u32[]{:S(2)}, u32[]{:S(2)}) collective-permute-start(bf16[96,640]{1,0:T(8,128)(2,1)S(1)} %get-tuple-element.27), channel_id=1, source_target_pairs={{0,3},{1,2},{2,1},{3,0},{4,7},{5,6},{6,5},{7,4},{8,11},{9,10},{10,... | collective-permute-start | bytes 368648 | tf_op jit(solution)/shard_map/ppermute | solution.py:20
  7.1 0.0 collective-permute-start.1
  7.1 1.4 %collective-permute-start.4 = (bf16[96,640]{1,0:T(8,128)(2,1)S(1)}, bf16[96,640]{1,0:T(8,128)(2,1)S(1)}, u32[]{:S(2)}, u32[]{:S(2)}) collective-permute-start(bf16[96,640]{1,0:T(8,128)(2,1)S(1)} %get-tuple-element.31), channel_id=1, source_target_pairs={{0,1},{1,0},{2,3},{3,2},{4,5},{5,4},{6,7},{7,6},{8,9},{9,8},{10,11... | collective-permute-start | bytes 368648 | tf_op jit(solution)/shard_map/ppermute | solution.py:20
  8.5 0.0 collective-permute-done.refs_0_
  8.5 0.9 %collective-permute-start.5 = (bf16[336,128]{1,0:T(8,128)(2,1)S(1)}, bf16[336,128]{1,0:T(8,128)(2,1)S(1)}, u32[]{:S(2)}, u32[]{:S(2)}) collective-permute-start(bf16[336,128]{1,0:T(8,128)(2,1)S(1)} %collective-permute-done.refs_0_), channel_id=1, source_target_pairs={{0,4},{1,9},{2,6},{3,11},{4,0},{5,13},{6,2},{7,15},{8,12},{9,1},{1... | collective-permute-start | bytes 258056 | tf_op jit(solution)/shard_map/ppermute | solution.py:25
  9.4 1.6 %stage.1 = (bf16[384,640]{1,0:T(8,128)(2,1)S(1)}, bf16[384,640]{1,0:T(8,128)(2,1)S(1)}) custom-call(s32[1]{0:T(128)} %bitcast.1.me, s32[1]{0:T(128)} %bitcast.me.my_head, bf16[512,640]{1,0:T(8,128)(2,1)} %k_ref.1, bf16[512,640]{1,0:T(8,128)(2,1)} %v_ref.1, bf16[336,128]{1,0:T(8,128)(2,1)S(1)} %collective-permute-done.refs_0_), custom_call_target="tpu_custom_call" | custom-call | tf_op jit(solution)/shard_map/stage/pallas_call | solution.py:296
  11.0 0.4 %collective-permute-done.1.packed = bf16[336,128]{1,0:T(8,128)(2,1)S(1)} collective-permute-done((bf16[336,128]{1,0:T(8,128)(2,1)S(1)}, bf16[336,128]{1,0:T(8,128)(2,1)S(1)}, u32[]{:S(2)}, u32[]{:S(2)}) %collective-permute-start.1) | collective-permute-done | bytes 86048 | tf_op jit(solution)/shard_map/ppermute | solution.py:25
  11.4 0.0 collective-permute-done.2.refs_0_.refs_4_
  11.4 1.1 %collective-permute-done.3.refs_1_.refs_5_ = bf16[96,640]{1,0:T(8,128)(2,1)S(1)} collective-permute-done((bf16[96,640]{1,0:T(8,128)(2,1)S(1)}, bf16[96,640]{1,0:T(8,128)(2,1)S(1)}, u32[]{:S(2)}, u32[]{:S(2)}) %collective-permute-start.3) | collective-permute-done | bytes 122912 | tf_op jit(solution)/shard_map/ppermute | solution.py:20
  12.5 0.2 %near.1 = (bf16[128,640]{1,0:T(8,128)(2,1)S(1)}, bf16[128,640]{1,0:T(8,128)(2,1)S(1)}) custom-call(bf16[384,640]{1,0:T(8,128)(2,1)S(1)} %get-tuple-element.24.k_st.refs_0_, bf16[384,640]{1,0:T(8,128)(2,1)S(1)} %get-tuple-element.25.v_st.refs_1_, bf16[336,128]{1,0:T(8,128)(2,1)S(1)} %collective-permute-done.1.packed, ...), custom_call_target="tpu_custom_call" | custom-call | flops 500000000 | tf_op jit(solution)/shard_map/near/pallas_call | solution.py:309
  12.8 0.0 collective-permute-done.4.refs_7_
  12.8 0.4 %score.1 = (bf16[128,640]{1,0:T(8,128)(2,1)S(1)}, bf16[256,640]{1,0:T(8,128)(2,1)S(1)}, f32[5,128,384]{2,1,0:T(8,128)S(1)}) custom-call(bf16[384,640]{1,0:T(8,128)(2,1)S(1)} %get-tuple-element.24.k_st.refs_0_, bf16[384,640]{1,0:T(8,128)(2,1)S(1)} %get-tuple-element.25.v_st.refs_1_, bf16[128,640]{1,0:T(8,128)(2,1)S(1)} %get-tuple-element.28.refs_2_, ...), custom_call_target="tpu_custom_call" | custom-call | tf_op jit(solution)/shard_map/score/pallas_call | solution.py:319
  13.1 1.0 %collective-permute-done.5.refs_5_ = bf16[336,128]{1,0:T(8,128)(2,1)S(1)} collective-permute-done((bf16[336,128]{1,0:T(8,128)(2,1)S(1)}, bf16[336,128]{1,0:T(8,128)(2,1)S(1)}, u32[]{:S(2)}, u32[]{:S(2)}) %collective-permute-start.5) | collective-permute-done | bytes 86048 | tf_op jit(solution)/shard_map/ppermute | solution.py:25
  14.1 0.6 %finish.2 = (bf16[32,640]{1,0:T(8,128)(2,1)S(1)}, bf16[32,640]{1,0:T(8,128)(2,1)S(1)}, bf16[128,640]{1,0:T(8,128)(2,1)S(1)}, bf16[128,640]{1,0:T(8,128)(2,1)S(1)}) custom-call(bf16[384,640]{1,0:T(8,128)(2,1)S(1)} %get-tuple-element.24.k_st.refs_0_, bf16[384,640]{1,0:T(8,128)(2,1)S(1)} %get-tuple-element.25.v_st.refs_1_, ...), custom_call_target="tpu_custom_call" | custom-call | tf_op jit(solution)/shard_map/finish/pallas_call | solution.py:331
  14.8 1.2 %collective-permute-start.6 = (bf16[32,640]{1,0:T(8,128)(2,1)S(1)}, bf16[32,640]{1,0:T(8,128)(2,1)S(1)}, u32[]{:S(2)}, u32[]{:S(2)}) collective-permute-start(bf16[32,640]{1,0:T(8,128)(2,1)S(1)} %get-tuple-element.35), channel_id=1, source_target_pairs={{0,2},{1,3},{2,0},{3,1},{4,6},{5,7},{6,4},{7,5},{8,10},{9,11},{10,... | collective-permute-start | bytes 122888 | tf_op jit(solution)/shard_map/ppermute | solution.py:20
  16.0 0.0 collective-permute-start.7
  16.0 0.5 %finish.3 = (bf16[32,640]{1,0:T(8,128)(2,1)S(1)}, bf16[32,640]{1,0:T(8,128)(2,1)S(1)}) custom-call(bf16[384,640]{1,0:T(8,128)(2,1)S(1)} %get-tuple-element.24.k_st.refs_0_, bf16[384,640]{1,0:T(8,128)(2,1)S(1)} %get-tuple-element.25.v_st.refs_1_, bf16[128,640]{1,0:T(8,128)(2,1)S(1)} %get-tuple-element.32.refs_2_, ...), custom_call_target="tpu_custom_call" | custom-call | tf_op jit(solution)/shard_map/finish/pallas_call | solution.py:331
  16.5 0.8 %collective-permute-start.8 = (bf16[32,640]{1,0:T(8,128)(2,1)S(1)}, bf16[32,640]{1,0:T(8,128)(2,1)S(1)}, u32[]{:S(2)}, u32[]{:S(2)}) collective-permute-start(bf16[32,640]{1,0:T(8,128)(2,1)S(1)} %get-tuple-element.40), channel_id=1, source_target_pairs={{0,1},{1,0},{2,3},{3,2},{4,5},{5,4},{6,7},{7,6},{8,9},{9,8},{10,11... | collective-permute-start | bytes 122888 | tf_op jit(solution)/shard_map/ppermute | solution.py:20
  17.3 0.5 %collective-permute-done.6.refs_0_ = bf16[32,640]{1,0:T(8,128)(2,1)S(1)} collective-permute-done((bf16[32,640]{1,0:T(8,128)(2,1)S(1)}, bf16[32,640]{1,0:T(8,128)(2,1)S(1)}, u32[]{:S(2)}, u32[]{:S(2)}) %collective-permute-start.6) | collective-permute-done | bytes 40992 | tf_op jit(solution)/shard_map/ppermute | solution.py:20
  17.8 1.6 %collective-permute-done.7.refs_1_ = bf16[32,640]{1,0:T(8,128)(2,1)S(1)} collective-permute-done((bf16[32,640]{1,0:T(8,128)(2,1)S(1)}, bf16[32,640]{1,0:T(8,128)(2,1)S(1)}, u32[]{:S(2)}, u32[]{:S(2)}) %collective-permute-start.7) | collective-permute-done | bytes 40992 | tf_op jit(solution)/shard_map/ppermute | solution.py:20
  19.4 0.0 collective-permute-done.8.refs_3_
  19.4 0.7 %join.1 = bf16[32,2560]{1,0:T(8,128)(2,1)} custom-call(s32[1]{0:T(128)} %bitcast.me.my_head, bf16[32,640]{1,0:T(8,128)(2,1)S(1)} %collective-permute-done.6.refs_0_, bf16[32,640]{1,0:T(8,128)(2,1)S(1)} %collective-permute-done.7.refs_1_, bf16[32,640]{1,0:T(8,128)(2,1)S(1)} %get-tuple-element.39.refs_2_, bf16[32,640]{1,0:T(8,128)(2,1)S(1)} %collective-permute-done.8.refs_3_), custom_call_target="tpu_custom_call" | custom-call | tf_op jit(solution)/shard_map/join/pallas_call | solution.py:343
Async XLA Ops:
  1.3 7.2 %collective-permute-start = (bf16[336,128]{1,0:T(8,128)(2,1)S(1)}, bf16[336,128]{1,0:T(8,128)(2,1)S(1)}, u32[]{:S(2)}, u32[]{:S(2)}) collective-permute-start(bf16[336,128]{1,0:T(8,128)(2,1)S(1)} %get-tuple-element.23), channel_id=1, source_target_pairs={{0,8},{1,5},{2,10},{3,7},{4,12},{5,1},{6,14},{7,3},{8,0},{9,13},{1... | collective-permute-start | bytes 258056 | tf_op jit(solution)/shard_map/ppermute | solution.py:25
  3.4 7.9 %collective-permute-start.2 = (bf16[96,640]{1,0:T(8,128)(2,1)S(1)}, bf16[96,640]{1,0:T(8,128)(2,1)S(1)}, u32[]{:S(2)}, u32[]{:S(2)}) collective-permute-start(bf16[96,640]{1,0:T(8,128)(2,1)S(1)} %get-tuple-element.26), channel_id=1, source_target_pairs={{0,2},{1,3},{2,0},{3,1},{4,6},{5,7},{6,4},{7,5},{8,10},{9,11},{10,... | collective-permute-start | bytes 368648 | tf_op jit(solution)/shard_map/ppermute | solution.py:20
  4.7 7.9 %collective-permute-start.3 = (bf16[96,640]{1,0:T(8,128)(2,1)S(1)}, bf16[96,640]{1,0:T(8,128)(2,1)S(1)}, u32[]{:S(2)}, u32[]{:S(2)}) collective-permute-start(bf16[96,640]{1,0:T(8,128)(2,1)S(1)} %get-tuple-element.27), channel_id=1, source_target_pairs={{0,3},{1,2},{2,1},{3,0},{4,7},{5,6},{6,5},{7,4},{8,11},{9,10},{10,... | collective-permute-start | bytes 368648 | tf_op jit(solution)/shard_map/ppermute | solution.py:20
  7.1 4.3 %collective-permute-start.1 = (bf16[336,128]{1,0:T(8,128)(2,1)S(1)}, bf16[336,128]{1,0:T(8,128)(2,1)S(1)}, u32[]{:S(2)}, u32[]{:S(2)}) collective-permute-start(bf16[336,128]{1,0:T(8,128)(2,1)S(1)} %get-tuple-element.23), channel_id=1, source_target_pairs={{0,4},{1,9},{2,6},{3,11},{4,0},{5,13},{6,2},{7,15},{8,12},{9,1},{1... | collective-permute-start | bytes 258056 | tf_op jit(solution)/shard_map/ppermute | solution.py:25
  7.1 5.7 %collective-permute-start.4 = (bf16[96,640]{1,0:T(8,128)(2,1)S(1)}, bf16[96,640]{1,0:T(8,128)(2,1)S(1)}, u32[]{:S(2)}, u32[]{:S(2)}) collective-permute-start(bf16[96,640]{1,0:T(8,128)(2,1)S(1)} %get-tuple-element.31), channel_id=1, source_target_pairs={{0,1},{1,0},{2,3},{3,2},{4,5},{5,4},{6,7},{7,6},{8,9},{9,8},{10,11... | collective-permute-start | bytes 368648 | tf_op jit(solution)/shard_map/ppermute | solution.py:20
  8.5 5.6 %collective-permute-start.5 = (bf16[336,128]{1,0:T(8,128)(2,1)S(1)}, bf16[336,128]{1,0:T(8,128)(2,1)S(1)}, u32[]{:S(2)}, u32[]{:S(2)}) collective-permute-start(bf16[336,128]{1,0:T(8,128)(2,1)S(1)} %collective-permute-done.refs_0_), channel_id=1, source_target_pairs={{0,4},{1,9},{2,6},{3,11},{4,0},{5,13},{6,2},{7,15},{8,12},{9,1},{1... | collective-permute-start | bytes 258056 | tf_op jit(solution)/shard_map/ppermute | solution.py:25
  14.8 3.0 %collective-permute-start.6 = (bf16[32,640]{1,0:T(8,128)(2,1)S(1)}, bf16[32,640]{1,0:T(8,128)(2,1)S(1)}, u32[]{:S(2)}, u32[]{:S(2)}) collective-permute-start(bf16[32,640]{1,0:T(8,128)(2,1)S(1)} %get-tuple-element.35), channel_id=1, source_target_pairs={{0,2},{1,3},{2,0},{3,1},{4,6},{5,7},{6,4},{7,5},{8,10},{9,11},{10,... | collective-permute-start | bytes 122888 | tf_op jit(solution)/shard_map/ppermute | solution.py:20
  16.0 3.4 %collective-permute-start.7 = (bf16[32,640]{1,0:T(8,128)(2,1)S(1)}, bf16[32,640]{1,0:T(8,128)(2,1)S(1)}, u32[]{:S(2)}, u32[]{:S(2)}) collective-permute-start(bf16[32,640]{1,0:T(8,128)(2,1)S(1)} %get-tuple-element.36), channel_id=1, source_target_pairs={{0,3},{1,2},{2,1},{3,0},{4,7},{5,6},{6,5},{7,4},{8,11},{9,10},{10,... | collective-permute-start | bytes 122888 | tf_op jit(solution)/shard_map/ppermute | solution.py:20
  16.5 2.9 %collective-permute-start.8 = (bf16[32,640]{1,0:T(8,128)(2,1)S(1)}, bf16[32,640]{1,0:T(8,128)(2,1)S(1)}, u32[]{:S(2)}, u32[]{:S(2)}) collective-permute-start(bf16[32,640]{1,0:T(8,128)(2,1)S(1)} %get-tuple-element.40), channel_id=1, source_target_pairs={{0,1},{1,0},{2,3},{3,2},{4,5},{5,4},{6,7},{7,6},{8,9},{9,8},{10,11... | collective-permute-start | bytes 122888 | tf_op jit(solution)/shard_map/ppermute | solution.py:20
